TPU v7x, 256 devices: a whole 4x4x8 slice. The times are simulated.
256 devices in a mesh: dp: 4 (over z_hi), gx: 16 (over z_lo, x, core), gy: 4 (over y).
Axes of the slice: x: 4, y: 4, z: 8 (z_hi: 4, z_lo: 2; z = z_hi * 2 + z_lo), core: 2. Of those that a mesh axis runs over, the one named last changes fastest.
Arguments:
- volume: bfloat16 [4, 64, 64, 8, 128], P('dp', 'gx', 'gy'), may hold values from -6 to 6
- cotangent: bfloat16 [4, 64, 64, 8, 128], P('dp', 'gx', 'gy'), may hold values from -0.3125 to 0.3125
- master: float32 [6912, 128], P('dp'), may hold values from -0.109375 to 0.109375
- moment_one: float32 [6912, 128], P('dp'), may hold values from -6 to 6
- moment_two: float32 [6912, 128], P('dp'), may hold values from 0.25 to 4
Outputs:
- activation: bfloat16 [4, 64, 64, 8, 128], P('dp', 'gx', 'gy')
- new_master: float32 [6912, 128], P('dp')
- new_moment_one: float32 [6912, 128], P('dp')
- new_moment_two: float32 [6912, 128], P('dp')
All inputs are finite; a program needn't handle non-finite values.
Results may differ from a plain program's by a relative error of at most 0.006.
The roundings to bfloat16 on the way count: a program that leaves them out, or rounds other values in their place, can miss the bound.
Values may be sent and summed in bfloat16 or wider, within the bound.
No kernel may reach another device: no remote copies, remote signals or barrier semaphores. Data moves between devices by JAX's collectives and lax.ppermute only.
A program may use at most 64 MiB of HBM per device.

v0:
```python
import jax
import jax.numpy as jnp
from jax import lax
from jax.sharding import PartitionSpec as P

inv_root_two = 0.7071067811865476
inv_root_tau = 0.3989422804014327
beta_one = 0.9
beta_two = 0.999
learn_rate = 0.01
epsilon = 1e-08


def extended(cells, sides, width):
    for axis, dim in sides:
        count = lax.axis_size(axis)
        ends = count - 1
        head = lax.slice_in_dim(cells, 0, width, axis=dim)
        tail = lax.slice_in_dim(cells, cells.shape[dim] - width, cells.shape[dim], axis=dim)
        cells = jnp.concatenate(
            [
                lax.ppermute(tail, axis, [(i, (i + 1) % count) for i in range(ends)]),
                cells,
                lax.ppermute(head, axis, [((i + 1) % count, i) for i in range(ends)]),
            ],
            axis=dim,
        )
    return cells


def gelu_value(field):
    return 0.5 * field * (1.0 + lax.erf(field * inv_root_two))


def gelu_slope(field):
    normal_cdf = 0.5 * (1.0 + lax.erf(field * inv_root_two))
    return normal_cdf + field * jnp.exp(-0.5 * field * field) * inv_root_tau


def depth_pad(field):
    return jnp.pad(field, ((0, 0), (0, 0), (1, 1), (0, 0)))


def convolve(padded, kernel, span_x, span_y, span_z):
    total = jnp.zeros((span_x * span_y * span_z, kernel.shape[2]), jnp.float32)
    for offset_x in range(3):
        for offset_y in range(3):
            for offset_z in range(3):
                window = padded[
                    offset_x : offset_x + span_x,
                    offset_y : offset_y + span_y,
                    offset_z : offset_z + span_z,
                ]
                total = total + jnp.dot(
                    window.reshape(-1, padded.shape[3]),
                    kernel[9 * offset_x + 3 * offset_y + offset_z],
                    preferred_element_type=jnp.float32,
                )
    return total


def weight_grad(padded, delta, span_x, span_y, span_z):
    pieces = []
    for offset_x in range(3):
        for offset_y in range(3):
            for offset_z in range(3):
                window = padded[
                    offset_x : offset_x + span_x,
                    offset_y : offset_y + span_y,
                    offset_z : offset_z + span_z,
                ]
                flat_window = window.reshape(-1, padded.shape[3])
                pieces.append(
                    lax.dot_general(
                        flat_window,
                        delta,
                        (((0,), (0,)), ((), ())),
                        preferred_element_type=jnp.float32,
                    )
                )
    return jnp.concatenate(pieces, axis=0)


def adam_update(master, moment_one, moment_two, gradient):
    new_one = beta_one * moment_one + (1.0 - beta_one) * gradient
    new_two = beta_two * moment_two + (1.0 - beta_two) * gradient * gradient
    update = new_one / (1.0 - beta_one**10) / (jnp.sqrt(new_two / (1.0 - beta_two**10)) + epsilon)
    return (master - learn_rate * update, new_one, new_two)


def per_device(volume, cotangent, master, moment_one, moment_two):
    field = volume[0]
    span_x, span_y, span_z, width = field.shape
    local_weights = master.astype(jnp.bfloat16)
    full_weights = lax.all_gather(local_weights, "dp", axis=0, tiled=True)
    kernels = full_weights.reshape(2, 27, width, width)
    flipped = kernels[1][::-1].transpose(0, 2, 1)
    padded_in = depth_pad(extended(field, (("gx", 0), ("gy", 1)), 1))
    first = convolve(padded_in, kernels[0], span_x, span_y, span_z)
    hidden = gelu_value(first).astype(jnp.bfloat16).reshape(span_x, span_y, span_z, width)
    padded_hidden = depth_pad(extended(hidden, (("gx", 0), ("gy", 1)), 1))
    second = convolve(padded_hidden, kernels[1], span_x, span_y, span_z)
    activation = gelu_value(second).astype(jnp.bfloat16).reshape(1, span_x, span_y, span_z, width)
    upstream = cotangent[0].reshape(span_x * span_y * span_z, width)
    delta_two = (upstream.astype(jnp.float32) * gelu_slope(second)).astype(jnp.bfloat16)
    grad_two = weight_grad(padded_hidden, delta_two, span_x, span_y, span_z)
    padded_delta = depth_pad(
        extended(delta_two.reshape(span_x, span_y, span_z, width), (("gx", 0), ("gy", 1)), 1)
    )
    back = convolve(padded_delta, flipped, span_x, span_y, span_z)
    delta_one = (back * gelu_slope(first)).astype(jnp.bfloat16)
    grad_one = weight_grad(padded_in, delta_one, span_x, span_y, span_z)
    gradient = jnp.concatenate([grad_one, grad_two], axis=0)
    summed = lax.psum(gradient, ("gx", "gy"))
    own_rows = lax.psum_scatter(
        summed.astype(jnp.bfloat16), "dp", scatter_dimension=0, tiled=True
    ).astype(jnp.float32)
    new_master, new_one, new_two = adam_update(master, moment_one, moment_two, own_rows)
    return (activation, new_master, new_one, new_two)


def solution(mesh):
    return jax.shard_map(
        per_device,
        mesh=mesh,
        in_specs=(
            P("dp", "gx", "gy", None, None),
            P("dp", "gx", "gy", None, None),
            P("dp", None),
            P("dp", None),
            P("dp", None),
        ),
        out_specs=(P("dp", "gx", "gy", None, None), P("dp", None), P("dp", None), P("dp", None)),
        check_vma=False,
    )
```

profile of v0, /device:TPU:1, one launch (start us, length us, event | category | flops | bytes accessed | tf_op | source)
XLA Modules:
  0.0 498.7 jit_solution(13223516718232298265)
XLA Ops:
  7.2 2.0 convert_element_type.31
  10.0 4.5 collective-permute-start
  14.5 1.9 collective-permute-start.1
  16.5 3.3 collective-permute-done.1
  20.5 3.2 collective-permute-start.2
  23.7 1.3 collective-permute-start.3
  25.0 1.0 pad_maximum_fusion.7
  26.0 2.1 collective-permute-done.3
  28.1 1.0 pad_maximum_fusion
  29.2 1.2 fusion.21
  31.1 29.4 %all-gather.2.cloned.1.call-done = bf16[6912,128]{1,0:T(8,128)(2,1)} async-done(((bf16[1728,128]{1,0:T(8,128)(2,1)}), bf16[6912,128]{1,0:T(8,128)(2,1)}) %all-gather.2.cloned.1.call-update) | async-done | bytes 1769488 | tf_op jit(solution)/shard_map/all_gather | solution.py:95
  60.6 1.1 fusion.72
  63.5 0.9 convolution_add_fusion.71
  64.4 1.0 convolution_add_fusion.70
  65.4 0.9 convolution_add_fusion.69
  66.4 0.9 fusion.6
  71.2 3.0 collective-permute-start.4
  74.2 1.9 collective-permute-start.5
  76.2 3.3 collective-permute-done.5
  79.5 3.1 collective-permute-start.6
  82.6 1.3 collective-permute-start.7
  84.0 3.1 collective-permute-done.7
  92.5 1.0 fusion.31
  93.5 3.4 collective-permute-start.8
  96.9 1.9 collective-permute-start.9
  98.9 3.2 collective-permute-done.9
  102.1 3.1 collective-permute-start.10
  105.2 1.5 collective-permute-start.11
  106.8 2.9 collective-permute-done.11
  129.0 308.0 %all-reduce.4 = bf16[6912,128]{1,0:T(8,128)(2,1)} all-reduce(f32[6912,128]{1,0:T(8,128)S(1)} %convolution_dynamic-update-slice_fusion), channel_id=1, replica_groups=mesh['dp'=4,'gx'=16,'gy'=4] {'gx','gy'}, use_global_device_ids=true, to_apply=%region_0.1 | all-reduce | flops 884736 | bytes 5308416 | tf_op jit(solution)/shard_map/psum | solution.py:114
  437.0 51.2 %reduce-scatter.2.cloned.1.call-done = bf16[1728,128]{1,0:T(8,128)(2,1)} async-done(((bf16[6912,128]{1,0:T(8,128)(2,1)}), bf16[1728,128]{1,0:T(8,128)(2,1)}) %reduce-scatter.2.cloned.1.call-update) | async-done | bytes 442384 | tf_op jit(solution)/shard_map/reduce_scatter | solution.py:115
  488.2 3.7 multiply_subtract_fusion
  (272 shorter events, 31.2 us)
Async XLA Ops:
  7.2 53.4 %all-gather.2.cloned.1.call-start = ((), (), s32[]{:S(2)}) async-start(), calls=%async_computation.1 | async-start | bytes 2211840 | tf_op jit(solution)/shard_map/all_gather | solution.py:95
  9.2 479.0 %reduce-scatter.2.cloned.1.call-start = ((), (), s32[]{:S(2)}) async-start(), calls=%async_computation.2 | async-start | bytes 2211840 | tf_op jit(solution)/shard_map/reduce_scatter | solution.py:115
  10.0 6.4 %collective-permute-start = (bf16[1,16,8,128]{3,2,1,0:T(8,128)(2,1)S(1)}, bf16[1,16,8,128]{3,2,1,0:T(8,128)(2,1)S(1)}, u32[]{:S(2)}, u32[]{:S(2)}) collective-permute-start(bf16[1,16,8,128]{3,2,1,0:T(8,128)(2,1)S(1)} %get-tuple-element.103), channel_id=1, source_target_pairs={{0,4},{4,8},{8,12},{12,16},{16,20},{20,24},{24,28},{28,32},{32,36}... | collective-permute-start | bytes 98312 | tf_op jit(solution)/shard_map/ppermute | solution.py:22
  14.5 5.2 %collective-permute-start.1 = (bf16[1,16,8,128]{3,2,1,0:T(8,128)(2,1)S(1)}, bf16[1,16,8,128]{3,2,1,0:T(8,128)(2,1)S(1)}, u32[]{:S(2)}, u32[]{:S(2)}) collective-permute-start(bf16[1,16,8,128]{3,2,1,0:T(8,128)(2,1)S(1)} %get-tuple-element.104), channel_id=1, source_target_pairs={{4,0},{8,4},{12,8},{16,12},{20,16},{24,20},{28,24},{32,28},{36,32}... | collective-permute-start | bytes 98312 | tf_op jit(solution)/shard_map/ppermute | solution.py:24
  20.5 5.5 %collective-permute-start.2 = (bf16[6,1,8,128]{3,2,1,0:T(8,128)(2,1)S(1)}, bf16[6,1,8,128]{3,2,1,0:T(8,128)(2,1)S(1)}, u32[]{:S(2)}, u32[]{:S(2)}) collective-permute-start(bf16[6,1,8,128]{3,2,1,0:T(8,128)(2,1)S(1)} %get-tuple-element.91), channel_id=1, source_target_pairs={{0,1},{1,2},{2,3},{4,5},{5,6},{6,7},{8,9},{9,10},{10,11},{12,13},{... | collective-permute-start | bytes 36872 | tf_op jit(solution)/shard_map/ppermute | solution.py:22
  23.7 4.4 collective-permute-start.3
  26.0 40.4 %copy-start.52 = (bf16[4,16,8,128]{3,2,1,0:T(8,128)(2,1)}, bf16[4,16,8,128]{3,2,1,0:T(8,128)(2,1)S(1)}, u32[]{:S(2)}) copy-start(bf16[4,16,8,128]{3,2,1,0:T(8,128)(2,1)S(1)} %get-tuple-element.102) | copy-start | bytes 393220
  26.0 44.4 %copy-start.50 = (bf16[4,16,8,128]{3,2,1,0:T(8,128)(2,1)}, bf16[4,16,8,128]{3,2,1,0:T(8,128)(2,1)S(1)}, u32[]{:S(2)}) copy-start(bf16[4,16,8,128]{3,2,1,0:T(8,128)(2,1)S(1)} %get-tuple-element.101) | copy-start | bytes 393220
  30.5 37.6 %copy-start.26 = (bf16[4,16,8,128]{3,2,1,0:T(8,128)(2,1)}, bf16[4,16,8,128]{3,2,1,0:T(8,128)(2,1)S(1)}, u32[]{:S(2)}) copy-start(bf16[4,16,8,128]{3,2,1,0:T(8,128)(2,1)S(1)} %get-tuple-element.108) | copy-start | bytes 393220
  30.6 38.7 %copy-start.16 = (bf16[4,16,8,128]{3,2,1,0:T(8,128)(2,1)}, bf16[4,16,8,128]{3,2,1,0:T(8,128)(2,1)S(1)}, u32[]{:S(2)}) copy-start(bf16[4,16,8,128]{3,2,1,0:T(8,128)(2,1)S(1)} %get-tuple-element.76) | copy-start | bytes 393220
  30.6 39.2 %copy-start.12 = (bf16[4,16,8,128]{3,2,1,0:T(8,128)(2,1)}, bf16[4,16,8,128]{3,2,1,0:T(8,128)(2,1)S(1)}, u32[]{:S(2)}) copy-start(bf16[4,16,8,128]{3,2,1,0:T(8,128)(2,1)S(1)} %get-tuple-element.109) | copy-start | bytes 393220
  30.6 40.2 %copy-start.10 = (bf16[4,16,8,128]{3,2,1,0:T(8,128)(2,1)}, bf16[4,16,8,128]{3,2,1,0:T(8,128)(2,1)S(1)}, u32[]{:S(2)}) copy-start(bf16[4,16,8,128]{3,2,1,0:T(8,128)(2,1)S(1)} %get-tuple-element.75) | copy-start | bytes 393220
  31.0 37.1 %copy-start.4 = (bf16[4,16,8,128]{3,2,1,0:T(8,128)(2,1)}, bf16[4,16,8,128]{3,2,1,0:T(8,128)(2,1)S(1)}, u32[]{:S(2)}) copy-start(bf16[4,16,8,128]{3,2,1,0:T(8,128)(2,1)S(1)} %get-tuple-element.45) | copy-start | bytes 393220
  31.0 37.1 %copy-start.6 = (bf16[4,16,8,128]{3,2,1,0:T(8,128)(2,1)}, bf16[4,16,8,128]{3,2,1,0:T(8,128)(2,1)S(1)}, u32[]{:S(2)}) copy-start(bf16[4,16,8,128]{3,2,1,0:T(8,128)(2,1)S(1)} %get-tuple-element.57) | copy-start | bytes 393220
  31.0 37.3 %copy-start.36 = (bf16[4,16,8,128]{3,2,1,0:T(8,128)(2,1)}, bf16[4,16,8,128]{3,2,1,0:T(8,128)(2,1)S(1)}, u32[]{:S(2)}) copy-start(bf16[4,16,8,128]{3,2,1,0:T(8,128)(2,1)S(1)} %get-tuple-element.53) | copy-start | bytes 393220
  31.1 37.4 %copy-start.34 = (bf16[4,16,8,128]{3,2,1,0:T(8,128)(2,1)}, bf16[4,16,8,128]{3,2,1,0:T(8,128)(2,1)S(1)}, u32[]{:S(2)}) copy-start(bf16[4,16,8,128]{3,2,1,0:T(8,128)(2,1)S(1)} %get-tuple-element.52) | copy-start | bytes 393220
  31.1 37.8 %copy-start.30 = (bf16[4,16,8,128]{3,2,1,0:T(8,128)(2,1)}, bf16[4,16,8,128]{3,2,1,0:T(8,128)(2,1)S(1)}, u32[]{:S(2)}) copy-start(bf16[4,16,8,128]{3,2,1,0:T(8,128)(2,1)S(1)} %get-tuple-element.51) | copy-start | bytes 393220
  31.1 38.0 %copy-start.28 = (bf16[4,16,8,128]{3,2,1,0:T(8,128)(2,1)}, bf16[4,16,8,128]{3,2,1,0:T(8,128)(2,1)S(1)}, u32[]{:S(2)}) copy-start(bf16[4,16,8,128]{3,2,1,0:T(8,128)(2,1)S(1)} %get-tuple-element.50) | copy-start | bytes 393220
  31.1 38.4 %copy-start.24 = (bf16[4,16,8,128]{3,2,1,0:T(8,128)(2,1)}, bf16[4,16,8,128]{3,2,1,0:T(8,128)(2,1)S(1)}, u32[]{:S(2)}) copy-start(bf16[4,16,8,128]{3,2,1,0:T(8,128)(2,1)S(1)} %get-tuple-element.49) | copy-start | bytes 393220
  31.1 38.5 %copy-start.22 = (bf16[4,16,8,128]{3,2,1,0:T(8,128)(2,1)}, bf16[4,16,8,128]{3,2,1,0:T(8,128)(2,1)S(1)}, u32[]{:S(2)}) copy-start(bf16[4,16,8,128]{3,2,1,0:T(8,128)(2,1)S(1)} %get-tuple-element.48) | copy-start | bytes 393220
  31.1 38.9 %copy-start.20 = (bf16[4,16,8,128]{3,2,1,0:T(8,128)(2,1)}, bf16[4,16,8,128]{3,2,1,0:T(8,128)(2,1)S(1)}, u32[]{:S(2)}) copy-start(bf16[4,16,8,128]{3,2,1,0:T(8,128)(2,1)S(1)} %get-tuple-element.47) | copy-start | bytes 393220
  31.1 39.1 %copy-start.18 = (bf16[4,16,8,128]{3,2,1,0:T(8,128)(2,1)}, bf16[4,16,8,128]{3,2,1,0:T(8,128)(2,1)S(1)}, u32[]{:S(2)}) copy-start(bf16[4,16,8,128]{3,2,1,0:T(8,128)(2,1)S(1)} %get-tuple-element.46) | copy-start | bytes 393220
  31.1 39.4 %copy-start.14 = (bf16[4,16,8,128]{3,2,1,0:T(8,128)(2,1)}, bf16[4,16,8,128]{3,2,1,0:T(8,128)(2,1)S(1)}, u32[]{:S(2)}) copy-start(bf16[4,16,8,128]{3,2,1,0:T(8,128)(2,1)S(1)} %get-tuple-element.44) | copy-start | bytes 393220
  31.1 39.8 %copy-start.2 = (bf16[4,16,8,128]{3,2,1,0:T(8,128)(2,1)}, bf16[4,16,8,128]{3,2,1,0:T(8,128)(2,1)S(1)}, u32[]{:S(2)}) copy-start(bf16[4,16,8,128]{3,2,1,0:T(8,128)(2,1)S(1)} %get-tuple-element.43) | copy-start | bytes 393220
  71.2 5.0 collective-permute-start.4
  74.2 5.2 %collective-permute-start.5 = (bf16[1,16,8,128]{3,2,1,0:T(8,128)(2,1)S(1)}, bf16[1,16,8,128]{3,2,1,0:T(8,128)(2,1)S(1)}, u32[]{:S(2)}, u32[]{:S(2)}) collective-permute-start(bf16[1,16,8,128]{3,2,1,0:T(8,128)(2,1)S(1)} %get-tuple-element.100), channel_id=1, source_target_pairs={{4,0},{8,4},{12,8},{16,12},{20,16},{24,20},{28,24},{32,28},{36,32}... | collective-permute-start | bytes 98312 | tf_op jit(solution)/shard_map/ppermute | solution.py:24
  79.5 4.5 collective-permute-start.6
  82.6 4.4 collective-permute-start.7
  93.5 5.4 %collective-permute-start.8 = (bf16[1,16,8,128]{3,2,1,0:T(8,128)(2,1)S(1)}, bf16[1,16,8,128]{3,2,1,0:T(8,128)(2,1)S(1)}, u32[]{:S(2)}, u32[]{:S(2)}) collective-permute-start(bf16[1,16,8,128]{3,2,1,0:T(8,128)(2,1)S(1)} %get-tuple-element.95), channel_id=1, source_target_pairs={{0,4},{4,8},{8,12},{12,16},{16,20},{20,24},{24,28},{28,32},{32,36}... | collective-permute-start | bytes 98312 | tf_op jit(solution)/shard_map/ppermute | solution.py:22
  96.9 5.2 %collective-permute-start.9 = (bf16[1,16,8,128]{3,2,1,0:T(8,128)(2,1)S(1)}, bf16[1,16,8,128]{3,2,1,0:T(8,128)(2,1)S(1)}, u32[]{:S(2)}, u32[]{:S(2)}) collective-permute-start(bf16[1,16,8,128]{3,2,1,0:T(8,128)(2,1)S(1)} %get-tuple-element.96), channel_id=1, source_target_pairs={{4,0},{8,4},{12,8},{16,12},{20,16},{24,20},{28,24},{32,28},{36,32}... | collective-permute-start | bytes 98312 | tf_op jit(solution)/shard_map/ppermute | solution.py:24
  102.1 4.7 collective-permute-start.10
  105.2 4.4 collective-permute-start.11
  (38 other events, 418.2 us)
Sparse Core Ops, SparseCore 0:
  10.4 50.1 all-gather.1
  437.1 51.0 reduce-scatter.1
where the time goes:
time: 500 us; the launch traced here: 499 us
  blocking collectives  308 us (62%)
  waiting for transfers between devices  98.6 us (20%)
  matrix products  32.8 us (7%)
  starting transfers between devices  30.2 us (6%)
  between operations  16.2 us (3%)
  other arithmetic  10.4 us (2%)
    psum x1, blocking collectives, per_device(): summed = lax.psum(gradient, ('gx', 'gy'))  308 us
    reduce_scatter x1, waiting for transfers between devices, per_device(): lax.psum_scatter(summed.astype(jnp.bfloat16), 'dp', scatter_dimension=0,...  51.2 us
    all_gather x1, waiting for transfers between devices, per_device(): full_weights = lax.all_gather(local_weights, 'dp', axis=0, tiled=True)  29.4 us
    dot_general x81, matrix products, convolve(): jnp.dot(window.reshape(-1, padded.shape[3]), kernel[9 * offset_x + 3 * of...  20.5 us
    ppermute x6, starting transfers between devices, extended(): lax.ppermute(tail, axis, [(i, (i + 1) % count) for i in range(ends)])  20.3 us
    ppermute x6, waiting for transfers between devices, extended(): lax.ppermute(head, axis, [((i + 1) % count, i) for i in range(ends)])  17.9 us
    dot_general x54, matrix products, weight_grad(): lax.dot_general(flat_window, delta, (((0,), (0,)), ((), ())), preferred_e...  12.3 us
  transfers between devices with their start and end apart: 14, of which 8 were waited for; matrix products, arithmetic and copies ran while one was open for 1% of the time, Pallas kernels for 0%

commit v1 on v0

v1 whole, which is shorter than its diff:
```python
import jax
import jax.numpy as jnp
from jax import lax
from jax.experimental import pallas as pl
from jax.experimental.pallas import tpu as pltpu
from jax.sharding import Mesh
from jax.sharding import PartitionSpec as P

inv_root_two = 0.7071067811865476
inv_root_tau = 0.3989422804014327
beta_one = 0.9
beta_two = 0.999
learn_rate = 0.01
epsilon = 1e-08

BF = jnp.bfloat16
F32 = jnp.float32

C = 128
SX, SY, SZ = 4, 16, 8
NX, NY = 64, 64
TAPS = 14
HALF = TAPS // 2 * C
PIECE = HALF // 16


def gelu_value(field):
    return 0.5 * field * (1.0 + lax.erf(field * inv_root_two))


def gelu_slope(field):
    normal_cdf = 0.5 * (1.0 + lax.erf(field * inv_root_two))
    return normal_cdf + field * jnp.exp(-0.5 * field * field) * inv_root_tau


def depth_triple(field):
    depth = lax.broadcasted_iota(jnp.int32, field.shape, 2)
    below = jnp.where(depth == 0, 0.0, pltpu.roll(field, 1, 2))
    above = jnp.where(depth == SZ - 1, 0.0, pltpu.roll(field, SZ - 1, 2))
    return [part.reshape(-1, C).astype(BF) for part in (below, field, above)]


def store_triple(ref, rows, field):
    for position, part in enumerate(depth_triple(field)):
        ref[rows, position * C : (position + 1) * C] = part


def conv_rows(ref, planes_out, wide, weights):
    rows = planes_out * wide * SZ
    step = wide * SZ
    left = jnp.concatenate([ref[a * step : a * step + rows, :] for a in range(3)], axis=1)
    prod = jnp.dot(left, weights, preferred_element_type=F32).reshape(planes_out, wide, SZ, 3 * C)
    return (
        prod[:, 0 : wide - 2, :, 0:C]
        + prod[:, 1 : wide - 1, :, C : 2 * C]
        + prod[:, 2:wide, :, 2 * C : 3 * C]
    )


def layer_weights(taps, layer):
    columns = []
    for b in range(3):
        rows = [(layer * 27 + 9 * a + 3 * b) * C for a in range(3)]
        columns.append(jnp.concatenate([taps[r : r + 3 * C] for r in rows], axis=0))
    return jnp.concatenate(columns, axis=1)


def grad_taps(grads, layer, ref, wide, first_plane, shift, delta):
    lefts = []
    for b in range(3):
        before, after = shift + b, wide - SY - shift - b
        padded = jnp.concatenate(
            [
                jnp.zeros((SX, before, SZ, C), F32),
                delta,
                jnp.zeros((SX, after, SZ, C), F32),
            ],
            axis=1,
        ).reshape(SX * wide * SZ, C)
        lefts.append(jnp.transpose(padded).astype(BF))
    left = jnp.concatenate(lefts, axis=0)
    step = wide * SZ
    for a in range(3):
        start = (first_plane + a) * step
        prod = jnp.dot(left, ref[start : start + SX * step, :], preferred_element_type=F32)
        for b in range(3):
            for c in range(3):
                grads[layer * 27 + 9 * a + 3 * b + c] = prod[b * C : (b + 1) * C, c * C : (c + 1) * C]


def step_kernel(
    place, vol, left, right, low, high, cot, *rest
):
    pieces = rest[:8]
    act, send, keep = rest[8:11]
    taps, flipped, field, hid, dlt, grads = rest[11:]
    gx, gy, core = place[0], place[1], place[2]

    for index, piece in enumerate(pieces):
        owner_core = core if index < 4 else 1 - core
        owner_y = lax.rem(gy + 4 - index % 4, 4)
        taps[
            pl.ds(owner_core * 54, 54), pl.ds(pl.multiple_of(owner_y * 16, 16), 16), :
        ] = piece[...].reshape(54, 16, C)
    tap_rows = taps[...].reshape(54 * C, C)

    middle = [left[0:3], vol[...], right[0:3]]
    for part, planes, start in zip(middle, (3, 4, 3), (0, 3, 7)):
        whole = jnp.concatenate(
            [
                low[3 * start : 3 * (start + planes)].reshape(planes, 3, SZ, C),
                part,
                high[3 * start : 3 * (start + planes)].reshape(planes, 3, SZ, C),
            ],
            axis=1,
        ).astype(F32)
        store_triple(field, slice(start * 176, (start + planes) * 176), whole)

    first = conv_rows(field, 8, 22, layer_weights(tap_rows, 0))
    x_at = lax.broadcasted_iota(jnp.int32, first.shape, 0) + (gx * SX - 2)
    y_at = lax.broadcasted_iota(jnp.int32, first.shape, 1) + (gy * SY - 2)
    inside = (x_at >= 0) & (x_at < NX) & (y_at >= 0) & (y_at < NY)
    hidden = jnp.where(inside, gelu_value(first), 0.0)
    slope_one = gelu_slope(first[2:6, 2:18])
    store_triple(hid, slice(0, 8 * 160), hidden)

    second = conv_rows(hid, 6, 20, layer_weights(tap_rows, 1))
    act[...] = gelu_value(second[1:5, 1:17]).astype(BF)
    upstream = jnp.concatenate(
        [
            low[30:36].reshape(6, 1, SZ, C),
            jnp.concatenate([left[3:4], cot[...], right[3:4]], axis=0),
            high[30:36].reshape(6, 1, SZ, C),
        ],
        axis=1,
    ).astype(F32)
    delta_two = upstream * gelu_slope(second)
    store_triple(dlt, slice(0, 6 * 144), delta_two)
    grad_taps(grads, 1, hid, 20, 1, 1, delta_two[1:5, 1:17])

    for t in range(27):
        a, b, c = t // 9, t // 3 % 3, t % 3
        row = (27 + 26 - t) * C
        block = jnp.transpose(tap_rows[row : row + C].astype(F32)).astype(BF)
        flipped[(3 * a + c) * C : (3 * a + c + 1) * C, b * C : (b + 1) * C] = block
    back = conv_rows(dlt, 4, 18, flipped[...])
    grad_taps(grads, 0, field, 22, 2, 2, back * slope_one)

    for shard in range(4):
        base = 27 * (shard // 2) + 13 * (shard % 2)
        keep[shard] = grads[pl.ds(base + 7 * core, 7)].reshape(HALF, C)
        send[shard] = grads[pl.ds(base + 7 * (1 - core), 7)].reshape(HALF, C).astype(BF)


def device_step(place, vol, left, right, low, high, cot, pieces):
    vmem = pl.BlockSpec(memory_space=pltpu.VMEM)
    return pl.pallas_call(
        step_kernel,
        out_shape=(
            jax.ShapeDtypeStruct((SX, SY, SZ, C), BF),
            jax.ShapeDtypeStruct((4, HALF, C), BF),
            jax.ShapeDtypeStruct((4, HALF, C), F32),
        ),
        in_specs=[pl.BlockSpec(memory_space=pltpu.SMEM)] + [vmem] * 14,
        out_specs=(vmem, vmem, vmem),
        scratch_shapes=[
            pltpu.VMEM((108, 64, C), BF),
            pltpu.VMEM((9 * C, 3 * C), BF),
            pltpu.VMEM((10 * 176, 3 * C), BF),
            pltpu.VMEM((8 * 160, 3 * C), BF),
            pltpu.VMEM((6 * 144, 3 * C), BF),
            pltpu.VMEM((54, C, C), F32),
        ],
        compiler_params=pltpu.CompilerParams(vmem_limit_bytes=48 * 2**20),
        cost_estimate=pl.CostEstimate(flops=3_500_000_000, bytes_accessed=8_000_000, transcendentals=1_000_000),
        name="unet_step",
    )(place, vol, left, right, low, high, cot, *pieces)


def adam_kernel(place, mine, other, master, one, two, new_master, new_one, new_two, grad):
    core, odd = place[2], lax.rem(place[3], 2)
    for source, owner in ((mine, core), (other, 1 - core)):
        for tap in range(TAPS // 2):
            block = source[tap * C : (tap + 1) * C].astype(F32)
            grad[pl.ds(pl.multiple_of((owner * (TAPS // 2) + tap) * C, C), C), :] = jnp.transpose(block)
    rows = master.shape[0]
    gradient = grad[pl.ds(pl.multiple_of(odd * (C // 2), C // 2), rows), :]
    first = beta_one * one[...] + (1.0 - beta_one) * gradient
    second = beta_two * two[...] + (1.0 - beta_two) * gradient * gradient
    update = first / (1.0 - beta_one**10) / (jnp.sqrt(second / (1.0 - beta_two**10)) + epsilon)
    new_master[...] = master[...] - learn_rate * update
    new_one[...] = first
    new_two[...] = second


def adam_update(place, mine, other, master, one, two):
    vmem = pl.BlockSpec(memory_space=pltpu.VMEM)
    shape = jax.ShapeDtypeStruct(master.shape, F32)
    return pl.pallas_call(
        adam_kernel,
        out_shape=(shape, shape, shape),
        in_specs=[pl.BlockSpec(memory_space=pltpu.SMEM)] + [vmem] * 5,
        out_specs=(vmem, vmem, vmem),
        scratch_shapes=[pltpu.VMEM((TAPS * C, C), F32)],
        compiler_params=pltpu.CompilerParams(vmem_limit_bytes=24 * 2**20),
        name="adam_step",
    )(place, mine, other, master, one, two)


GX = ("zl", "x", "c")


def shifted(cells, axis, count, by):
    return lax.ppermute(cells, axis, [(i, (i + by) % count) for i in range(count)])


def gathered_weights(master, dp, core, gy):
    local = master.astype(BF).reshape(27, 64, C)
    own = lax.dynamic_slice(local, (0, 16 * gy, 0), (27, 16, C))
    got = [
        lax.ppermute(
            own,
            ("dp", "c"),
            [((d ^ s) * 2 + c, d * 2 + c) for d in range(4) for c in range(2) if (d ^ s) // 2 == c],
        )
        for s in (1, 2, 3)
    ]
    both = []
    for parity in range(2):
        distance = jnp.bitwise_xor(dp, 2 * core + parity)
        both.append(
            jnp.where(
                distance == 0,
                own,
                jnp.where(distance == 1, got[0], jnp.where(distance == 2, got[1], got[2])),
            )
        )
    stack = jnp.stack(both)
    mine = [stack] + [shifted(stack, "gy", 4, s) for s in (1, 2, 3)]
    return mine + [shifted(part, "c", 2, 1) for part in mine]


def per_device(volume, cotangent, master, moment_one, moment_two):
    vol, cot = volume[0], cotangent[0]
    dp, core, gy = lax.axis_index("dp"), lax.axis_index("c"), lax.axis_index("gy")
    gx = lax.axis_index(GX)
    place = jnp.stack([gx, gy, core, dp]).astype(jnp.int32)

    up_x = [(i, i + 1) for i in range(15)]
    down_x = [(i + 1, i) for i in range(15)]
    left = lax.ppermute(jnp.concatenate([vol[1:4], cot[3:4]]), GX, up_x)
    right = lax.ppermute(jnp.concatenate([vol[0:3], cot[0:1]]), GX, down_x)

    def edge(at, width, field):
        return field[:, at : at + width].reshape(-1, SZ, C)

    def side(at_field, at_cot):
        return jnp.concatenate(
            [
                edge(at_field, 3, left[0:3]),
                edge(at_field, 3, vol),
                edge(at_field, 3, right[0:3]),
                edge(at_cot, 1, left[3:4]),
                edge(at_cot, 1, cot),
                edge(at_cot, 1, right[3:4]),
            ]
        )

    low = lax.ppermute(side(SY - 3, SY - 1), "gy", [(i, i + 1) for i in range(3)])
    high = lax.ppermute(side(0, 0), "gy", [(i + 1, i) for i in range(3)])

    pieces = gathered_weights(master, dp, core, gy)
    act, send, keep = device_step(place, vol, left, right, low, high, cot, pieces)

    pair = (keep + shifted(send, "c", 2, 1).astype(F32)).astype(BF)
    spread = pair.reshape(4, 16, PIECE, C).transpose(1, 0, 2, 3)
    plane = lax.all_to_all(spread, ("x", "gy"), 0, 0)
    plane = jnp.sum(plane.astype(F32), axis=0).astype(BF)
    twice = jnp.broadcast_to(plane[:, None], (4, 2, PIECE, C)).reshape(8, PIECE, C)
    column = lax.all_to_all(twice, ("dp", "zl"), 0, 0)
    column = jnp.sum(column.astype(F32), axis=0).astype(BF)
    mine = lax.all_to_all(jnp.broadcast_to(column, (16, PIECE, C)), ("x", "gy"), 0, 0).reshape(HALF, C)
    other = shifted(mine, "c", 2, 1)
    new_master, new_one, new_two = adam_update(place, mine, other, master, moment_one, moment_two)
    return (act[None], new_master, new_one, new_two)


def solution(mesh):
    fine = Mesh(mesh.devices.reshape(4, 2, 4, 2, 4), ("dp", "zl", "x", "c", "gy"))
    cells = P("dp", GX, "gy", None, None)
    rows = P("dp", None)
    return jax.shard_map(
        per_device,
        mesh=fine,
        in_specs=(cells, cells, rows, rows, rows),
        out_specs=(cells, rows, rows, rows),
        check_vma=False,
    )
```

time: 500 us -> 116 us (0.23)
  blocking collectives: 308 us -> 43.3 us
  waiting for transfers between devices: 98.6 us -> 19.9 us
  matrix products: 32.8 us -> 0 us
  between operations: 16.2 us -> 0.94 us
  Pallas kernels: 0 us -> 11.2 us
  other arithmetic: 10.4 us -> 3 us
    psum x1 -> x0, blocking collectives: 308 us -> none  [per_device(): summed = lax.psum(gradient, ('gx', 'gy'))]
    reduce_scatter x1 -> x0, waiting for transfers between devices: 51.2 us -> none  [per_device(): lax.psum_scatter(summed.astype(jnp.bfloat16), 'dp', scatter_dimension=0,...]
    all_to_all x0 -> x3, blocking collectives: none -> 43.3 us  [the longest x1 21.7 us: per_device(): plane = lax.all_to_all(spread, ('x', 'gy'), 0, 0)]
    dot_general x135 -> x0, matrix products: 32.8 us -> none  [the longest x81 20.5 us: convolve(): jnp.dot(window.reshape(-1, padded.shape[3]), kernel[9 * offset_x + 3 * of...]
    all_gather x1 -> x0, waiting for transfers between devices: 29.4 us -> none  [per_device(): full_weights = lax.all_gather(local_weights, 'dp', axis=0, tiled=True)]
    pallas_call x0 -> x2, Pallas kernels: none -> 11.2 us  [the longest x1 8.21 us: device_step(): pl.pallas_call(step_kernel, out_shape=(jax.ShapeDtypeStruct((SX, SY, SZ,...]
    ppermute x12 -> x16, starting transfers between devices: 30.2 us -> 34.7 us  [the longest x1 15 us: per_device(): left = lax.ppermute(jnp.concatenate([vol[1:4], cot[3:4]]), GX, up_x)]
    ppermute x12 -> x16, waiting for transfers between devices: 17.9 us -> 19.9 us  [the longest x9 13.6 us: shifted(): lax.ppermute(cells, axis, [(i, (i + by) % count) for i in range(count)])]
  transfers between devices with their start and end apart: 14 -> 16, of which waited for: 8 -> 7; matrix products, arithmetic and copies ran while one was open for 1% -> 2% of each run, Pallas kernels for 0% -> 0%
where the time goes in v1:
time: 116 us; the launch traced here: 115 us
  blocking collectives  43.3 us (37%)
  starting transfers between devices  34.7 us (30%)
  waiting for transfers between devices  19.9 us (17%)
  Pallas kernels  11.2 us (10%)
  other arithmetic  3 us (3%)
  local copies, waits for them, and re-layouts  2.03 us (2%)
    all_to_all x1, blocking collectives, per_device(): plane = lax.all_to_all(spread, ('x', 'gy'), 0, 0)  21.7 us
    ppermute x1, starting transfers between devices, per_device(): left = lax.ppermute(jnp.concatenate([vol[1:4], cot[3:4]]), GX, up_x)  15 us
    ppermute x9, waiting for transfers between devices, shifted(): lax.ppermute(cells, axis, [(i, (i + by) % count) for i in range(count)])  13.6 us
    ppermute x9, starting transfers between devices, shifted(): lax.ppermute(cells, axis, [(i, (i + by) % count) for i in range(count)])  11.9 us
    all_to_all x1, blocking collectives, per_device(): lax.all_to_all(jnp.broadcast_to(column, (16, PIECE, C)), ('x', 'gy'), 0, 0)  11.2 us
    all_to_all x1, blocking collectives, per_device(): column = lax.all_to_all(twice, ('dp', 'zl'), 0, 0)  10.5 us
    pallas_call x1, Pallas kernels, device_step(): pl.pallas_call(step_kernel, out_shape=(jax.ShapeDtypeStruct((SX, SY, SZ,...  8.21 us
    ppermute x1, waiting for transfers between devices, per_device(): high = lax.ppermute(side(0, 0), 'gy', [(i + 1, i) for i in range(3)])  4.47 us
  transfers between devices with their start and end apart: 16, of which 7 were waited for; matrix products, arithmetic and copies ran while one was open for 2% of the time, Pallas kernels for 0%

profile of v1, /device:TPU:1, one launch (start us, length us, event | category | flops | bytes accessed | tf_op | source)
XLA Modules:
  0.0 115.0 jit_solution(9435124300103734267)
XLA Ops:
  0.7 1.3 %convert_element_type.6 = bf16[1728,128]{1,0:T(8,128)(2,1)S(1)} convert(f32[1728,128]{1,0:T(8,128)} %master.1) | non-fusion elementwise | flops 221184 | bytes 1327104 | tf_op jit(solution)/shard_map/convert_element_type | solution.py:218
  1.9 1.3 %collective-permute-start.6 = (bf16[27,16,128]{2,1,0:T(8,128)(2,1)S(1)}, bf16[27,16,128]{2,1,0:T(8,128)(2,1)S(1)}, u32[]{:S(2)}, u32[]{:S(2)}) collective-permute-start(bf16[27,16,128]{2,1,0:T(8,128)(2,1)S(1)} %constant_dynamic-slice_fusion), channel_id=1, source_target_pairs={{196,4},{132,68},{64,128},{0,192},{197,5},{133,69},{65,129},{1,193... | collective-permute-start | bytes 331784 | tf_op jit(solution)/shard_map/ppermute | solution.py:221
  3.2 1.3 %collective-permute-start.5 = (bf16[27,16,128]{2,1,0:T(8,128)(2,1)S(1)}, bf16[27,16,128]{2,1,0:T(8,128)(2,1)S(1)}, u32[]{:S(2)}, u32[]{:S(2)}) collective-permute-start(bf16[27,16,128]{2,1,0:T(8,128)(2,1)S(1)} %constant_dynamic-slice_fusion), channel_id=1, source_target_pairs={{132,4},{196,68},{0,128},{64,192},{133,5},{197,69},{1,129},{65,193... | collective-permute-start | bytes 331784 | tf_op jit(solution)/shard_map/ppermute | solution.py:221
  4.5 0.7 collective-permute-start.4
  5.2 0.8 slice_bitcast_fusion.2
  6.0 1.0 slice_bitcast_fusion
  7.0 15.0 %collective-permute-start = (bf16[4,16,8,128]{3,2,1,0:T(8,128)(2,1)S(1)}, bf16[4,16,8,128]{3,2,1,0:T(8,128)(2,1)S(1)}, u32[]{:S(2)}, u32[]{:S(2)}) collective-permute-start(bf16[4,16,8,128]{3,2,1,0:T(8,128)(2,1)S(1)} %pad_maximum_fusion.1), channel_id=1, source_target_pairs={{0,4},{4,8},{8,12},{12,16},{16,20},{20,24},{24,28},{28,32},{32,36}... | collective-permute-start | bytes 393224 | tf_op jit(solution)/shard_map/ppermute | solution.py:251
  22.1 1.9 %collective-permute-start.1 = (bf16[4,16,8,128]{3,2,1,0:T(8,128)(2,1)S(1)}, bf16[4,16,8,128]{3,2,1,0:T(8,128)(2,1)S(1)}, u32[]{:S(2)}, u32[]{:S(2)}) collective-permute-start(bf16[4,16,8,128]{3,2,1,0:T(8,128)(2,1)S(1)} %pad_maximum_fusion.2), channel_id=1, source_target_pairs={{4,0},{8,4},{12,8},{16,12},{20,16},{24,20},{28,24},{32,28},{36,32}... | collective-permute-start | bytes 393224 | tf_op jit(solution)/shard_map/ppermute | solution.py:252
  24.3 2.8 %collective-permute-start.9 = (bf16[2,27,16,128]{3,2,1,0:T(8,128)(2,1)S(1)}, bf16[2,27,16,128]{3,2,1,0:T(8,128)(2,1)S(1)}, u32[]{:S(2)}, u32[]{:S(2)}) collective-permute-start(bf16[2,27,16,128]{3,2,1,0:T(8,128)(2,1)S(1)} %pad_maximum_fusion.rest_0_), channel_id=1, source_target_pairs={{0,3},{1,0},{2,1},{3,2},{4,7},{5,4},{6,5},{7,6},{8,11},{9,8},{10,9... | collective-permute-start | bytes 663560 | tf_op jit(solution)/shard_map/ppermute | solution.py:214
  27.1 0.3 collective-permute-start.8
  27.5 0.7 collective-permute-start.7
  28.2 0.4 collective-permute-done.1.right
  28.7 7.4 %collective-permute-done.9.rest_3_ = bf16[2,27,16,128]{3,2,1,0:T(8,128)(2,1)S(1)} collective-permute-done((bf16[2,27,16,128]{3,2,1,0:T(8,128)(2,1)S(1)}, bf16[2,27,16,128]{3,2,1,0:T(8,128)(2,1)S(1)}, u32[]{:S(2)}, u32[]{:S(2)}) %collective-permute-start.9) | collective-permute-done | bytes 221216 | tf_op jit(solution)/shard_map/ppermute | solution.py:214
  36.1 1.4 %collective-permute-start.13 = (bf16[2,27,16,128]{3,2,1,0:T(8,128)(2,1)S(1)}, bf16[2,27,16,128]{3,2,1,0:T(8,128)(2,1)S(1)}, u32[]{:S(2)}, u32[]{:S(2)}) collective-permute-start(bf16[2,27,16,128]{3,2,1,0:T(8,128)(2,1)S(1)} %collective-permute-done.9.rest_3_), channel_id=1, source_target_pairs={{0,4},{4,0},{1,5},{5,1},{2,6},{6,2},{3,7},{7,3},{8,12},{12,8},{9,1... | collective-permute-start | bytes 663560 | tf_op jit(solution)/shard_map/ppermute | solution.py:214
  37.5 0.2 collective-permute-start.12
  37.7 3.0 %collective-permute-done.7.rest_1_ = bf16[2,27,16,128]{3,2,1,0:T(8,128)(2,1)S(1)} collective-permute-done((bf16[2,27,16,128]{3,2,1,0:T(8,128)(2,1)S(1)}, bf16[2,27,16,128]{3,2,1,0:T(8,128)(2,1)S(1)}, u32[]{:S(2)}, u32[]{:S(2)}) %collective-permute-start.7) | collective-permute-done | bytes 221216 | tf_op jit(solution)/shard_map/ppermute | solution.py:214
  40.7 0.5 collective-permute-start.11
  41.2 1.3 %collective-permute-start.3 = (bf16[36,8,128]{2,1,0:T(8,128)(2,1)S(1)}, bf16[36,8,128]{2,1,0:T(8,128)(2,1)S(1)}, u32[]{:S(2)}, u32[]{:S(2)}) collective-permute-start(bf16[36,8,128]{2,1,0:T(8,128)(2,1)S(1)} %get-tuple-element.18), channel_id=1, source_target_pairs={{1,0},{2,1},{3,2},{5,4},{6,5},{7,6},{9,8},{10,9},{11,10},{13,12},{... | collective-permute-start | bytes 221192 | tf_op jit(solution)/shard_map/ppermute | solution.py:270
  42.5 4.5 %collective-permute-done.3.high = bf16[36,8,128]{2,1,0:T(8,128)(2,1)S(1)} collective-permute-done((bf16[36,8,128]{2,1,0:T(8,128)(2,1)S(1)}, bf16[36,8,128]{2,1,0:T(8,128)(2,1)S(1)}, u32[]{:S(2)}, u32[]{:S(2)}) %collective-permute-start.3) | collective-permute-done | bytes 73760 | tf_op jit(solution)/shard_map/ppermute | solution.py:270
  47.0 1.3 %collective-permute-start.2 = (bf16[36,8,128]{2,1,0:T(8,128)(2,1)S(1)}, bf16[36,8,128]{2,1,0:T(8,128)(2,1)S(1)}, u32[]{:S(2)}, u32[]{:S(2)}) collective-permute-start(bf16[36,8,128]{2,1,0:T(8,128)(2,1)S(1)} %get-tuple-element.19), channel_id=1, source_target_pairs={{0,1},{1,2},{2,3},{4,5},{5,6},{6,7},{8,9},{9,10},{10,11},{12,13},{... | collective-permute-start | bytes 221192 | tf_op jit(solution)/shard_map/ppermute | solution.py:269
  48.4 1.3 %collective-permute-done.2.low = bf16[36,8,128]{2,1,0:T(8,128)(2,1)S(1)} collective-permute-done((bf16[36,8,128]{2,1,0:T(8,128)(2,1)S(1)}, bf16[36,8,128]{2,1,0:T(8,128)(2,1)S(1)}, u32[]{:S(2)}, u32[]{:S(2)}) %collective-permute-start.2) | collective-permute-done | bytes 73760 | tf_op jit(solution)/shard_map/ppermute | solution.py:269
  49.7 8.2 %unet_step.1 = (bf16[4,16,8,128]{3,2,1,0:T(8,128)(2,1)}, bf16[4,896,128]{2,1,0:T(8,128)(2,1)S(1)}, f32[4,896,128]{2,1,0:T(8,128)S(1)}) custom-call(s32[4]{0:T(128)S(1)} %pad_add_fusion.place, bf16[4,16,8,128]{3,2,1,0:T(8,128)(2,1)S(1)} %bitcast.59, bf16[4,16,8,128]{3,2,1,0:T(8,128)(2,1)S(1)} %collective-permute-done.left, ...), custom_call_target="tpu_custom_call" | custom-call | flops 3500000000 | bytes 8000000 | tf_op jit(solution)/shard_map/unet_step/pallas_call | solution.py:157
  57.9 1.5 %collective-permute-start.14 = (bf16[4,896,128]{2,1,0:T(8,128)(2,1)S(1)}, bf16[4,896,128]{2,1,0:T(8,128)(2,1)S(1)}, u32[]{:S(2)}, u32[]{:S(2)}) collective-permute-start(bf16[4,896,128]{2,1,0:T(8,128)(2,1)S(1)} %get-tuple-element.12), channel_id=1, source_target_pairs={{0,4},{4,0},{1,5},{5,1},{2,6},{6,2},{3,7},{7,3},{8,12},{12,8},{9,1... | collective-permute-start | bytes 2752520 | tf_op jit(solution)/shard_map/ppermute | solution.py:214
  59.4 2.1 %collective-permute-done.14 = bf16[4,896,128]{2,1,0:T(8,128)(2,1)S(1)} collective-permute-done((bf16[4,896,128]{2,1,0:T(8,128)(2,1)S(1)}, bf16[4,896,128]{2,1,0:T(8,128)(2,1)S(1)}, u32[]{:S(2)}, u32[]{:S(2)}) %collective-permute-start.14) | collective-permute-done | bytes 917536 | tf_op jit(solution)/shard_map/ppermute | solution.py:214
  61.5 0.2 add_convert_fusion
  61.8 21.7 %all_to_all.15 = bf16[16,4,56,128]{3,2,1,0:T(8,128)(2,1)} all-to-all(bf16[16,4,56,128]{3,2,1,0:T(8,128)(2,1)S(1)} %bitcast.63), channel_id=1, replica_groups=mesh['dp'=4,'zl'=2,'x'=4,'c'=2,'gy'=4] {'x','gy'}, dimensions={0} | all-to-all | bytes 1835008 | tf_op jit(solution)/shard_map/all_to_all | solution.py:277
  83.5 1.3 %reduce_sum.24 = bf16[4,56,128]{2,1,0:T(8,128)(2,1)S(1)} reduce(bf16[16,4,56,128]{3,2,1,0:T(8,128)(2,1)} %all_to_all.15, bf16[]{:T(256)} %constant.35.clone.1), dimensions={0}, to_apply=%region_0.1 | reduce | flops 430080 | bytes 974850 | tf_op jit(solution)/shard_map/reduce_sum | solution.py:278
  84.9 10.5 %all_to_all.16 = bf16[8,56,128]{2,1,0:T(8,128)(2,1)S(1)} all-to-all(bf16[8,56,128]{2,1,0:T(8,128)(2,1)S(1)} %bitcast.66), channel_id=1, replica_groups=mesh['dp'=4,'zl'=2,'x'=4,'c'=2,'gy'=4] {'dp','zl'}, dimensions={0} | all-to-all | bytes 229376 | tf_op jit(solution)/shard_map/all_to_all | solution.py:280
  95.4 11.2 %all_to_all.17 = bf16[16,56,128]{2,1,0:T(8,128)(2,1)S(1)} all-to-all(bf16[16,56,128]{2,1,0:T(8,128)(2,1)S(1)} %broadcast_in_dim.14), channel_id=1, replica_groups=mesh['dp'=4,'zl'=2,'x'=4,'c'=2,'gy'=4] {'x','gy'}, dimensions={0} | all-to-all | bytes 458752 | tf_op jit(solution)/shard_map/all_to_all | solution.py:282
  106.5 4.4 %collective-permute-start.15 = (bf16[896,128]{1,0:T(8,128)(2,1)S(1)}, bf16[896,128]{1,0:T(8,128)(2,1)S(1)}, u32[]{:S(2)}, u32[]{:S(2)}) collective-permute-start(bf16[896,128]{1,0:T(8,128)(2,1)S(1)} %bitcast.56), channel_id=1, source_target_pairs={{0,4},{4,0},{1,5},{5,1},{2,6},{6,2},{3,7},{7,3},{8,12},{12,8},{9,1... | collective-permute-start | bytes 688136 | tf_op jit(solution)/shard_map/ppermute | solution.py:214
  110.9 1.1 collective-permute-done.15.other
  112.0 3.0 %adam_step.1 = (f32[1728,128]{1,0:T(8,128)}, f32[1728,128]{1,0:T(8,128)}, f32[1728,128]{1,0:T(8,128)}) custom-call(s32[4]{0:T(128)S(1)} %pad_add_fusion.place, bf16[896,128]{1,0:T(8,128)(2,1)S(1)} %bitcast.57, bf16[896,128]{1,0:T(8,128)(2,1)S(1)} %collective-permute-done.15.other, f32[1728,128]{1,0:T(8,128)S(1)} %copy-done, f32[1728,128]{1,0:T(8,128)S(1)} %copy-done.1, ...), custom_call_target="tpu_custom_call" | custom-call | tf_op jit(solution)/shard_map/adam_step/pallas_call | solution.py:199
  (41 shorter events, 0.6 us)
Async XLA Ops:
  0.6 23.4 %copy-start.3 = (bf16[1,4,16,8,128]{4,3,2,1,0:T(8,128)(2,1)S(1)}, bf16[1,4,16,8,128]{4,3,2,1,0:T(8,128)(2,1)}, u32[]{:S(2)}) copy-start(bf16[1,4,16,8,128]{4,3,2,1,0:T(8,128)(2,1)} %param.5) | copy-start | bytes 393220
  0.6 28.0 %copy-start.4 = (bf16[1,4,16,8,128]{4,3,2,1,0:T(8,128)(2,1)S(1)}, bf16[1,4,16,8,128]{4,3,2,1,0:T(8,128)(2,1)}, u32[]{:S(2)}) copy-start(bf16[1,4,16,8,128]{4,3,2,1,0:T(8,128)(2,1)} %param.6) | copy-start | bytes 393220
  1.9 22.1 %collective-permute-start.6 = (bf16[27,16,128]{2,1,0:T(8,128)(2,1)S(1)}, bf16[27,16,128]{2,1,0:T(8,128)(2,1)S(1)}, u32[]{:S(2)}, u32[]{:S(2)}) collective-permute-start(bf16[27,16,128]{2,1,0:T(8,128)(2,1)S(1)} %constant_dynamic-slice_fusion), channel_id=1, source_target_pairs={{196,4},{132,68},{64,128},{0,192},{197,5},{133,69},{65,129},{1,193... | collective-permute-start | bytes 331784 | tf_op jit(solution)/shard_map/ppermute | solution.py:221
  3.2 20.8 %collective-permute-start.5 = (bf16[27,16,128]{2,1,0:T(8,128)(2,1)S(1)}, bf16[27,16,128]{2,1,0:T(8,128)(2,1)S(1)}, u32[]{:S(2)}, u32[]{:S(2)}) collective-permute-start(bf16[27,16,128]{2,1,0:T(8,128)(2,1)S(1)} %constant_dynamic-slice_fusion), channel_id=1, source_target_pairs={{132,4},{196,68},{0,128},{64,192},{133,5},{197,69},{1,129},{65,193... | collective-permute-start | bytes 331784 | tf_op jit(solution)/shard_map/ppermute | solution.py:221
  4.5 19.5 %collective-permute-start.4 = (bf16[27,16,128]{2,1,0:T(8,128)(2,1)S(1)}, bf16[27,16,128]{2,1,0:T(8,128)(2,1)S(1)}, u32[]{:S(2)}, u32[]{:S(2)}) collective-permute-start(bf16[27,16,128]{2,1,0:T(8,128)(2,1)S(1)} %constant_dynamic-slice_fusion), channel_id=1, source_target_pairs={{64,0},{0,64},{196,132},{132,196},{65,1},{1,65},{197,133},{133,197... | collective-permute-start | bytes 331784 | tf_op jit(solution)/shard_map/ppermute | solution.py:221
  7.0 20.5 %collective-permute-start = (bf16[4,16,8,128]{3,2,1,0:T(8,128)(2,1)S(1)}, bf16[4,16,8,128]{3,2,1,0:T(8,128)(2,1)S(1)}, u32[]{:S(2)}, u32[]{:S(2)}) collective-permute-start(bf16[4,16,8,128]{3,2,1,0:T(8,128)(2,1)S(1)} %pad_maximum_fusion.1), channel_id=1, source_target_pairs={{0,4},{4,8},{8,12},{12,16},{16,20},{20,24},{24,28},{28,32},{32,36}... | collective-permute-start | bytes 393224 | tf_op jit(solution)/shard_map/ppermute | solution.py:251
  22.1 6.6 %collective-permute-start.1 = (bf16[4,16,8,128]{3,2,1,0:T(8,128)(2,1)S(1)}, bf16[4,16,8,128]{3,2,1,0:T(8,128)(2,1)S(1)}, u32[]{:S(2)}, u32[]{:S(2)}) collective-permute-start(bf16[4,16,8,128]{3,2,1,0:T(8,128)(2,1)S(1)} %pad_maximum_fusion.2), channel_id=1, source_target_pairs={{4,0},{8,4},{12,8},{16,12},{20,16},{24,20},{28,24},{32,28},{36,32}... | collective-permute-start | bytes 393224 | tf_op jit(solution)/shard_map/ppermute | solution.py:252
  24.2 25.5 %collective-permute-start.10 = (bf16[2,27,16,128]{3,2,1,0:T(8,128)(2,1)S(1)}, bf16[2,27,16,128]{3,2,1,0:T(8,128)(2,1)S(1)}, u32[]{:S(2)}, u32[]{:S(2)}) collective-permute-start(bf16[2,27,16,128]{3,2,1,0:T(8,128)(2,1)S(1)} %pad_maximum_fusion.rest_0_), channel_id=1, source_target_pairs={{0,4},{4,0},{1,5},{5,1},{2,6},{6,2},{3,7},{7,3},{8,12},{12,8},{9,1... | collective-permute-start | bytes 663560 | tf_op jit(solution)/shard_map/ppermute | solution.py:214
  24.3 11.8 %collective-permute-start.9 = (bf16[2,27,16,128]{3,2,1,0:T(8,128)(2,1)S(1)}, bf16[2,27,16,128]{3,2,1,0:T(8,128)(2,1)S(1)}, u32[]{:S(2)}, u32[]{:S(2)}) collective-permute-start(bf16[2,27,16,128]{3,2,1,0:T(8,128)(2,1)S(1)} %pad_maximum_fusion.rest_0_), channel_id=1, source_target_pairs={{0,3},{1,0},{2,1},{3,2},{4,7},{5,4},{6,5},{7,6},{8,11},{9,8},{10,9... | collective-permute-start | bytes 663560 | tf_op jit(solution)/shard_map/ppermute | solution.py:214
  27.1 10.4 %collective-permute-start.8 = (bf16[2,27,16,128]{3,2,1,0:T(8,128)(2,1)S(1)}, bf16[2,27,16,128]{3,2,1,0:T(8,128)(2,1)S(1)}, u32[]{:S(2)}, u32[]{:S(2)}) collective-permute-start(bf16[2,27,16,128]{3,2,1,0:T(8,128)(2,1)S(1)} %pad_maximum_fusion.rest_0_), channel_id=1, source_target_pairs={{0,2},{1,3},{2,0},{3,1},{4,6},{5,7},{6,4},{7,5},{8,10},{9,11},{10,... | collective-permute-start | bytes 663560 | tf_op jit(solution)/shard_map/ppermute | solution.py:214
  27.5 13.2 %collective-permute-start.7 = (bf16[2,27,16,128]{3,2,1,0:T(8,128)(2,1)S(1)}, bf16[2,27,16,128]{3,2,1,0:T(8,128)(2,1)S(1)}, u32[]{:S(2)}, u32[]{:S(2)}) collective-permute-start(bf16[2,27,16,128]{3,2,1,0:T(8,128)(2,1)S(1)} %pad_maximum_fusion.rest_0_), channel_id=1, source_target_pairs={{0,1},{1,2},{2,3},{3,0},{4,5},{5,6},{6,7},{7,4},{8,9},{9,10},{10,1... | collective-permute-start | bytes 663560 | tf_op jit(solution)/shard_map/ppermute | solution.py:214
  36.1 13.6 %collective-permute-start.13 = (bf16[2,27,16,128]{3,2,1,0:T(8,128)(2,1)S(1)}, bf16[2,27,16,128]{3,2,1,0:T(8,128)(2,1)S(1)}, u32[]{:S(2)}, u32[]{:S(2)}) collective-permute-start(bf16[2,27,16,128]{3,2,1,0:T(8,128)(2,1)S(1)} %collective-permute-done.9.rest_3_), channel_id=1, source_target_pairs={{0,4},{4,0},{1,5},{5,1},{2,6},{6,2},{3,7},{7,3},{8,12},{12,8},{9,1... | collective-permute-start | bytes 663560 | tf_op jit(solution)/shard_map/ppermute | solution.py:214
  37.5 12.2 %collective-permute-start.12 = (bf16[2,27,16,128]{3,2,1,0:T(8,128)(2,1)S(1)}, bf16[2,27,16,128]{3,2,1,0:T(8,128)(2,1)S(1)}, u32[]{:S(2)}, u32[]{:S(2)}) collective-permute-start(bf16[2,27,16,128]{3,2,1,0:T(8,128)(2,1)S(1)} %collective-permute-done.8.rest_2_), channel_id=1, source_target_pairs={{0,4},{4,0},{1,5},{5,1},{2,6},{6,2},{3,7},{7,3},{8,12},{12,8},{9,1... | collective-permute-start | bytes 663560 | tf_op jit(solution)/shard_map/ppermute | solution.py:214
  40.7 9.0 %collective-permute-start.11 = (bf16[2,27,16,128]{3,2,1,0:T(8,128)(2,1)S(1)}, bf16[2,27,16,128]{3,2,1,0:T(8,128)(2,1)S(1)}, u32[]{:S(2)}, u32[]{:S(2)}) collective-permute-start(bf16[2,27,16,128]{3,2,1,0:T(8,128)(2,1)S(1)} %collective-permute-done.7.rest_1_), channel_id=1, source_target_pairs={{0,4},{4,0},{1,5},{5,1},{2,6},{6,2},{3,7},{7,3},{8,12},{12,8},{9,1... | collective-permute-start | bytes 663560 | tf_op jit(solution)/shard_map/ppermute | solution.py:214
  41.2 5.8 %collective-permute-start.3 = (bf16[36,8,128]{2,1,0:T(8,128)(2,1)S(1)}, bf16[36,8,128]{2,1,0:T(8,128)(2,1)S(1)}, u32[]{:S(2)}, u32[]{:S(2)}) collective-permute-start(bf16[36,8,128]{2,1,0:T(8,128)(2,1)S(1)} %get-tuple-element.18), channel_id=1, source_target_pairs={{1,0},{2,1},{3,2},{5,4},{6,5},{7,6},{9,8},{10,9},{11,10},{13,12},{... | collective-permute-start | bytes 221192 | tf_op jit(solution)/shard_map/ppermute | solution.py:270
  47.0 2.7 %collective-permute-start.2 = (bf16[36,8,128]{2,1,0:T(8,128)(2,1)S(1)}, bf16[36,8,128]{2,1,0:T(8,128)(2,1)S(1)}, u32[]{:S(2)}, u32[]{:S(2)}) collective-permute-start(bf16[36,8,128]{2,1,0:T(8,128)(2,1)S(1)} %get-tuple-element.19), channel_id=1, source_target_pairs={{0,1},{1,2},{2,3},{4,5},{5,6},{6,7},{8,9},{9,10},{10,11},{12,13},{... | collective-permute-start | bytes 221192 | tf_op jit(solution)/shard_map/ppermute | solution.py:269
  57.9 3.6 %collective-permute-start.14 = (bf16[4,896,128]{2,1,0:T(8,128)(2,1)S(1)}, bf16[4,896,128]{2,1,0:T(8,128)(2,1)S(1)}, u32[]{:S(2)}, u32[]{:S(2)}) collective-permute-start(bf16[4,896,128]{2,1,0:T(8,128)(2,1)S(1)} %get-tuple-element.12), channel_id=1, source_target_pairs={{0,4},{4,0},{1,5},{5,1},{2,6},{6,2},{3,7},{7,3},{8,12},{12,8},{9,1... | collective-permute-start | bytes 2752520 | tf_op jit(solution)/shard_map/ppermute | solution.py:214
  61.8 50.2 %copy-start = (f32[1728,128]{1,0:T(8,128)S(1)}, f32[1728,128]{1,0:T(8,128)}, u32[]{:S(2)}) copy-start(f32[1728,128]{1,0:T(8,128)} %master.1) | copy-start | bytes 2654212
  61.8 50.2 %copy-start.1 = (f32[1728,128]{1,0:T(8,128)S(1)}, f32[1728,128]{1,0:T(8,128)}, u32[]{:S(2)}) copy-start(f32[1728,128]{1,0:T(8,128)} %one.1) | copy-start | bytes 2654212
  61.8 50.2 %copy-start.2 = (f32[1728,128]{1,0:T(8,128)S(1)}, f32[1728,128]{1,0:T(8,128)}, u32[]{:S(2)}) copy-start(f32[1728,128]{1,0:T(8,128)} %two.1) | copy-start | bytes 2654212
  106.5 5.5 %collective-permute-start.15 = (bf16[896,128]{1,0:T(8,128)(2,1)S(1)}, bf16[896,128]{1,0:T(8,128)(2,1)S(1)}, u32[]{:S(2)}, u32[]{:S(2)}) collective-permute-start(bf16[896,128]{1,0:T(8,128)(2,1)S(1)} %bitcast.56), channel_id=1, source_target_pairs={{0,4},{4,0},{1,5},{5,1},{2,6},{6,2},{3,7},{7,3},{8,12},{12,8},{9,1... | collective-permute-start | bytes 688136 | tf_op jit(solution)/shard_map/ppermute | solution.py:214

commit v2 on v1

v2 whole, which is shorter than its diff:
```python
import jax
import jax.numpy as jnp
from jax import lax
from jax.experimental import pallas as pl
from jax.experimental.pallas import tpu as pltpu
from jax.sharding import Mesh
from jax.sharding import PartitionSpec as P

inv_root_two = 0.7071067811865476
inv_root_tau = 0.3989422804014327
beta_one = 0.9
beta_two = 0.999
learn_rate = 0.01
epsilon = 1e-08

BF = jnp.bfloat16
F32 = jnp.float32

C = 128
SX, SY, SZ = 4, 16, 8
NX, NY = 64, 64
TAPS = 14
HALF = TAPS // 2 * C
PIECE = HALF // 16


def position():
    x, core, gy = lax.axis_index("x"), lax.axis_index("c"), lax.axis_index("gy")
    gx = (lax.axis_index("zl") * 4 + x) * 2 + core
    return gx, gy, core, lax.axis_index("dp"), gy ^ (2 * lax.rem(x, 2) + lax.div(x, 2))


def gelu_value(field):
    return 0.5 * field * (1.0 + lax.erf(field * inv_root_two))


def gelu_slope(field):
    normal_cdf = 0.5 * (1.0 + lax.erf(field * inv_root_two))
    return normal_cdf + field * jnp.exp(-0.5 * field * field) * inv_root_tau


def depth_triple(field):
    depth = lax.broadcasted_iota(jnp.int32, field.shape, 2)
    below = jnp.where(depth == 0, 0.0, pltpu.roll(field, 1, 2))
    above = jnp.where(depth == SZ - 1, 0.0, pltpu.roll(field, SZ - 1, 2))
    return [part.reshape(-1, C).astype(BF) for part in (below, field, above)]


def store_triple(ref, rows, field):
    for position, part in enumerate(depth_triple(field)):
        ref[rows, position * C : (position + 1) * C] = part


def conv_rows(ref, planes_out, wide, weights):
    rows = planes_out * wide * SZ
    step = wide * SZ
    left = jnp.concatenate([ref[a * step : a * step + rows, :] for a in range(3)], axis=1)
    prod = jnp.dot(left, weights, preferred_element_type=F32).reshape(planes_out, wide, SZ, 3 * C)
    return (
        prod[:, 0 : wide - 2, :, 0:C]
        + prod[:, 1 : wide - 1, :, C : 2 * C]
        + prod[:, 2:wide, :, 2 * C : 3 * C]
    )


def layer_weights(taps, layer):
    columns = []
    for b in range(3):
        rows = [(layer * 27 + 9 * a + 3 * b) * C for a in range(3)]
        columns.append(jnp.concatenate([taps[r : r + 3 * C] for r in rows], axis=0))
    return jnp.concatenate(columns, axis=1)


def grad_taps(grads, layer, ref, wide, first_plane, shift, delta):
    lefts = []
    for b in range(3):
        before, after = shift + b, wide - SY - shift - b
        padded = jnp.concatenate(
            [
                jnp.zeros((SX, before, SZ, C), F32),
                delta,
                jnp.zeros((SX, after, SZ, C), F32),
            ],
            axis=1,
        ).reshape(SX * wide * SZ, C)
        lefts.append(jnp.transpose(padded).astype(BF))
    left = jnp.concatenate(lefts, axis=0)
    step = wide * SZ
    for a in range(3):
        start = (first_plane + a) * step
        prod = jnp.dot(left, ref[start : start + SX * step, :], preferred_element_type=F32)
        for b in range(3):
            for c in range(3):
                grads[layer * 27 + 9 * a + 3 * b + c] = prod[b * C : (b + 1) * C, c * C : (c + 1) * C]


def payload_kernel(vol, cot, master, whole, half, near, far, first, last, rows, sems):
    gx, gy, core, dp, quarter = position()
    moves = [
        (master.at[:, pl.ds(pl.multiple_of(16 * quarter, 16), 16), :], rows),
        (vol.at[pl.ds(1 - core, 3)], near.at[0:3]),
        (vol.at[pl.ds(core, 3)], far.at[0:3]),
        (cot.at[pl.ds(3 * (1 - core), 1)], near.at[3:4]),
        (cot.at[pl.ds(3 * core, 1)], far.at[3:4]),
        (vol.at[:, 0:3], first.at[:, 0:3]),
        (cot.at[:, 0:1], first.at[:, 3:4]),
        (vol.at[:, SY - 3 : SY], last.at[:, 0:3]),
        (cot.at[:, SY - 1 : SY], last.at[:, 3:4]),
    ]
    copies = [pltpu.make_async_copy(src, dst, sems.at[i]) for i, (src, dst) in enumerate(moves)]
    for copy in copies:
        copy.start()
    copies[0].wait()
    whole[...] = rows[...].astype(BF)
    half[...] = rows[pl.ds(13 * core, 14)].astype(BF)
    for copy in copies[1:]:
        copy.wait()


def payloads(vol, cot, master):
    vmem = pl.BlockSpec(memory_space=pltpu.VMEM)
    hbm = pl.BlockSpec(memory_space=pltpu.HBM)
    side = pltpu.VMEM((4, SY, SZ, C), BF)
    edge = pltpu.VMEM((4, 4, SZ, C), BF)
    return pl.pallas_call(
        payload_kernel,
        out_shape=(
            pltpu.VMEM((27, 16, C), BF),
            pltpu.VMEM((14, 16, C), BF),
            side,
            side,
            edge,
            edge,
        ),
        in_specs=[hbm] * 3,
        out_specs=(vmem,) * 6,
        scratch_shapes=[pltpu.VMEM((27, 16, C), F32), pltpu.SemaphoreType.DMA((9,))],
        compiler_params=pltpu.CompilerParams(vmem_limit_bytes=8 * 2**20),
        name="payloads",
    )(*(pltpu.with_memory_space_constraint(a, pltpu.HBM) for a in (vol, cot, master.reshape(27, 64, C))))


SIDE = 36 * SZ // 16


def relay_kernel(stack, near, far, first, last, even, odd):
    gx, gy, core, dp, quarter = position()
    parity = lax.rem(gy, 2)
    even[0:41] = stack[...]
    odd[0:41] = stack[...]
    for out, upper in ((even, 1 - parity), (odd, parity)):
        own = jnp.where(upper == 0, first[...].astype(F32), last[...].astype(F32)).astype(BF)
        groups = []
        for part, planes in ((near, 3), (own, 4), (far, 3)):
            rows = part[:, 0:3] if planes == 4 else part[0:3, pl.ds(upper * (SY - 3), 3)]
            groups.append(rows.reshape(-1, SZ, C))
        for part, planes in ((near, 1), (own, 4), (far, 1)):
            rows = part[:, 3:4] if planes == 4 else part[3:4, pl.ds(upper * (SY - 1), 1)]
            groups.append(rows.reshape(-1, SZ, C))
        out[41 : 41 + SIDE] = jnp.concatenate(groups).reshape(SIDE, 16, C)


def relay(stack, near, far, first, last):
    vmem = pl.BlockSpec(memory_space=pltpu.VMEM)
    both = jax.ShapeDtypeStruct((41 + SIDE, 16, C), BF)
    return pl.pallas_call(
        relay_kernel,
        out_shape=(both, both),
        in_specs=[vmem] * 5,
        out_specs=(vmem,) * 2,
        compiler_params=pltpu.CompilerParams(vmem_limit_bytes=8 * 2**20),
        name="relay",
    )(stack, near, far, first, last)


def prepare_kernel(vol, cot, near, far, even, odd, field, upstream):
    gx, gy, core, dp, quarter = position()
    parity = lax.rem(gy, 2)

    def ordered(first, second, swap):
        return jnp.where(swap == 0, first, second), jnp.where(swap == 0, second, first)

    left, right = ordered(far[...].astype(F32), near[...].astype(F32), core)
    even_side = even[41 : 41 + SIDE].reshape(36, SZ, C).astype(F32)
    odd_side = odd[41 : 41 + SIDE].reshape(36, SZ, C).astype(F32)
    low, high = ordered(odd_side, even_side, parity)
    low = jnp.where(gy == 0, 0.0, low)
    high = jnp.where(gy == 3, 0.0, high)
    sides = []
    for side in (low, high):
        lower, upper = ordered(side[21:30], side[0:9], core)
        sides.append(jnp.concatenate([lower, side[9:21], upper]).reshape(10, 3, SZ, C))
        lower, upper = ordered(side[35:36], side[30:31], core)
        sides.append(jnp.concatenate([lower, side[31:35], upper]).reshape(6, 1, SZ, C))
    own = jnp.concatenate([left[0:3], vol[...].astype(F32), right[0:3]], axis=0)
    store_triple(field, slice(0, 1760), jnp.concatenate([sides[0], own, sides[2]], axis=1))
    own = jnp.concatenate([left[3:4], cot[...].astype(F32), right[3:4]], axis=0)
    upstream[...] = jnp.concatenate([sides[1], own, sides[3]], axis=1)


def prepare(vol, cot, near, far, even, odd):
    vmem = pl.BlockSpec(memory_space=pltpu.VMEM)
    return pl.pallas_call(
        prepare_kernel,
        out_shape=(
            jax.ShapeDtypeStruct((10 * 176, 3 * C), BF),
            jax.ShapeDtypeStruct((6, 18, SZ, C), F32),
        ),
        in_specs=[vmem] * 6,
        out_specs=(vmem, vmem),
        compiler_params=pltpu.CompilerParams(vmem_limit_bytes=16 * 2**20),
        cost_estimate=pl.CostEstimate(flops=4_000_000, bytes_accessed=3_000_000, transcendentals=0),
        name="prepare",
    )(vol, cot, near, far, even, odd)


def step_kernel(field, upstream, master, *rest):
    pieces = rest[:8]
    act, send, keep = rest[8:11]
    taps, flipped, hid, dlt, grads = rest[11:]
    gx, gy, core, dp, quarter = position()

    taps[pl.ds(dp * 27, 27)] = master[...].astype(BF).reshape(27, 64, C)
    for index, piece in enumerate(pieces):
        owner_core = core if index < 4 else 1 - core
        rows = pl.ds(pl.multiple_of((quarter ^ (0, 1, 3, 2)[index % 4]) * 16, 16), 16)
        whole = dp ^ (1 + owner_core)
        taps[pl.ds(whole * 27, 27), rows, :] = piece[0:27]
        taps[pl.ds((dp ^ 3) * 27 + 13 * owner_core, 14), rows, :] = piece[27:41]
    tap_rows = taps[...].reshape(54 * C, C)

    first = conv_rows(field, 8, 22, layer_weights(tap_rows, 0))
    x_at = lax.broadcasted_iota(jnp.int32, first.shape, 0) + (gx * SX - 2)
    y_at = lax.broadcasted_iota(jnp.int32, first.shape, 1) + (gy * SY - 2)
    inside = (x_at >= 0) & (x_at < NX) & (y_at >= 0) & (y_at < NY)
    hidden = jnp.where(inside, gelu_value(first), 0.0)
    slope_one = gelu_slope(first[2:6, 2:18])
    store_triple(hid, slice(0, 8 * 160), hidden)

    second = conv_rows(hid, 6, 20, layer_weights(tap_rows, 1))
    act[...] = gelu_value(second[1:5, 1:17]).astype(BF)
    delta_two = upstream[...] * gelu_slope(second)
    store_triple(dlt, slice(0, 6 * 144), delta_two)
    grad_taps(grads, 1, hid, 20, 1, 1, delta_two[1:5, 1:17])

    for t in range(27):
        a, b, c = t // 9, t // 3 % 3, t % 3
        row = (27 + 26 - t) * C
        block = jnp.transpose(tap_rows[row : row + C].astype(F32)).astype(BF)
        flipped[(3 * a + c) * C : (3 * a + c + 1) * C, b * C : (b + 1) * C] = block
    back = conv_rows(dlt, 4, 18, flipped[...])
    grad_taps(grads, 0, field, 22, 2, 2, back * slope_one)

    for shard in range(4):
        base = 27 * (shard // 2) + 13 * (shard % 2)
        keep[shard] = grads[pl.ds(base + 7 * core, 7)].reshape(HALF, C)
        send[shard] = grads[pl.ds(base + 7 * (1 - core), 7)].reshape(HALF, C).astype(BF)


def device_step(field, upstream, master, pieces):
    vmem = pl.BlockSpec(memory_space=pltpu.VMEM)
    return pl.pallas_call(
        step_kernel,
        out_shape=(
            jax.ShapeDtypeStruct((SX, SY, SZ, C), BF),
            jax.ShapeDtypeStruct((4, HALF, C), BF),
            jax.ShapeDtypeStruct((4, HALF, C), F32),
        ),
        in_specs=[vmem] * 11,
        out_specs=(vmem, vmem, vmem),
        scratch_shapes=[
            pltpu.VMEM((108, 64, C), BF),
            pltpu.VMEM((9 * C, 3 * C), BF),
            pltpu.VMEM((8 * 160, 3 * C), BF),
            pltpu.VMEM((6 * 144, 3 * C), BF),
            pltpu.VMEM((54, C, C), F32),
        ],
        compiler_params=pltpu.CompilerParams(vmem_limit_bytes=44 * 2**20),
        cost_estimate=pl.CostEstimate(flops=3_500_000_000, bytes_accessed=8_000_000, transcendentals=1_000_000),
        name="unet_step",
    )(field, upstream, master, *pieces)


ADAM_ROWS = 576


def adam_kernel(mine, other, master, one, two, new_master, new_one, new_two, grad, parts, sems):
    gx, gy, core, dp, quarter = position()
    odd = lax.rem(dp, 2)
    for source, owner in ((mine, core), (other, 1 - core)):
        for tap in range(TAPS // 2):
            block = source[tap * C : (tap + 1) * C].astype(F32)
            grad[pl.ds(pl.multiple_of((owner * (TAPS // 2) + tap) * C, C), C), :] = jnp.transpose(block)
    copies = []
    for chunk in range(master.shape[0] // ADAM_ROWS):
        rows = pl.ds(chunk * ADAM_ROWS, ADAM_ROWS)
        shifted_rows = pl.ds(pl.multiple_of(odd * (C // 2) + chunk * ADAM_ROWS, C // 2), ADAM_ROWS)
        gradient = grad[shifted_rows, :]
        first = beta_one * one[rows, :] + (1.0 - beta_one) * gradient
        second = beta_two * two[rows, :] + (1.0 - beta_two) * gradient * gradient
        update = first / (1.0 - beta_one**10) / (jnp.sqrt(second / (1.0 - beta_two**10)) + epsilon)
        parts[0, rows, :] = master[rows, :] - learn_rate * update
        parts[1, rows, :] = first
        parts[2, rows, :] = second
        for index, out in enumerate((new_master, new_one, new_two)):
            copy = pltpu.make_async_copy(parts.at[index, rows], out.at[rows], sems.at[chunk, index])
            copy.start()
            copies.append(copy)
    for copy in copies:
        copy.wait()


def adam_update(mine, other, master, one, two):
    vmem = pl.BlockSpec(memory_space=pltpu.VMEM)
    hbm = pl.BlockSpec(memory_space=pl.ANY)
    shape = jax.ShapeDtypeStruct(master.shape, F32)
    return pl.pallas_call(
        adam_kernel,
        out_shape=(shape, shape, shape),
        in_specs=[vmem] * 5,
        out_specs=(hbm, hbm, hbm),
        scratch_shapes=[
            pltpu.VMEM((TAPS * C, C), F32),
            pltpu.VMEM((3,) + master.shape, F32),
            pltpu.SemaphoreType.DMA((master.shape[0] // ADAM_ROWS, 3)),
        ],
        compiler_params=pltpu.CompilerParams(vmem_limit_bytes=24 * 2**20),
        name="adam_step",
    )(mine, other, master, one, two)


GX = ("zl", "x", "c")


def exchanged(cells, axis, count, by):
    return lax.ppermute(cells, axis, [(i, i ^ by) for i in range(count)])


def paired(cells, axis, count):
    pairs = [(i, i + 1) for i in range(1, count - 1, 2)]
    return lax.ppermute(cells, axis, pairs + [(j, i) for i, j in pairs])


def over_dp(whole, half):
    whole = lax.ppermute(
        whole, ("dp", "c"), [(2 * d + c, 2 * (d ^ (1 + c)) + c) for d in range(4) for c in range(2)]
    )
    return whole, exchanged(half, "dp", 4, 3)


def per_device(volume, cotangent, master, moment_one, moment_two):
    vol, cot = volume[0], cotangent[0]
    whole, half, near, far, first, last = payloads(vol, cot, master)
    whole, half = over_dp(whole, half)
    near = exchanged(near, "c", 2, 1)
    far = paired(far, GX, 16)

    stack = jnp.concatenate([whole, half])
    opposite = exchanged(stack, "x", 4, 1)
    even, odd = relay(stack, near, far, first, last)
    odd = exchanged(odd, "gy", 4, 3)
    even = exchanged(even, "gy", 4, 1)
    mine = [stack, even, odd, opposite]
    pieces = mine + [exchanged(part, "c", 2, 1) for part in mine]
    field, upstream = prepare(vol, cot, near, far, even, odd)
    act, send, keep = device_step(field, upstream, master, pieces)

    pair = (keep + exchanged(send, "c", 2, 1).astype(F32)).astype(BF)
    spread = pair.reshape(4, 16, PIECE, C).transpose(1, 0, 2, 3).reshape(16, 4 * PIECE, C)
    plane = lax.all_to_all(spread, ("x", "gy"), 0, 0)
    plane = jnp.sum(plane.astype(F32), axis=0).astype(BF).reshape(4, PIECE, C)
    twice = jnp.broadcast_to(plane[:, None], (4, 2, PIECE, C)).reshape(8, PIECE, C)
    column = lax.all_to_all(twice, ("dp", "zl"), 0, 0)
    column = jnp.sum(column.astype(F32), axis=0).astype(BF)
    mine = lax.all_to_all(jnp.broadcast_to(column, (16, PIECE, C)), ("x", "gy"), 0, 0).reshape(HALF, C)
    other = exchanged(mine, "c", 2, 1)
    new_master, new_one, new_two = adam_update(mine, other, master, moment_one, moment_two)
    return (act[None], new_master, new_one, new_two)


def solution(mesh):
    fine = Mesh(mesh.devices.reshape(4, 2, 4, 2, 4), ("dp", "zl", "x", "c", "gy"))
    cells = P("dp", GX, "gy", None, None)
    rows = P("dp", None)
    return jax.shard_map(
        per_device,
        mesh=fine,
        in_specs=(cells, cells, rows, rows, rows),
        out_specs=(cells, rows, rows, rows),
        check_vma=False,
    )
```

time: 116 us -> 93.3 us (0.80)
  starting transfers between devices: 34.7 us -> 22.5 us
  waiting for transfers between devices: 19.9 us -> 11.5 us
  blocking collectives: 43.3 us -> 45.2 us
  local copies, waits for them, and re-layouts: 2.03 us -> 0.17 us
  other arithmetic: 3 us -> 1.55 us
    ppermute x16 -> x13, starting transfers between devices: 34.7 us -> 22.5 us  [the longest x11 11.6 us: exchanged(): return lax.ppermute(cells, axis, [(i, i ^ by) for i in range(count)])]
    ppermute x16 -> x13, waiting for transfers between devices: 19.9 us -> 11.5 us  [the longest x11 9.53 us: exchanged(): return lax.ppermute(cells, axis, [(i, i ^ by) for i in range(count)])]
    all_to_all x1, blocking collectives: 10.5 us -> 12.4 us  [per_device(): column = lax.all_to_all(twice, ('dp', 'zl'), 0, 0)]
    slice x5 -> x0, local copies, waits for them, and re-layouts: 1.78 us -> none  [the longest x2 1.76 us: per_device(): right = lax.ppermute(jnp.concatenate([vol[0:3], cot[0:1]]), GX, down_x)]
    convert_element_type x2 -> x1, other arithmetic: 1.44 us -> 0.22 us  [per_device(): pair = (keep + exchanged(send, 'c', 2, 1).astype(F32)).astype(BF)]
    pallas_call x1 -> x4, Pallas kernels: 2.99 us -> 3.88 us  [the longest x1 2.18 us: adam_update(): pl.pallas_call(adam_kernel, out_shape=(shape, shape, shape), in_specs=[vm...]
  transfers between devices with their start and end apart: 16 -> 13, of which waited for: 7 -> 8; matrix products, arithmetic and copies ran while one was open for 2% -> 0% of each run, Pallas kernels for 0% -> 0%
where the time goes in v2:
time: 93.3 us; the launch traced here: 93.1 us
  blocking collectives  45.2 us (48%)
  starting transfers between devices  22.5 us (24%)
  waiting for transfers between devices  11.5 us (12%)
  Pallas kernels  11.2 us (12%)
  other arithmetic  1.55 us (2%)
    all_to_all x1, blocking collectives, per_device(): plane = lax.all_to_all(spread, ('x', 'gy'), 0, 0)  22.1 us
    all_to_all x1, blocking collectives, per_device(): column = lax.all_to_all(twice, ('dp', 'zl'), 0, 0)  12.4 us
    ppermute x11, starting transfers between devices, exchanged(): return lax.ppermute(cells, axis, [(i, i ^ by) for i in range(count)])  11.6 us
    all_to_all x1, blocking collectives, per_device(): lax.all_to_all(jnp.broadcast_to(column, (16, PIECE, C)), ('x', 'gy'), 0, 0)  10.8 us
    ppermute x11, waiting for transfers between devices, exchanged(): return lax.ppermute(cells, axis, [(i, i ^ by) for i in range(count)])  9.53 us
    ppermute x1, starting transfers between devices, over_dp(): lax.ppermute(whole, ('dp', 'c'), [(2 * d + c, 2 * (d ^ 1 + c) + c) for d...  7.83 us
    pallas_call x1, Pallas kernels, device_step(): pl.pallas_call(step_kernel, out_shape=(jax.ShapeDtypeStruct((SX, SY, SZ,...  7.36 us
    ppermute x1, starting transfers between devices, paired(): return lax.ppermute(cells, axis, pairs + [(j, i) for i, j in pairs])  3 us
  transfers between devices with their start and end apart: 13, of which 8 were waited for; matrix products, arithmetic and copies ran while one was open for 0% of the time, Pallas kernels for 0%

profile of v2, /device:TPU:1, one launch (start us, length us, event | category | flops | bytes accessed | tf_op | source)
XLA Modules:
  0.0 93.1 jit_solution(11581059406229168587)
XLA Ops:
  0.7 1.2 %payloads.1 = (bf16[27,16,128]{2,1,0:T(8,128)(2,1)S(1)}, bf16[14,16,128]{2,1,0:T(8,128)(2,1)S(1)}, bf16[4,16,8,128]{3,2,1,0:T(8,128)(2,1)S(1)}, bf16[4,16,8,128]...) custom-call(bf16[4,16,8,128]{3,2,1,0:T(8,128)(2,1)} %bitcast.14, ...), custom_call_target="tpu_custom_call" | custom-call | tf_op jit(solution)/shard_map/payloads/pallas_call | solution.py:125
  1.9 7.8 %collective-permute-start.2 = (bf16[27,16,128]{2,1,0:T(8,128)(2,1)S(1)}, bf16[27,16,128]{2,1,0:T(8,128)(2,1)S(1)}, u32[]{:S(2)}, u32[]{:S(2)}) collective-permute-start(bf16[27,16,128]{2,1,0:T(8,128)(2,1)S(1)} %get-tuple-element.22), channel_id=1, source_target_pairs={{0,64},{4,132},{64,0},{68,196},{128,192},{132,4},{192,128},{196,68... | collective-permute-start | bytes 331784 | tf_op jit(solution)/shard_map/ppermute | solution.py:345
  9.7 0.0 collective-permute-start.3
  9.7 1.5 %collective-permute-start = (bf16[4,16,8,128]{3,2,1,0:T(8,128)(2,1)S(1)}, bf16[4,16,8,128]{3,2,1,0:T(8,128)(2,1)S(1)}, u32[]{:S(2)}, u32[]{:S(2)}) collective-permute-start(bf16[4,16,8,128]{3,2,1,0:T(8,128)(2,1)S(1)} %get-tuple-element.20), channel_id=1, source_target_pairs={{0,4},{4,0},{1,5},{5,1},{2,6},{6,2},{3,7},{7,3},{8,12},{12,8},{9,1... | collective-permute-start | bytes 393224 | tf_op jit(solution)/shard_map/ppermute | solution.py:336
  11.3 3.0 %collective-permute-start.1 = (bf16[4,16,8,128]{3,2,1,0:T(8,128)(2,1)S(1)}, bf16[4,16,8,128]{3,2,1,0:T(8,128)(2,1)S(1)}, u32[]{:S(2)}, u32[]{:S(2)}) collective-permute-start(bf16[4,16,8,128]{3,2,1,0:T(8,128)(2,1)S(1)} %get-tuple-element.21), channel_id=1, source_target_pairs={{4,8},{12,16},{20,24},{28,32},{36,40},{44,48},{52,56},{8,4},{16,12... | collective-permute-start | bytes 393224 | tf_op jit(solution)/shard_map/ppermute | solution.py:341
  14.3 1.2 %collective-permute-done.3 = bf16[14,16,128]{2,1,0:T(8,128)(2,1)S(1)} collective-permute-done((bf16[14,16,128]{2,1,0:T(8,128)(2,1)S(1)}, bf16[14,16,128]{2,1,0:T(8,128)(2,1)S(1)}, u32[]{:S(2)}, u32[]{:S(2)}) %collective-permute-start.3) | collective-permute-done | bytes 57376 | tf_op jit(solution)/shard_map/ppermute | solution.py:336
  15.5 2.0 %collective-permute-done.1.far = bf16[4,16,8,128]{3,2,1,0:T(8,128)(2,1)S(1)} collective-permute-done((bf16[4,16,8,128]{3,2,1,0:T(8,128)(2,1)S(1)}, bf16[4,16,8,128]{3,2,1,0:T(8,128)(2,1)S(1)}, u32[]{:S(2)}, u32[]{:S(2)}) %collective-permute-start.1) | collective-permute-done | bytes 131104 | tf_op jit(solution)/shard_map/ppermute | solution.py:341
  17.5 0.1 relay.1
  17.6 1.4 %collective-permute-start.4 = (bf16[59,16,128]{2,1,0:T(8,128)(2,1)S(1)}, bf16[59,16,128]{2,1,0:T(8,128)(2,1)S(1)}, u32[]{:S(2)}, u32[]{:S(2)}) collective-permute-start(bf16[59,16,128]{2,1,0:T(8,128)(2,1)S(1)} %get-tuple-element.26), channel_id=1, source_target_pairs={{0,1},{1,0},{2,3},{3,2},{4,5},{5,4},{6,7},{7,6},{8,9},{9,8},{10,11... | collective-permute-start | bytes 725000 | tf_op jit(solution)/shard_map/ppermute | solution.py:336
  19.0 1.9 %collective-permute-start.5 = (bf16[59,16,128]{2,1,0:T(8,128)(2,1)S(1)}, bf16[59,16,128]{2,1,0:T(8,128)(2,1)S(1)}, u32[]{:S(2)}, u32[]{:S(2)}) collective-permute-start(bf16[59,16,128]{2,1,0:T(8,128)(2,1)S(1)} %get-tuple-element.27), channel_id=1, source_target_pairs={{0,3},{1,2},{2,1},{3,0},{4,7},{5,6},{6,5},{7,4},{8,11},{9,10},{10,... | collective-permute-start | bytes 725000 | tf_op jit(solution)/shard_map/ppermute | solution.py:336
  20.9 1.2 %collective-permute-start.6 = (bf16[41,16,128]{2,1,0:T(8,128)(2,1)S(1)}, bf16[41,16,128]{2,1,0:T(8,128)(2,1)S(1)}, u32[]{:S(2)}, u32[]{:S(2)}) collective-permute-start(bf16[41,16,128]{2,1,0:T(8,128)(2,1)S(1)} %constant_dynamic-update-slice_fusion.stack.rest_0_), channel_id=1, source_target_pairs={{0,8},{8,0},{16,24},{24,16},{1,9},{9,1},{17,25},{25,17},{2,10},{10... | collective-permute-start | bytes 503816 | tf_op jit(solution)/shard_map/ppermute | solution.py:336
  22.1 1.9 %collective-permute-done.4.even.rest_1_ = bf16[59,16,128]{2,1,0:T(8,128)(2,1)S(1)} collective-permute-done((bf16[59,16,128]{2,1,0:T(8,128)(2,1)S(1)}, bf16[59,16,128]{2,1,0:T(8,128)(2,1)S(1)}, u32[]{:S(2)}, u32[]{:S(2)}) %collective-permute-start.4) | collective-permute-done | bytes 241696 | tf_op jit(solution)/shard_map/ppermute | solution.py:336
  24.0 2.5 %collective-permute-done.5.odd.rest_2_ = bf16[59,16,128]{2,1,0:T(8,128)(2,1)S(1)} collective-permute-done((bf16[59,16,128]{2,1,0:T(8,128)(2,1)S(1)}, bf16[59,16,128]{2,1,0:T(8,128)(2,1)S(1)}, u32[]{:S(2)}, u32[]{:S(2)}) %collective-permute-start.5) | collective-permute-done | bytes 241696 | tf_op jit(solution)/shard_map/ppermute | solution.py:336
  26.5 0.5 collective-permute-start.7
  27.1 0.5 collective-permute-start.10
  27.6 0.4 prepare.1
  28.0 0.3 collective-permute-done.7.rest_4_
  28.3 0.3 collective-permute-done.10.rest_7_
  28.6 7.4 %unet_step.1 = (bf16[4,16,8,128]{3,2,1,0:T(8,128)(2,1)}, bf16[4,896,128]{2,1,0:T(8,128)(2,1)S(1)}, f32[4,896,128]{2,1,0:T(8,128)S(1)}) custom-call(bf16[1760,384]{1,0:T(8,128)(2,1)S(1)} %get-tuple-element.28.field, f32[6,18,8,128]{3,2,1,0:T(8,128)S(1)} %get-tuple-element.29.upstream, f32[1728,128]{1,0:T(8,128)S(1)} %copy-done, ...), custom_call_target="tpu_custom_call" | custom-call | flops 3500000000 | bytes 8000000 | tf_op jit(solution)/shard_map/unet_step/pallas_call | solution.py:262
  36.0 0.4 collective-permute-start.11
  36.4 2.1 %collective-permute-done.11 = bf16[4,896,128]{2,1,0:T(8,128)(2,1)S(1)} collective-permute-done((bf16[4,896,128]{2,1,0:T(8,128)(2,1)S(1)}, bf16[4,896,128]{2,1,0:T(8,128)(2,1)S(1)}, u32[]{:S(2)}, u32[]{:S(2)}) %collective-permute-start.11) | collective-permute-done | bytes 917536 | tf_op jit(solution)/shard_map/ppermute | solution.py:336
  38.6 0.2 add_convert_fusion
  38.8 0.1 copy.10
  38.9 0.0 copy-start.1
  38.9 0.0 copy-start.2
  38.9 22.1 %all_to_all.15 = bf16[16,224,128]{2,1,0:T(8,128)(2,1)} all-to-all(bf16[16,224,128]{2,1,0:T(8,128)(2,1)S(1)} %bitcast.19), channel_id=1, replica_groups=mesh['dp'=4,'zl'=2,'x'=4,'c'=2,'gy'=4] {'x','gy'}, dimensions={0} | all-to-all | bytes 1835008 | tf_op jit(solution)/shard_map/all_to_all | solution.py:370
  61.0 1.3 %reduce_sum.24 = bf16[224,128]{1,0:T(8,128)(2,1)S(1)} reduce(bf16[16,224,128]{2,1,0:T(8,128)(2,1)} %all_to_all.15, bf16[]{:T(256)} %constant.3.clone.1), dimensions={0}, to_apply=%region_0.0 | reduce | flops 430080 | bytes 974850 | tf_op jit(solution)/shard_map/reduce_sum | solution.py:371
  62.3 12.4 %all_to_all.16 = bf16[8,56,128]{2,1,0:T(8,128)(2,1)S(1)} all-to-all(bf16[8,56,128]{2,1,0:T(8,128)(2,1)S(1)} %bitcast.20), channel_id=1, replica_groups=mesh['dp'=4,'zl'=2,'x'=4,'c'=2,'gy'=4] {'dp','zl'}, dimensions={0} | all-to-all | bytes 229376 | tf_op jit(solution)/shard_map/all_to_all | solution.py:373
  74.7 10.8 %all_to_all.17 = bf16[16,56,128]{2,1,0:T(8,128)(2,1)S(1)} all-to-all(bf16[16,56,128]{2,1,0:T(8,128)(2,1)S(1)} %broadcast_in_dim.16), channel_id=1, replica_groups=mesh['dp'=4,'zl'=2,'x'=4,'c'=2,'gy'=4] {'x','gy'}, dimensions={0} | all-to-all | bytes 458752 | tf_op jit(solution)/shard_map/all_to_all | solution.py:375
  85.5 4.1 %collective-permute-start.12 = (bf16[896,128]{1,0:T(8,128)(2,1)S(1)}, bf16[896,128]{1,0:T(8,128)(2,1)S(1)}, u32[]{:S(2)}, u32[]{:S(2)}) collective-permute-start(bf16[896,128]{1,0:T(8,128)(2,1)S(1)} %bitcast.12), channel_id=1, source_target_pairs={{0,4},{4,0},{1,5},{5,1},{2,6},{6,2},{3,7},{7,3},{8,12},{12,8},{9,1... | collective-permute-start | bytes 688136 | tf_op jit(solution)/shard_map/ppermute | solution.py:336
  89.6 1.1 %collective-permute-done.12.other = bf16[896,128]{1,0:T(8,128)(2,1)S(1)} collective-permute-done((bf16[896,128]{1,0:T(8,128)(2,1)S(1)}, bf16[896,128]{1,0:T(8,128)(2,1)S(1)}, u32[]{:S(2)}, u32[]{:S(2)}) %collective-permute-start.12) | collective-permute-done | bytes 229408 | tf_op jit(solution)/shard_map/ppermute | solution.py:336
  90.7 2.2 %adam_step.1 = (f32[1728,128]{1,0:T(8,128)}, f32[1728,128]{1,0:T(8,128)}, f32[1728,128]{1,0:T(8,128)}) custom-call(bf16[896,128]{1,0:T(8,128)(2,1)S(1)} %bitcast.13, bf16[896,128]{1,0:T(8,128)(2,1)S(1)} %collective-permute-done.12.other, f32[1728,128]{1,0:T(8,128)S(1)} %copy-done, f32[1728,128]{1,0:T(8,128)S(1)} %copy-done.1, f32[1728,128]{1,0:T(8,128)S(1)} %copy-done.2), custom_call_target="tpu_custom_call" | custom-call | tf_op jit(solution)/shard_map/adam_step/pallas_call | solution.py:317
  (20 shorter events, 0.1 us)
Async XLA Ops:
  0.6 28.0 %copy-start = (f32[1728,128]{1,0:T(8,128)S(1)}, f32[1728,128]{1,0:T(8,128)}, u32[]{:S(2)}) copy-start(f32[1728,128]{1,0:T(8,128)} %master.3) | copy-start | bytes 2654212
  0.6 26.9 %copy-start.4 = (bf16[1,4,16,8,128]{4,3,2,1,0:T(8,128)(2,1)S(1)}, bf16[1,4,16,8,128]{4,3,2,1,0:T(8,128)(2,1)}, u32[]{:S(2)}) copy-start(bf16[1,4,16,8,128]{4,3,2,1,0:T(8,128)(2,1)} %param.6) | copy-start | bytes 393220
  0.7 26.9 %copy-start.3 = (bf16[1,4,16,8,128]{4,3,2,1,0:T(8,128)(2,1)S(1)}, bf16[1,4,16,8,128]{4,3,2,1,0:T(8,128)(2,1)}, u32[]{:S(2)}) copy-start(bf16[1,4,16,8,128]{4,3,2,1,0:T(8,128)(2,1)} %param.5) | copy-start | bytes 393220
  1.9 12.4 %collective-permute-start.2 = (bf16[27,16,128]{2,1,0:T(8,128)(2,1)S(1)}, bf16[27,16,128]{2,1,0:T(8,128)(2,1)S(1)}, u32[]{:S(2)}, u32[]{:S(2)}) collective-permute-start(bf16[27,16,128]{2,1,0:T(8,128)(2,1)S(1)} %get-tuple-element.22), channel_id=1, source_target_pairs={{0,64},{4,132},{64,0},{68,196},{128,192},{132,4},{192,128},{196,68... | collective-permute-start | bytes 331784 | tf_op jit(solution)/shard_map/ppermute | solution.py:345
  9.7 5.8 %collective-permute-start.3 = (bf16[14,16,128]{2,1,0:T(8,128)(2,1)S(1)}, bf16[14,16,128]{2,1,0:T(8,128)(2,1)S(1)}, u32[]{:S(2)}, u32[]{:S(2)}) collective-permute-start(bf16[14,16,128]{2,1,0:T(8,128)(2,1)S(1)} %get-tuple-element.23), channel_id=1, source_target_pairs={{0,192},{64,128},{128,64},{192,0},{1,193},{65,129},{129,65},{193,1... | collective-permute-start | bytes 172040 | tf_op jit(solution)/shard_map/ppermute | solution.py:336
  9.7 5.8 %collective-permute-start = (bf16[4,16,8,128]{3,2,1,0:T(8,128)(2,1)S(1)}, bf16[4,16,8,128]{3,2,1,0:T(8,128)(2,1)S(1)}, u32[]{:S(2)}, u32[]{:S(2)}) collective-permute-start(bf16[4,16,8,128]{3,2,1,0:T(8,128)(2,1)S(1)} %get-tuple-element.20), channel_id=1, source_target_pairs={{0,4},{4,0},{1,5},{5,1},{2,6},{6,2},{3,7},{7,3},{8,12},{12,8},{9,1... | collective-permute-start | bytes 393224 | tf_op jit(solution)/shard_map/ppermute | solution.py:336
  11.3 6.3 %collective-permute-start.1 = (bf16[4,16,8,128]{3,2,1,0:T(8,128)(2,1)S(1)}, bf16[4,16,8,128]{3,2,1,0:T(8,128)(2,1)S(1)}, u32[]{:S(2)}, u32[]{:S(2)}) collective-permute-start(bf16[4,16,8,128]{3,2,1,0:T(8,128)(2,1)S(1)} %get-tuple-element.21), channel_id=1, source_target_pairs={{4,8},{12,16},{20,24},{28,32},{36,40},{44,48},{52,56},{8,4},{16,12... | collective-permute-start | bytes 393224 | tf_op jit(solution)/shard_map/ppermute | solution.py:341
  17.6 6.4 %collective-permute-start.4 = (bf16[59,16,128]{2,1,0:T(8,128)(2,1)S(1)}, bf16[59,16,128]{2,1,0:T(8,128)(2,1)S(1)}, u32[]{:S(2)}, u32[]{:S(2)}) collective-permute-start(bf16[59,16,128]{2,1,0:T(8,128)(2,1)S(1)} %get-tuple-element.26), channel_id=1, source_target_pairs={{0,1},{1,0},{2,3},{3,2},{4,5},{5,4},{6,7},{7,6},{8,9},{9,8},{10,11... | collective-permute-start | bytes 725000 | tf_op jit(solution)/shard_map/ppermute | solution.py:336
  19.0 7.6 %collective-permute-start.5 = (bf16[59,16,128]{2,1,0:T(8,128)(2,1)S(1)}, bf16[59,16,128]{2,1,0:T(8,128)(2,1)S(1)}, u32[]{:S(2)}, u32[]{:S(2)}) collective-permute-start(bf16[59,16,128]{2,1,0:T(8,128)(2,1)S(1)} %get-tuple-element.27), channel_id=1, source_target_pairs={{0,3},{1,2},{2,1},{3,0},{4,7},{5,6},{6,5},{7,4},{8,11},{9,10},{10,... | collective-permute-start | bytes 725000 | tf_op jit(solution)/shard_map/ppermute | solution.py:336
  20.9 6.2 %collective-permute-start.6 = (bf16[41,16,128]{2,1,0:T(8,128)(2,1)S(1)}, bf16[41,16,128]{2,1,0:T(8,128)(2,1)S(1)}, u32[]{:S(2)}, u32[]{:S(2)}) collective-permute-start(bf16[41,16,128]{2,1,0:T(8,128)(2,1)S(1)} %constant_dynamic-update-slice_fusion.stack.rest_0_), channel_id=1, source_target_pairs={{0,8},{8,0},{16,24},{24,16},{1,9},{9,1},{17,25},{25,17},{2,10},{10... | collective-permute-start | bytes 503816 | tf_op jit(solution)/shard_map/ppermute | solution.py:336
  24.0 4.6 %collective-permute-start.8 = (bf16[59,16,128]{2,1,0:T(8,128)(2,1)S(1)}, bf16[59,16,128]{2,1,0:T(8,128)(2,1)S(1)}, u32[]{:S(2)}, u32[]{:S(2)}) collective-permute-start(bf16[59,16,128]{2,1,0:T(8,128)(2,1)S(1)} %collective-permute-done.4.even.rest_1_), channel_id=1, source_target_pairs={{0,4},{4,0},{1,5},{5,1},{2,6},{6,2},{3,7},{7,3},{8,12},{12,8},{9,1... | collective-permute-start | bytes 725000 | tf_op jit(solution)/shard_map/ppermute | solution.py:336
  26.5 2.1 %collective-permute-start.9 = (bf16[59,16,128]{2,1,0:T(8,128)(2,1)S(1)}, bf16[59,16,128]{2,1,0:T(8,128)(2,1)S(1)}, u32[]{:S(2)}, u32[]{:S(2)}) collective-permute-start(bf16[59,16,128]{2,1,0:T(8,128)(2,1)S(1)} %collective-permute-done.5.odd.rest_2_), channel_id=1, source_target_pairs={{0,4},{4,0},{1,5},{5,1},{2,6},{6,2},{3,7},{7,3},{8,12},{12,8},{9,1... | collective-permute-start | bytes 725000 | tf_op jit(solution)/shard_map/ppermute | solution.py:336
  26.5 1.7 %collective-permute-start.7 = (bf16[41,16,128]{2,1,0:T(8,128)(2,1)S(1)}, bf16[41,16,128]{2,1,0:T(8,128)(2,1)S(1)}, u32[]{:S(2)}, u32[]{:S(2)}) collective-permute-start(bf16[41,16,128]{2,1,0:T(8,128)(2,1)S(1)} %constant_dynamic-update-slice_fusion.stack.rest_0_), channel_id=1, source_target_pairs={{0,4},{4,0},{1,5},{5,1},{2,6},{6,2},{3,7},{7,3},{8,12},{12,8},{9,1... | collective-permute-start | bytes 503816 | tf_op jit(solution)/shard_map/ppermute | solution.py:336
  27.1 1.6 %collective-permute-start.10 = (bf16[41,16,128]{2,1,0:T(8,128)(2,1)S(1)}, bf16[41,16,128]{2,1,0:T(8,128)(2,1)S(1)}, u32[]{:S(2)}, u32[]{:S(2)}) collective-permute-start(bf16[41,16,128]{2,1,0:T(8,128)(2,1)S(1)} %collective-permute-done.6.rest_3_), channel_id=1, source_target_pairs={{0,4},{4,0},{1,5},{5,1},{2,6},{6,2},{3,7},{7,3},{8,12},{12,8},{9,1... | collective-permute-start | bytes 503816 | tf_op jit(solution)/shard_map/ppermute | solution.py:336
  36.0 2.6 %collective-permute-start.11 = (bf16[4,896,128]{2,1,0:T(8,128)(2,1)S(1)}, bf16[4,896,128]{2,1,0:T(8,128)(2,1)S(1)}, u32[]{:S(2)}, u32[]{:S(2)}) collective-permute-start(bf16[4,896,128]{2,1,0:T(8,128)(2,1)S(1)} %get-tuple-element.32), channel_id=1, source_target_pairs={{0,4},{4,0},{1,5},{5,1},{2,6},{6,2},{3,7},{7,3},{8,12},{12,8},{9,1... | collective-permute-start | bytes 2752520 | tf_op jit(solution)/shard_map/ppermute | solution.py:336
  38.9 51.9 %copy-start.1 = (f32[1728,128]{1,0:T(8,128)S(1)}, f32[1728,128]{1,0:T(8,128)}, u32[]{:S(2)}) copy-start(f32[1728,128]{1,0:T(8,128)} %one.1) | copy-start | bytes 2654212
  38.9 51.8 %copy-start.2 = (f32[1728,128]{1,0:T(8,128)S(1)}, f32[1728,128]{1,0:T(8,128)}, u32[]{:S(2)}) copy-start(f32[1728,128]{1,0:T(8,128)} %two.1) | copy-start | bytes 2654212
  85.5 5.2 %collective-permute-start.12 = (bf16[896,128]{1,0:T(8,128)(2,1)S(1)}, bf16[896,128]{1,0:T(8,128)(2,1)S(1)}, u32[]{:S(2)}, u32[]{:S(2)}) collective-permute-start(bf16[896,128]{1,0:T(8,128)(2,1)S(1)} %bitcast.12), channel_id=1, source_target_pairs={{0,4},{4,0},{1,5},{5,1},{2,6},{6,2},{3,7},{7,3},{8,12},{12,8},{9,1... | collective-permute-start | bytes 688136 | tf_op jit(solution)/shard_map/ppermute | solution.py:336

commit v3 on v2

--- a/solution.py
+++ b/solution.py
@@ -1,3 +1,5 @@
+import functools
+
 import jax
 import jax.numpy as jnp
 from jax import lax
@@ -86,26 +88,25 @@
         lefts.append(jnp.transpose(padded).astype(BF))
     left = jnp.concatenate(lefts, axis=0)
     step = wide * SZ
-    for a in range(3):
-        start = (first_plane + a) * step
-        prod = jnp.dot(left, ref[start : start + SX * step, :], preferred_element_type=F32)
-        for b in range(3):
-            for c in range(3):
-                grads[layer * 27 + 9 * a + 3 * b + c] = prod[b * C : (b + 1) * C, c * C : (c + 1) * C]
-
-
-def payload_kernel(vol, cot, master, whole, half, near, far, first, last, rows, sems):
+    starts = [(first_plane + a) * step for a in range(3)]
+    right = jnp.concatenate([ref[start : start + SX * step, :] for start in starts], axis=1)
+    prod = jnp.dot(left, right, preferred_element_type=F32)
+    for tap in range(27):
+        a, b, c = tap // 9, tap // 3 % 3, tap % 3
+        column = (3 * a + c) * C
+        grads[layer * 27 + tap] = prod[b * C : (b + 1) * C, column : column + C]
+
+
+def payload_kernel(vol, cot, master, whole, half, near, far, vol_out, cot_out, rows, sems):
     gx, gy, core, dp, quarter = position()
     moves = [
         (master.at[:, pl.ds(pl.multiple_of(16 * quarter, 16), 16), :], rows),
+        (vol.at[pl.ds(core, 3)], far.at[0:3]),
+        (cot.at[pl.ds(3 * core, 1)], far.at[3:4]),
         (vol.at[pl.ds(1 - core, 3)], near.at[0:3]),
-        (vol.at[pl.ds(core, 3)], far.at[0:3]),
         (cot.at[pl.ds(3 * (1 - core), 1)], near.at[3:4]),
-        (cot.at[pl.ds(3 * core, 1)], far.at[3:4]),
-        (vol.at[:, 0:3], first.at[:, 0:3]),
-        (cot.at[:, 0:1], first.at[:, 3:4]),
-        (vol.at[:, SY - 3 : SY], last.at[:, 0:3]),
-        (cot.at[:, SY - 1 : SY], last.at[:, 3:4]),
+        (vol, vol_out),
+        (cot, cot_out),
     ]
     copies = [pltpu.make_async_copy(src, dst, sems.at[i]) for i, (src, dst) in enumerate(moves)]
     for copy in copies:
@@ -120,85 +121,74 @@
 def payloads(vol, cot, master):
     vmem = pl.BlockSpec(memory_space=pltpu.VMEM)
     hbm = pl.BlockSpec(memory_space=pltpu.HBM)
-    side = pltpu.VMEM((4, SY, SZ, C), BF)
-    edge = pltpu.VMEM((4, 4, SZ, C), BF)
+    cells = pltpu.VMEM((4, SY, SZ, C), BF)
     return pl.pallas_call(
         payload_kernel,
-        out_shape=(
-            pltpu.VMEM((27, 16, C), BF),
-            pltpu.VMEM((14, 16, C), BF),
-            side,
-            side,
-            edge,
-            edge,
-        ),
+        out_shape=(pltpu.VMEM((27, 16, C), BF), pltpu.VMEM((14, 16, C), BF)) + (cells,) * 4,
         in_specs=[hbm] * 3,
         out_specs=(vmem,) * 6,
-        scratch_shapes=[pltpu.VMEM((27, 16, C), F32), pltpu.SemaphoreType.DMA((9,))],
+        scratch_shapes=[pltpu.VMEM((27, 16, C), F32), pltpu.SemaphoreType.DMA((7,))],
         compiler_params=pltpu.CompilerParams(vmem_limit_bytes=8 * 2**20),
         name="payloads",
     )(*(pltpu.with_memory_space_constraint(a, pltpu.HBM) for a in (vol, cot, master.reshape(27, 64, C))))
 
 
-SIDE = 36 * SZ // 16
-
-
-def relay_kernel(stack, near, far, first, last, even, odd):
+SIDE = 26 * SZ // 16
+
+
+def relay_kernel(stack, vol, cot, far, even, odd):
     gx, gy, core, dp, quarter = position()
     parity = lax.rem(gy, 2)
-    even[0:41] = stack[...]
-    odd[0:41] = stack[...]
     for out, upper in ((even, 1 - parity), (odd, parity)):
-        own = jnp.where(upper == 0, first[...].astype(F32), last[...].astype(F32)).astype(BF)
-        groups = []
-        for part, planes in ((near, 3), (own, 4), (far, 3)):
-            rows = part[:, 0:3] if planes == 4 else part[0:3, pl.ds(upper * (SY - 3), 3)]
-            groups.append(rows.reshape(-1, SZ, C))
-        for part, planes in ((near, 1), (own, 4), (far, 1)):
-            rows = part[:, 3:4] if planes == 4 else part[3:4, pl.ds(upper * (SY - 1), 1)]
-            groups.append(rows.reshape(-1, SZ, C))
-        out[41 : 41 + SIDE] = jnp.concatenate(groups).reshape(SIDE, 16, C)
-
-
-def relay(stack, near, far, first, last):
+        three, one = pl.ds(upper * (SY - 3), 3), pl.ds(upper * (SY - 1), 1)
+        groups = [vol[:, three], far[0:3, three], cot[:, one], far[3:4, one]]
+        out[0:41] = stack[...]
+        out[41 : 41 + SIDE] = jnp.concatenate([g.reshape(-1, SZ, C) for g in groups]).reshape(SIDE, 16, C)
+
+
+def relay(stack, vol, cot, far):
     vmem = pl.BlockSpec(memory_space=pltpu.VMEM)
     both = jax.ShapeDtypeStruct((41 + SIDE, 16, C), BF)
     return pl.pallas_call(
         relay_kernel,
         out_shape=(both, both),
-        in_specs=[vmem] * 5,
+        in_specs=[vmem] * 4,
         out_specs=(vmem,) * 2,
         compiler_params=pltpu.CompilerParams(vmem_limit_bytes=8 * 2**20),
         name="relay",
-    )(stack, near, far, first, last)
-
-
-def prepare_kernel(vol, cot, near, far, even, odd, field, upstream):
+    )(stack, vol, cot, far)
+
+
+def prepare_kernel(vol, cot, near, far, even, odd, mate_even, mate_odd, field, upstream):
     gx, gy, core, dp, quarter = position()
     parity = lax.rem(gy, 2)
 
     def ordered(first, second, swap):
         return jnp.where(swap == 0, first, second), jnp.where(swap == 0, second, first)
 
+    def side_of(ref):
+        return ref[41 : 41 + SIDE].reshape(26, SZ, C).astype(F32)
+
     left, right = ordered(far[...].astype(F32), near[...].astype(F32), core)
-    even_side = even[41 : 41 + SIDE].reshape(36, SZ, C).astype(F32)
-    odd_side = odd[41 : 41 + SIDE].reshape(36, SZ, C).astype(F32)
-    low, high = ordered(odd_side, even_side, parity)
-    low = jnp.where(gy == 0, 0.0, low)
-    high = jnp.where(gy == 3, 0.0, high)
     sides = []
-    for side in (low, high):
-        lower, upper = ordered(side[21:30], side[0:9], core)
-        sides.append(jnp.concatenate([lower, side[9:21], upper]).reshape(10, 3, SZ, C))
-        lower, upper = ordered(side[35:36], side[30:31], core)
-        sides.append(jnp.concatenate([lower, side[31:35], upper]).reshape(6, 1, SZ, C))
+    lower, upper = ordered(side_of(odd), side_of(even), parity)
+    mate_lower, mate_upper = ordered(side_of(mate_odd), side_of(mate_even), parity)
+    for side, mate, outside in ((lower, mate_lower, gy == 0), (upper, mate_upper, gy == 3)):
+        mate_planes = jnp.where(core == 0, mate[0:9], mate[3:12])
+        mate_plane = jnp.where(core == 0, mate[21:22], mate[24:25])
+        first, last = ordered(side[12:21], mate_planes, core)
+        planes = jnp.concatenate([first, side[0:12], last]).reshape(10, 3, SZ, C)
+        sides.append(jnp.where(outside, 0.0, planes))
+        first, last = ordered(side[25:26], mate_plane, core)
+        planes = jnp.concatenate([first, side[21:25], last]).reshape(6, 1, SZ, C)
+        sides.append(jnp.where(outside, 0.0, planes))
     own = jnp.concatenate([left[0:3], vol[...].astype(F32), right[0:3]], axis=0)
     store_triple(field, slice(0, 1760), jnp.concatenate([sides[0], own, sides[2]], axis=1))
     own = jnp.concatenate([left[3:4], cot[...].astype(F32), right[3:4]], axis=0)
     upstream[...] = jnp.concatenate([sides[1], own, sides[3]], axis=1)
 
 
-def prepare(vol, cot, near, far, even, odd):
+def prepare(vol, cot, near, far, even, odd, mate_even, mate_odd):
     vmem = pl.BlockSpec(memory_space=pltpu.VMEM)
     return pl.pallas_call(
         prepare_kernel,
@@ -206,12 +196,12 @@
             jax.ShapeDtypeStruct((10 * 176, 3 * C), BF),
             jax.ShapeDtypeStruct((6, 18, SZ, C), F32),
         ),
-        in_specs=[vmem] * 6,
+        in_specs=[vmem] * 8,
         out_specs=(vmem, vmem),
         compiler_params=pltpu.CompilerParams(vmem_limit_bytes=16 * 2**20),
         cost_estimate=pl.CostEstimate(flops=4_000_000, bytes_accessed=3_000_000, transcendentals=0),
         name="prepare",
-    )(vol, cot, near, far, even, odd)
+    )(vol, cot, near, far, even, odd, mate_even, mate_odd)
 
 
 def step_kernel(field, upstream, master, *rest):
@@ -224,9 +214,9 @@
     for index, piece in enumerate(pieces):
         owner_core = core if index < 4 else 1 - core
         rows = pl.ds(pl.multiple_of((quarter ^ (0, 1, 3, 2)[index % 4]) * 16, 16), 16)
-        whole = dp ^ (1 + owner_core)
+        whole = dp ^ (1 + 2 * owner_core)
         taps[pl.ds(whole * 27, 27), rows, :] = piece[0:27]
-        taps[pl.ds((dp ^ 3) * 27 + 13 * owner_core, 14), rows, :] = piece[27:41]
+        taps[pl.ds((dp ^ 2) * 27 + 13 * owner_core, 14), rows, :] = piece[27:41]
     tap_rows = taps[...].reshape(54 * C, C)
 
     first = conv_rows(field, 8, 22, layer_weights(tap_rows, 0))
@@ -281,52 +271,84 @@
     )(field, upstream, master, *pieces)
 
 
-ADAM_ROWS = 576
-
-
-def adam_kernel(mine, other, master, one, two, new_master, new_one, new_two, grad, parts, sems):
-    gx, gy, core, dp, quarter = position()
-    odd = lax.rem(dp, 2)
-    for source, owner in ((mine, core), (other, 1 - core)):
-        for tap in range(TAPS // 2):
-            block = source[tap * C : (tap + 1) * C].astype(F32)
-            grad[pl.ds(pl.multiple_of((owner * (TAPS // 2) + tap) * C, C), C), :] = jnp.transpose(block)
+def plane_kernel(parts, out):
+    for shard in range(4):
+        total = parts[0, shard].astype(F32)
+        for sender in range(1, 16):
+            total = total + parts[sender, shard].astype(F32)
+        out[2 * shard] = total.astype(BF)
+        out[2 * shard + 1] = total.astype(BF)
+
+
+def plane_sum(parts):
+    vmem = pl.BlockSpec(memory_space=pltpu.VMEM)
+    return pl.pallas_call(
+        plane_kernel,
+        out_shape=jax.ShapeDtypeStruct((8, PIECE, C), BF),
+        in_specs=[vmem],
+        out_specs=vmem,
+        compiler_params=pltpu.CompilerParams(vmem_limit_bytes=8 * 2**20),
+        name="plane_sum",
+    )(parts)
+
+
+OWN_ROWS = HALF - C // 2
+CHUNKS = 4
+
+
+def adam_kernel(own_step, rows_now, *refs):
+    sources, (master, one, two) = refs[: 1 if own_step else 2], refs[1 if own_step else 2 :][:3]
+    new_master, new_one, new_two, grad, parts, sems = refs[-6:]
+    core, odd = lax.axis_index("c"), lax.rem(lax.axis_index("dp"), 2)
+    half = TAPS // 2
+    owned = ((sources[0], core, range(half)),)
+    if not own_step:
+        owned = ((sources[1], 1 - core, range(half)), (sources[0], core, (half - 1, 0)))
+    for source, owner, taps in owned:
+        for tap in taps:
+            block = jnp.transpose(source[tap * C : (tap + 1) * C].astype(F32))
+            grad[pl.ds(pl.multiple_of((owner * half + tap) * C, C), C), :] = block
+    begin = core * HALF if own_step else (1 - core) * OWN_ROWS
+    size = rows_now // CHUNKS
     copies = []
-    for chunk in range(master.shape[0] // ADAM_ROWS):
-        rows = pl.ds(chunk * ADAM_ROWS, ADAM_ROWS)
-        shifted_rows = pl.ds(pl.multiple_of(odd * (C // 2) + chunk * ADAM_ROWS, C // 2), ADAM_ROWS)
-        gradient = grad[shifted_rows, :]
+    for chunk in range(CHUNKS):
+        start = pl.multiple_of(begin + chunk * size, 16)
+        rows, held = pl.ds(start, size), pl.ds(chunk * size, size)
+        gradient = grad[pl.ds(pl.multiple_of(start + odd * (C // 2), 16), size), :]
         first = beta_one * one[rows, :] + (1.0 - beta_one) * gradient
         second = beta_two * two[rows, :] + (1.0 - beta_two) * gradient * gradient
         update = first / (1.0 - beta_one**10) / (jnp.sqrt(second / (1.0 - beta_two**10)) + epsilon)
-        parts[0, rows, :] = master[rows, :] - learn_rate * update
-        parts[1, rows, :] = first
-        parts[2, rows, :] = second
+        parts[0, held, :] = master[rows, :] - learn_rate * update
+        parts[1, held, :] = first
+        parts[2, held, :] = second
         for index, out in enumerate((new_master, new_one, new_two)):
-            copy = pltpu.make_async_copy(parts.at[index, rows], out.at[rows], sems.at[chunk, index])
+            copy = pltpu.make_async_copy(parts.at[index, held], out.at[rows], sems.at[chunk, index])
             copy.start()
             copies.append(copy)
     for copy in copies:
         copy.wait()
 
 
-def adam_update(mine, other, master, one, two):
+def adam_step(own_step, sources, state, held=()):
+    rows_now = OWN_ROWS if own_step else state[0].shape[0] - OWN_ROWS
     vmem = pl.BlockSpec(memory_space=pltpu.VMEM)
     hbm = pl.BlockSpec(memory_space=pl.ANY)
-    shape = jax.ShapeDtypeStruct(master.shape, F32)
-    return pl.pallas_call(
-        adam_kernel,
-        out_shape=(shape, shape, shape),
-        in_specs=[vmem] * 5,
-        out_specs=(hbm, hbm, hbm),
+    inputs = len(sources) + len(state)
+    return pl.pallas_call(
+        functools.partial(adam_kernel, own_step, rows_now),
+        out_shape=(jax.ShapeDtypeStruct(state[0].shape, F32),) * 3,
+        in_specs=[vmem] * inputs + [hbm] * len(held),
+        out_specs=(hbm,) * 3,
+        input_output_aliases={inputs + i: i for i in range(len(held))},
         scratch_shapes=[
             pltpu.VMEM((TAPS * C, C), F32),
-            pltpu.VMEM((3,) + master.shape, F32),
-            pltpu.SemaphoreType.DMA((master.shape[0] // ADAM_ROWS, 3)),
+            pltpu.VMEM((3, rows_now, C), F32),
+            pltpu.SemaphoreType.DMA((CHUNKS, 3)),
         ],
-        compiler_params=pltpu.CompilerParams(vmem_limit_bytes=24 * 2**20),
-        name="adam_step",
-    )(mine, other, master, one, two)
+        compiler_params=pltpu.CompilerParams(vmem_limit_bytes=16 * 2**20),
+        cost_estimate=pl.CostEstimate(flops=3_000_000, bytes_accessed=4_000_000, transcendentals=200_000),
+        name="adam_own" if own_step else "adam_rest",
+    )(*sources, *state, *held)
 
 
 GX = ("zl", "x", "c")
@@ -343,38 +365,40 @@
 
 def over_dp(whole, half):
     whole = lax.ppermute(
-        whole, ("dp", "c"), [(2 * d + c, 2 * (d ^ (1 + c)) + c) for d in range(4) for c in range(2)]
+        whole, ("dp", "c"), [(2 * d + c, 2 * (d ^ (1 + 2 * c)) + c) for d in range(4) for c in range(2)]
     )
-    return whole, exchanged(half, "dp", 4, 3)
+    return whole, exchanged(half, "dp", 4, 2)
 
 
 def per_device(volume, cotangent, master, moment_one, moment_two):
     vol, cot = volume[0], cotangent[0]
-    whole, half, near, far, first, last = payloads(vol, cot, master)
+    whole, half, near, far, vol, cot = payloads(vol, cot, master)
     whole, half = over_dp(whole, half)
+    far = paired(far, GX, 16)
     near = exchanged(near, "c", 2, 1)
-    far = paired(far, GX, 16)
 
     stack = jnp.concatenate([whole, half])
     opposite = exchanged(stack, "x", 4, 1)
-    even, odd = relay(stack, near, far, first, last)
+    even, odd = relay(stack, vol, cot, far)
     odd = exchanged(odd, "gy", 4, 3)
     even = exchanged(even, "gy", 4, 1)
+    even, odd, near = lax.optimization_barrier((even, odd, near))
     mine = [stack, even, odd, opposite]
-    pieces = mine + [exchanged(part, "c", 2, 1) for part in mine]
-    field, upstream = prepare(vol, cot, near, far, even, odd)
+    mates = [exchanged(part, "c", 2, 1) for part in mine]
+    pieces = mine + mates
+    field, upstream = prepare(vol, cot, near, far, even, odd, mates[1], mates[2])
     act, send, keep = device_step(field, upstream, master, pieces)
 
     pair = (keep + exchanged(send, "c", 2, 1).astype(F32)).astype(BF)
     spread = pair.reshape(4, 16, PIECE, C).transpose(1, 0, 2, 3).reshape(16, 4 * PIECE, C)
     plane = lax.all_to_all(spread, ("x", "gy"), 0, 0)
-    plane = jnp.sum(plane.astype(F32), axis=0).astype(BF).reshape(4, PIECE, C)
-    twice = jnp.broadcast_to(plane[:, None], (4, 2, PIECE, C)).reshape(8, PIECE, C)
-    column = lax.all_to_all(twice, ("dp", "zl"), 0, 0)
+    column = lax.all_to_all(plane_sum(plane.reshape(16, 4, PIECE, C)), ("dp", "zl"), 0, 0)
     column = jnp.sum(column.astype(F32), axis=0).astype(BF)
     mine = lax.all_to_all(jnp.broadcast_to(column, (16, PIECE, C)), ("x", "gy"), 0, 0).reshape(HALF, C)
     other = exchanged(mine, "c", 2, 1)
-    new_master, new_one, new_two = adam_update(mine, other, master, moment_one, moment_two)
+    state = (master, moment_one, moment_two)
+    held = adam_step(True, (mine,), state)
+    new_master, new_one, new_two = adam_step(False, (mine, other), state, held)
     return (act[None], new_master, new_one, new_two)
 
 

time: 93.3 us -> 90.8 us (0.973)
  blocking collectives: 45.2 us -> 42.6 us
  starting transfers between devices: 22.5 us -> 25.1 us
  waiting for transfers between devices: 11.5 us -> 9.59 us
  other arithmetic: 1.55 us -> 0.2 us
    ppermute x1, starting transfers between devices: 3 us -> 5.32 us  [paired(): return lax.ppermute(cells, axis, pairs + [(j, i) for i, j in pairs])]
    all_to_all x1, blocking collectives: 22.1 us -> 20.6 us  [per_device(): plane = lax.all_to_all(spread, ('x', 'gy'), 0, 0)]
    reduce_sum x1 -> x0, other arithmetic: 1.31 us -> none  [per_device(): plane = jnp.sum(plane.astype(F32), axis=0).astype(BF).reshape(4, PIECE, C)]
    ppermute x11, starting transfers between devices: 11.6 us -> 12.8 us  [exchanged(): return lax.ppermute(cells, axis, [(i, i ^ by) for i in range(count)])]
    ppermute x1, waiting for transfers between devices: 2 us -> 1.02 us  [paired(): return lax.ppermute(cells, axis, pairs + [(j, i) for i, j in pairs])]
    ppermute x11, waiting for transfers between devices: 9.53 us -> 8.57 us  [exchanged(): return lax.ppermute(cells, axis, [(i, i ^ by) for i in range(count)])]
    pallas_call x2 -> x4, Pallas kernels: 2.24 us -> 3.07 us  [the longest x2 2.89 us: adam_step(): pl.pallas_call(functools.partial(adam_kernel, own_step, rows_now), out_sh...]
  transfers between devices with their start and end apart: 13 -> 13, of which waited for: 8 -> 8; matrix products, arithmetic and copies ran while one was open for 0% -> 0% of each run, Pallas kernels for 0% -> 2%
where the time goes in v3:
time: 90.8 us; the launch traced here: 90.6 us
  blocking collectives  42.6 us (47%)
  starting transfers between devices  25.1 us (28%)
  Pallas kernels  12.1 us (13%)
  waiting for transfers between devices  9.59 us (11%)
  between operations  0.92 us (1%)
    all_to_all x1, blocking collectives, per_device(): plane = lax.all_to_all(spread, ('x', 'gy'), 0, 0)  20.6 us
    ppermute x11, starting transfers between devices, exchanged(): return lax.ppermute(cells, axis, [(i, i ^ by) for i in range(count)])  12.8 us
    all_to_all x1, blocking collectives, per_device(): lax.all_to_all(plane_sum(plane.reshape(16, 4, PIECE, C)), ('dp', 'zl'), 0...  11.5 us
    all_to_all x1, blocking collectives, per_device(): lax.all_to_all(jnp.broadcast_to(column, (16, PIECE, C)), ('x', 'gy'), 0, 0)  10.5 us
    ppermute x11, waiting for transfers between devices, exchanged(): return lax.ppermute(cells, axis, [(i, i ^ by) for i in range(count)])  8.57 us
    pallas_call x1, Pallas kernels, device_step(): pl.pallas_call(step_kernel, out_shape=(jax.ShapeDtypeStruct((SX, SY, SZ,...  7.26 us
    ppermute x1, starting transfers between devices, over_dp(): lax.ppermute(whole, ('dp', 'c'), [(2 * d + c, 2 * (d ^ 1 + 2 * c) + c) fo...  6.94 us
    ppermute x1, starting transfers between devices, paired(): return lax.ppermute(cells, axis, pairs + [(j, i) for i, j in pairs])  5.32 us
  transfers between devices with their start and end apart: 13, of which 8 were waited for; matrix products, arithmetic and copies ran while one was open for 0% of the time, Pallas kernels for 2%

profile of v3, /device:TPU:1, one launch (start us, length us, event | category | flops | bytes accessed | tf_op | source)
XLA Modules:
  0.0 90.6 jit_solution(4181487219424806516)
XLA Ops:
  0.6 1.4 %payloads.1 = (bf16[27,16,128]{2,1,0:T(8,128)(2,1)S(1)}, bf16[14,16,128]{2,1,0:T(8,128)(2,1)S(1)}, bf16[4,16,8,128]{3,2,1,0:T(8,128)(2,1)S(1)}, bf16[4,16,8,128]...) custom-call(bf16[4,16,8,128]{3,2,1,0:T(8,128)(2,1)} %bitcast.17, ...), custom_call_target="tpu_custom_call" | custom-call | tf_op jit(solution)/shard_map/payloads/pallas_call | solution.py:125
  2.0 6.9 %collective-permute-start = (bf16[27,16,128]{2,1,0:T(8,128)(2,1)S(1)}, bf16[27,16,128]{2,1,0:T(8,128)(2,1)S(1)}, u32[]{:S(2)}, u32[]{:S(2)}) collective-permute-start(bf16[27,16,128]{2,1,0:T(8,128)(2,1)S(1)} %get-tuple-element.28), channel_id=1, source_target_pairs={{0,64},{4,196},{64,0},{68,132},{128,192},{132,68},{192,128},{196,4... | collective-permute-start | bytes 331784 | tf_op jit(solution)/shard_map/ppermute | solution.py:367
  8.9 1.0 %collective-permute-start.1 = (bf16[14,16,128]{2,1,0:T(8,128)(2,1)S(1)}, bf16[14,16,128]{2,1,0:T(8,128)(2,1)S(1)}, u32[]{:S(2)}, u32[]{:S(2)}) collective-permute-start(bf16[14,16,128]{2,1,0:T(8,128)(2,1)S(1)} %get-tuple-element.29), channel_id=1, source_target_pairs={{0,128},{64,192},{128,0},{192,64},{1,129},{65,193},{129,1},{193,65... | collective-permute-start | bytes 172040 | tf_op jit(solution)/shard_map/ppermute | solution.py:358
  9.9 5.3 %collective-permute-start.2 = (bf16[4,16,8,128]{3,2,1,0:T(8,128)(2,1)S(1)}, bf16[4,16,8,128]{3,2,1,0:T(8,128)(2,1)S(1)}, u32[]{:S(2)}, u32[]{:S(2)}) collective-permute-start(bf16[4,16,8,128]{3,2,1,0:T(8,128)(2,1)S(1)} %get-tuple-element.30), channel_id=1, source_target_pairs={{4,8},{12,16},{20,24},{28,32},{36,40},{44,48},{52,56},{8,4},{16,12... | collective-permute-start | bytes 393224 | tf_op jit(solution)/shard_map/ppermute | solution.py:363
  15.3 1.6 %collective-permute-done.1 = bf16[14,16,128]{2,1,0:T(8,128)(2,1)S(1)} collective-permute-done((bf16[14,16,128]{2,1,0:T(8,128)(2,1)S(1)}, bf16[14,16,128]{2,1,0:T(8,128)(2,1)S(1)}, u32[]{:S(2)}, u32[]{:S(2)}) %collective-permute-start.1) | collective-permute-done | bytes 57376 | tf_op jit(solution)/shard_map/ppermute | solution.py:358
  16.9 1.0 %collective-permute-done.2.far = bf16[4,16,8,128]{3,2,1,0:T(8,128)(2,1)S(1)} collective-permute-done((bf16[4,16,8,128]{3,2,1,0:T(8,128)(2,1)S(1)}, bf16[4,16,8,128]{3,2,1,0:T(8,128)(2,1)S(1)}, u32[]{:S(2)}, u32[]{:S(2)}) %collective-permute-start.2) | collective-permute-done | bytes 131104 | tf_op jit(solution)/shard_map/ppermute | solution.py:363
  17.9 0.1 relay.1
  18.0 1.4 %collective-permute-start.3 = (bf16[54,16,128]{2,1,0:T(8,128)(2,1)S(1)}, bf16[54,16,128]{2,1,0:T(8,128)(2,1)S(1)}, u32[]{:S(2)}, u32[]{:S(2)}) collective-permute-start(bf16[54,16,128]{2,1,0:T(8,128)(2,1)S(1)} %get-tuple-element.31), channel_id=1, source_target_pairs={{0,1},{1,0},{2,3},{3,2},{4,5},{5,4},{6,7},{7,6},{8,9},{9,8},{10,11... | collective-permute-start | bytes 663560 | tf_op jit(solution)/shard_map/ppermute | solution.py:358
  19.3 1.9 %collective-permute-start.4 = (bf16[54,16,128]{2,1,0:T(8,128)(2,1)S(1)}, bf16[54,16,128]{2,1,0:T(8,128)(2,1)S(1)}, u32[]{:S(2)}, u32[]{:S(2)}) collective-permute-start(bf16[54,16,128]{2,1,0:T(8,128)(2,1)S(1)} %get-tuple-element.32), channel_id=1, source_target_pairs={{0,3},{1,2},{2,1},{3,0},{4,7},{5,6},{6,5},{7,4},{8,11},{9,10},{10,... | collective-permute-start | bytes 663560 | tf_op jit(solution)/shard_map/ppermute | solution.py:358
  21.2 0.4 collective-permute-start.5
  21.7 2.0 %collective-permute-start.8 = (bf16[41,16,128]{2,1,0:T(8,128)(2,1)S(1)}, bf16[41,16,128]{2,1,0:T(8,128)(2,1)S(1)}, u32[]{:S(2)}, u32[]{:S(2)}) collective-permute-start(bf16[41,16,128]{2,1,0:T(8,128)(2,1)S(1)} %constant_dynamic-update-slice_fusion.stack.rest_0_), channel_id=1, source_target_pairs={{0,8},{8,0},{16,24},{24,16},{1,9},{9,1},{17,25},{25,17},{2,10},{10... | collective-permute-start | bytes 503816 | tf_op jit(solution)/shard_map/ppermute | solution.py:358
  23.7 1.5 %collective-permute-done.3.even.rest_1_ = bf16[54,16,128]{2,1,0:T(8,128)(2,1)S(1)} collective-permute-done((bf16[54,16,128]{2,1,0:T(8,128)(2,1)S(1)}, bf16[54,16,128]{2,1,0:T(8,128)(2,1)S(1)}, u32[]{:S(2)}, u32[]{:S(2)}) %collective-permute-start.3) | collective-permute-done | bytes 221216 | tf_op jit(solution)/shard_map/ppermute | solution.py:358
  25.2 2.3 %collective-permute-done.4.odd.rest_2_ = bf16[54,16,128]{2,1,0:T(8,128)(2,1)S(1)} collective-permute-done((bf16[54,16,128]{2,1,0:T(8,128)(2,1)S(1)}, bf16[54,16,128]{2,1,0:T(8,128)(2,1)S(1)}, u32[]{:S(2)}, u32[]{:S(2)}) %collective-permute-start.4) | collective-permute-done | bytes 221216 | tf_op jit(solution)/shard_map/ppermute | solution.py:358
  27.4 0.9 %collective-permute-start.6 = (bf16[54,16,128]{2,1,0:T(8,128)(2,1)S(1)}, bf16[54,16,128]{2,1,0:T(8,128)(2,1)S(1)}, u32[]{:S(2)}, u32[]{:S(2)}) collective-permute-start(bf16[54,16,128]{2,1,0:T(8,128)(2,1)S(1)} %collective-permute-done.3.even.rest_1_), channel_id=1, source_target_pairs={{0,4},{4,0},{1,5},{5,1},{2,6},{6,2},{3,7},{7,3},{8,12},{12,8},{9,1... | collective-permute-start | bytes 663560 | tf_op jit(solution)/shard_map/ppermute | solution.py:358
  28.4 0.5 collective-permute-start.9
  28.9 0.6 collective-permute-done.6.mate_even.rest_5_
  29.5 0.4 collective-permute-done.7.mate_odd.rest_6_
  29.9 0.4 prepare.1
  30.3 0.1 collective-permute-done.10.rest_7_
  30.4 7.3 %unet_step.1 = (bf16[4,16,8,128]{3,2,1,0:T(8,128)(2,1)}, bf16[4,896,128]{2,1,0:T(8,128)(2,1)S(1)}, f32[4,896,128]{2,1,0:T(8,128)S(1)}) custom-call(bf16[1760,384]{1,0:T(8,128)(2,1)S(1)} %get-tuple-element.37.field, f32[6,18,8,128]{3,2,1,0:T(8,128)S(1)} %get-tuple-element.38.upstream, f32[1728,128]{1,0:T(8,128)S(1)} %copy-done, ...), custom_call_target="tpu_custom_call" | custom-call | flops 3500000000 | bytes 8000000 | tf_op jit(solution)/shard_map/unet_step/pallas_call | solution.py:252
  37.6 0.4 collective-permute-start.11
  38.0 2.2 %collective-permute-done.11 = bf16[4,896,128]{2,1,0:T(8,128)(2,1)S(1)} collective-permute-done((bf16[4,896,128]{2,1,0:T(8,128)(2,1)S(1)}, bf16[4,896,128]{2,1,0:T(8,128)(2,1)S(1)}, u32[]{:S(2)}, u32[]{:S(2)}) %collective-permute-start.11) | collective-permute-done | bytes 917536 | tf_op jit(solution)/shard_map/ppermute | solution.py:358
  40.2 0.2 add_convert_fusion
  40.4 0.1 copy.12
  40.4 0.0 copy-start.1
  40.5 20.6 %all_to_all.15 = bf16[16,224,128]{2,1,0:T(8,128)(2,1)S(1)} all-to-all(bf16[16,224,128]{2,1,0:T(8,128)(2,1)S(1)} %bitcast.16), channel_id=1, replica_groups=mesh['dp'=4,'zl'=2,'x'=4,'c'=2,'gy'=4] {'x','gy'}, dimensions={0} | all-to-all | bytes 1835008 | tf_op jit(solution)/shard_map/all_to_all | solution.py:394
  61.1 0.1 plane_sum.1
  61.2 11.5 %all_to_all.16 = bf16[8,56,128]{2,1,0:T(8,128)(2,1)S(1)} all-to-all(bf16[8,56,128]{2,1,0:T(8,128)(2,1)S(1)} %plane_sum.1), channel_id=1, replica_groups=mesh['dp'=4,'zl'=2,'x'=4,'c'=2,'gy'=4] {'dp','zl'}, dimensions={0} | all-to-all | bytes 229376 | tf_op jit(solution)/shard_map/all_to_all | solution.py:395
  72.7 10.5 %all_to_all.17 = bf16[16,56,128]{2,1,0:T(8,128)(2,1)S(1)} all-to-all(bf16[16,56,128]{2,1,0:T(8,128)(2,1)S(1)} %broadcast_in_dim.7), channel_id=1, replica_groups=mesh['dp'=4,'zl'=2,'x'=4,'c'=2,'gy'=4] {'x','gy'}, dimensions={0} | all-to-all | bytes 458752 | tf_op jit(solution)/shard_map/all_to_all | solution.py:397
  83.2 4.3 %collective-permute-start.12 = (bf16[896,128]{1,0:T(8,128)(2,1)S(1)}, bf16[896,128]{1,0:T(8,128)(2,1)S(1)}, u32[]{:S(2)}, u32[]{:S(2)}) collective-permute-start(bf16[896,128]{1,0:T(8,128)(2,1)S(1)} %bitcast.12), channel_id=1, source_target_pairs={{0,4},{4,0},{1,5},{5,1},{2,6},{6,2},{3,7},{7,3},{8,12},{12,8},{9,1... | collective-permute-start | bytes 688136 | tf_op jit(solution)/shard_map/ppermute | solution.py:358
  87.5 1.4 %adam_own.1 = (f32[1728,128]{1,0:T(8,128)}, f32[1728,128]{1,0:T(8,128)}, f32[1728,128]{1,0:T(8,128)}) custom-call(bf16[896,128]{1,0:T(8,128)(2,1)S(1)} %bitcast.13, f32[1728,128]{1,0:T(8,128)S(1)} %copy-done, f32[1728,128]{1,0:T(8,128)S(1)} %copy-done.1, f32[1728,128]{1,0:T(8,128)S(1)} %copy-done.2), custom_call_target="tpu_custom_call" | custom-call | flops 3000000 | bytes 4000000 | tf_op jit(solution)/shard_map/adam_own/pallas_call | solution.py:337
  88.9 1.5 %adam_rest.1 = (f32[1728,128]{1,0:T(8,128)}, f32[1728,128]{1,0:T(8,128)}, f32[1728,128]{1,0:T(8,128)}) custom-call(bf16[896,128]{1,0:T(8,128)(2,1)S(1)} %bitcast.14, bf16[896,128]{1,0:T(8,128)(2,1)S(1)} %collective-permute-done.12.refs_1_, f32[1728,128]{1,0:T(8,128)S(1)} %copy-done, ...), custom_call_target="tpu_custom_call", output_to_operand_aliasing={{0}: (5, {}), {1}: (6, {}), {2}: (7, {})} | custom-call | flops 3000000 | bytes 4000000 | tf_op jit(solution)/shard_map/adam_rest/pallas_call | solution.py:337
  (16 shorter events, 0.1 us)
Async XLA Ops:
  0.6 29.7 %copy-start = (f32[1728,128]{1,0:T(8,128)S(1)}, f32[1728,128]{1,0:T(8,128)}, u32[]{:S(2)}) copy-start(f32[1728,128]{1,0:T(8,128)} %refs_2_.3) | copy-start | bytes 2654212
  2.0 13.3 %collective-permute-start = (bf16[27,16,128]{2,1,0:T(8,128)(2,1)S(1)}, bf16[27,16,128]{2,1,0:T(8,128)(2,1)S(1)}, u32[]{:S(2)}, u32[]{:S(2)}) collective-permute-start(bf16[27,16,128]{2,1,0:T(8,128)(2,1)S(1)} %get-tuple-element.28), channel_id=1, source_target_pairs={{0,64},{4,196},{64,0},{68,132},{128,192},{132,68},{192,128},{196,4... | collective-permute-start | bytes 331784 | tf_op jit(solution)/shard_map/ppermute | solution.py:367
  8.9 7.9 %collective-permute-start.1 = (bf16[14,16,128]{2,1,0:T(8,128)(2,1)S(1)}, bf16[14,16,128]{2,1,0:T(8,128)(2,1)S(1)}, u32[]{:S(2)}, u32[]{:S(2)}) collective-permute-start(bf16[14,16,128]{2,1,0:T(8,128)(2,1)S(1)} %get-tuple-element.29), channel_id=1, source_target_pairs={{0,128},{64,192},{128,0},{192,64},{1,129},{65,193},{129,1},{193,65... | collective-permute-start | bytes 172040 | tf_op jit(solution)/shard_map/ppermute | solution.py:358
  9.9 8.0 %collective-permute-start.2 = (bf16[4,16,8,128]{3,2,1,0:T(8,128)(2,1)S(1)}, bf16[4,16,8,128]{3,2,1,0:T(8,128)(2,1)S(1)}, u32[]{:S(2)}, u32[]{:S(2)}) collective-permute-start(bf16[4,16,8,128]{3,2,1,0:T(8,128)(2,1)S(1)} %get-tuple-element.30), channel_id=1, source_target_pairs={{4,8},{12,16},{20,24},{28,32},{36,40},{44,48},{52,56},{8,4},{16,12... | collective-permute-start | bytes 393224 | tf_op jit(solution)/shard_map/ppermute | solution.py:363
  18.0 7.2 %collective-permute-start.3 = (bf16[54,16,128]{2,1,0:T(8,128)(2,1)S(1)}, bf16[54,16,128]{2,1,0:T(8,128)(2,1)S(1)}, u32[]{:S(2)}, u32[]{:S(2)}) collective-permute-start(bf16[54,16,128]{2,1,0:T(8,128)(2,1)S(1)} %get-tuple-element.31), channel_id=1, source_target_pairs={{0,1},{1,0},{2,3},{3,2},{4,5},{5,4},{6,7},{7,6},{8,9},{9,8},{10,11... | collective-permute-start | bytes 663560 | tf_op jit(solution)/shard_map/ppermute | solution.py:358
  19.3 8.1 %collective-permute-start.4 = (bf16[54,16,128]{2,1,0:T(8,128)(2,1)S(1)}, bf16[54,16,128]{2,1,0:T(8,128)(2,1)S(1)}, u32[]{:S(2)}, u32[]{:S(2)}) collective-permute-start(bf16[54,16,128]{2,1,0:T(8,128)(2,1)S(1)} %get-tuple-element.32), channel_id=1, source_target_pairs={{0,3},{1,2},{2,1},{3,0},{4,7},{5,6},{6,5},{7,4},{8,11},{9,10},{10,... | collective-permute-start | bytes 663560 | tf_op jit(solution)/shard_map/ppermute | solution.py:358
  21.2 2.4 %collective-permute-start.5 = (bf16[4,16,8,128]{3,2,1,0:T(8,128)(2,1)S(1)}, bf16[4,16,8,128]{3,2,1,0:T(8,128)(2,1)S(1)}, u32[]{:S(2)}, u32[]{:S(2)}) collective-permute-start(bf16[4,16,8,128]{3,2,1,0:T(8,128)(2,1)S(1)} %get-tuple-element.33), channel_id=1, source_target_pairs={{0,4},{4,0},{1,5},{5,1},{2,6},{6,2},{3,7},{7,3},{8,12},{12,8},{9,1... | collective-permute-start | bytes 393224 | tf_op jit(solution)/shard_map/ppermute | solution.py:358
  21.7 7.2 %collective-permute-start.8 = (bf16[41,16,128]{2,1,0:T(8,128)(2,1)S(1)}, bf16[41,16,128]{2,1,0:T(8,128)(2,1)S(1)}, u32[]{:S(2)}, u32[]{:S(2)}) collective-permute-start(bf16[41,16,128]{2,1,0:T(8,128)(2,1)S(1)} %constant_dynamic-update-slice_fusion.stack.rest_0_), channel_id=1, source_target_pairs={{0,8},{8,0},{16,24},{24,16},{1,9},{9,1},{17,25},{25,17},{2,10},{10... | collective-permute-start | bytes 503816 | tf_op jit(solution)/shard_map/ppermute | solution.py:358
  27.4 2.1 %collective-permute-start.6 = (bf16[54,16,128]{2,1,0:T(8,128)(2,1)S(1)}, bf16[54,16,128]{2,1,0:T(8,128)(2,1)S(1)}, u32[]{:S(2)}, u32[]{:S(2)}) collective-permute-start(bf16[54,16,128]{2,1,0:T(8,128)(2,1)S(1)} %collective-permute-done.3.even.rest_1_), channel_id=1, source_target_pairs={{0,4},{4,0},{1,5},{5,1},{2,6},{6,2},{3,7},{7,3},{8,12},{12,8},{9,1... | collective-permute-start | bytes 663560 | tf_op jit(solution)/shard_map/ppermute | solution.py:358
  28.4 1.5 %collective-permute-start.7 = (bf16[54,16,128]{2,1,0:T(8,128)(2,1)S(1)}, bf16[54,16,128]{2,1,0:T(8,128)(2,1)S(1)}, u32[]{:S(2)}, u32[]{:S(2)}) collective-permute-start(bf16[54,16,128]{2,1,0:T(8,128)(2,1)S(1)} %collective-permute-done.4.odd.rest_2_), channel_id=1, source_target_pairs={{0,4},{4,0},{1,5},{5,1},{2,6},{6,2},{3,7},{7,3},{8,12},{12,8},{9,1... | collective-permute-start | bytes 663560 | tf_op jit(solution)/shard_map/ppermute | solution.py:358
  28.4 1.9 %collective-permute-start.9 = (bf16[41,16,128]{2,1,0:T(8,128)(2,1)S(1)}, bf16[41,16,128]{2,1,0:T(8,128)(2,1)S(1)}, u32[]{:S(2)}, u32[]{:S(2)}) collective-permute-start(bf16[41,16,128]{2,1,0:T(8,128)(2,1)S(1)} %constant_dynamic-update-slice_fusion.stack.rest_0_), channel_id=1, source_target_pairs={{0,4},{4,0},{1,5},{5,1},{2,6},{6,2},{3,7},{7,3},{8,12},{12,8},{9,1... | collective-permute-start | bytes 503816 | tf_op jit(solution)/shard_map/ppermute | solution.py:358
  28.9 1.4 %collective-permute-start.10 = (bf16[41,16,128]{2,1,0:T(8,128)(2,1)S(1)}, bf16[41,16,128]{2,1,0:T(8,128)(2,1)S(1)}, u32[]{:S(2)}, u32[]{:S(2)}) collective-permute-start(bf16[41,16,128]{2,1,0:T(8,128)(2,1)S(1)} %collective-permute-done.8.rest_3_), channel_id=1, source_target_pairs={{0,4},{4,0},{1,5},{5,1},{2,6},{6,2},{3,7},{7,3},{8,12},{12,8},{9,1... | collective-permute-start | bytes 503816 | tf_op jit(solution)/shard_map/ppermute | solution.py:358
  37.6 2.6 %collective-permute-start.11 = (bf16[4,896,128]{2,1,0:T(8,128)(2,1)S(1)}, bf16[4,896,128]{2,1,0:T(8,128)(2,1)S(1)}, u32[]{:S(2)}, u32[]{:S(2)}) collective-permute-start(bf16[4,896,128]{2,1,0:T(8,128)(2,1)S(1)} %get-tuple-element.41), channel_id=1, source_target_pairs={{0,4},{4,0},{1,5},{5,1},{2,6},{6,2},{3,7},{7,3},{8,12},{12,8},{9,1... | collective-permute-start | bytes 2752520 | tf_op jit(solution)/shard_map/ppermute | solution.py:358
  40.4 47.1 %copy-start.1 = (f32[1728,128]{1,0:T(8,128)S(1)}, f32[1728,128]{1,0:T(8,128)}, u32[]{:S(2)}) copy-start(f32[1728,128]{1,0:T(8,128)} %refs_3_.3) | copy-start | bytes 2654212
  40.5 47.1 %copy-start.2 = (f32[1728,128]{1,0:T(8,128)S(1)}, f32[1728,128]{1,0:T(8,128)}, u32[]{:S(2)}) copy-start(f32[1728,128]{1,0:T(8,128)} %refs_4_.1) | copy-start | bytes 2654212
  83.2 5.7 %collective-permute-start.12 = (bf16[896,128]{1,0:T(8,128)(2,1)S(1)}, bf16[896,128]{1,0:T(8,128)(2,1)S(1)}, u32[]{:S(2)}, u32[]{:S(2)}) collective-permute-start(bf16[896,128]{1,0:T(8,128)(2,1)S(1)} %bitcast.12), channel_id=1, source_target_pairs={{0,4},{4,0},{1,5},{5,1},{2,6},{6,2},{3,7},{7,3},{8,12},{12,8},{9,1... | collective-permute-start | bytes 688136 | tf_op jit(solution)/shard_map/ppermute | solution.py:358

commit v4 on v3

--- a/solution.py
+++ b/solution.py
@@ -21,6 +21,7 @@
 C = 128
 SX, SY, SZ = 4, 16, 8
 NX, NY = 64, 64
+PLANES_ONE, PLANES_TWO, PLANES_BACK = 2, 3, 2
 TAPS = 14
 HALF = TAPS // 2 * C
 PIECE = HALF // 16
@@ -53,10 +54,11 @@
         ref[rows, position * C : (position + 1) * C] = part
 
 
-def conv_rows(ref, planes_out, wide, weights):
+def conv_planes(ref, first, planes_out, wide, weights):
     rows = planes_out * wide * SZ
     step = wide * SZ
-    left = jnp.concatenate([ref[a * step : a * step + rows, :] for a in range(3)], axis=1)
+    starts = [(first + a) * step for a in range(3)]
+    left = jnp.concatenate([ref[start : start + rows, :] for start in starts], axis=1)
     prod = jnp.dot(left, weights, preferred_element_type=F32).reshape(planes_out, wide, SZ, 3 * C)
     return (
         prod[:, 0 : wide - 2, :, 0:C]
@@ -73,7 +75,7 @@
     return jnp.concatenate(columns, axis=1)
 
 
-def grad_taps(grads, layer, ref, wide, first_plane, shift, delta):
+def grad_taps(grads, ref, wide, first_plane, shift, delta):
     lefts = []
     for b in range(3):
         before, after = shift + b, wide - SY - shift - b
@@ -94,7 +96,7 @@
     for tap in range(27):
         a, b, c = tap // 9, tap // 3 % 3, tap % 3
         column = (3 * a + c) * C
-        grads[layer * 27 + tap] = prod[b * C : (b + 1) * C, column : column + C]
+        grads[tap] = prod[b * C : (b + 1) * C, column : column + C]
 
 
 def payload_kernel(vol, cot, master, whole, half, near, far, vol_out, cot_out, rows, sems):
@@ -204,10 +206,16 @@
     )(vol, cot, near, far, even, odd, mate_even, mate_odd)
 
 
-def step_kernel(field, upstream, master, *rest):
+def halves(grads, core, keep, send):
+    for shard in range(2):
+        keep[shard] = grads[pl.ds(13 * shard + 7 * core, 7)].reshape(16, PIECE, C)
+        send[shard] = grads[pl.ds(13 * shard + 7 * (1 - core), 7)].reshape(16, PIECE, C).astype(send.dtype)
+
+
+def forward_kernel(field, upstream, master, *rest):
     pieces = rest[:8]
-    act, send, keep = rest[8:11]
-    taps, flipped, hid, dlt, grads = rest[11:]
+    act, dlt, slope, flipped, send, keep = rest[8:14]
+    taps, hid, grads = rest[14:]
     gx, gy, core, dp, quarter = position()
 
     taps[pl.ds(dp * 27, 27)] = master[...].astype(BF).reshape(27, 64, C)
@@ -219,56 +227,106 @@
         taps[pl.ds((dp ^ 2) * 27 + 13 * owner_core, 14), rows, :] = piece[27:41]
     tap_rows = taps[...].reshape(54 * C, C)
 
-    first = conv_rows(field, 8, 22, layer_weights(tap_rows, 0))
-    x_at = lax.broadcasted_iota(jnp.int32, first.shape, 0) + (gx * SX - 2)
-    y_at = lax.broadcasted_iota(jnp.int32, first.shape, 1) + (gy * SY - 2)
-    inside = (x_at >= 0) & (x_at < NX) & (y_at >= 0) & (y_at < NY)
-    hidden = jnp.where(inside, gelu_value(first), 0.0)
-    slope_one = gelu_slope(first[2:6, 2:18])
-    store_triple(hid, slice(0, 8 * 160), hidden)
-
-    second = conv_rows(hid, 6, 20, layer_weights(tap_rows, 1))
-    act[...] = gelu_value(second[1:5, 1:17]).astype(BF)
-    delta_two = upstream[...] * gelu_slope(second)
-    store_triple(dlt, slice(0, 6 * 144), delta_two)
-    grad_taps(grads, 1, hid, 20, 1, 1, delta_two[1:5, 1:17])
+    weights = layer_weights(tap_rows, 0)
+    slopes = []
+    for at in range(0, 8, PLANES_ONE):
+        first = conv_planes(field, at, PLANES_ONE, 22, weights)
+        x_at = lax.broadcasted_iota(jnp.int32, first.shape, 0) + (gx * SX - 2 + at)
+        y_at = lax.broadcasted_iota(jnp.int32, first.shape, 1) + (gy * SY - 2)
+        inside = (x_at >= 0) & (x_at < NX) & (y_at >= 0) & (y_at < NY)
+        store_triple(hid, slice(at * 160, (at + PLANES_ONE) * 160), jnp.where(inside, gelu_value(first), 0.0))
+        begin, end = max(at, 2) - at, min(at + PLANES_ONE, 6) - at
+        if begin < end:
+            slopes.append(gelu_slope(first[begin:end, 2:18]))
+    slope[...] = jnp.concatenate(slopes)
+
+    weights = layer_weights(tap_rows, 1)
+    deltas = []
+    for at in range(0, 6, PLANES_TWO):
+        second = conv_planes(hid, at, PLANES_TWO, 20, weights)
+        delta = upstream[at : at + PLANES_TWO] * gelu_slope(second)
+        store_triple(dlt, slice(at * 144, (at + PLANES_TWO) * 144), delta)
+        begin, end = max(at, 1) - at, min(at + PLANES_TWO, 5) - at
+        if begin < end:
+            act[at + begin - 1 : at + end - 1] = gelu_value(second[begin:end, 1:17]).astype(BF)
+            deltas.append(delta[begin:end, 1:17])
+    grad_taps(grads, hid, 20, 1, 1, jnp.concatenate(deltas))
+    halves(grads, core, keep, send)
 
     for t in range(27):
         a, b, c = t // 9, t // 3 % 3, t % 3
         row = (27 + 26 - t) * C
         block = jnp.transpose(tap_rows[row : row + C].astype(F32)).astype(BF)
         flipped[(3 * a + c) * C : (3 * a + c + 1) * C, b * C : (b + 1) * C] = block
-    back = conv_rows(dlt, 4, 18, flipped[...])
-    grad_taps(grads, 0, field, 22, 2, 2, back * slope_one)
-
-    for shard in range(4):
-        base = 27 * (shard // 2) + 13 * (shard % 2)
-        keep[shard] = grads[pl.ds(base + 7 * core, 7)].reshape(HALF, C)
-        send[shard] = grads[pl.ds(base + 7 * (1 - core), 7)].reshape(HALF, C).astype(BF)
-
-
-def device_step(field, upstream, master, pieces):
-    vmem = pl.BlockSpec(memory_space=pltpu.VMEM)
-    return pl.pallas_call(
-        step_kernel,
+
+
+def backward_kernel(field, dlt, slope, flipped, send, keep, grads):
+    weights = flipped[...]
+    back = [conv_planes(dlt, at, PLANES_BACK, 18, weights) for at in range(0, 4, PLANES_BACK)]
+    grad_taps(grads, field, 22, 2, 2, jnp.concatenate(back) * slope[...])
+    halves(grads, lax.axis_index("c"), keep, send)
+
+
+GRADIENT = (2, 16, PIECE, C)
+
+
+def forward(field, upstream, master, pieces):
+    vmem = pl.BlockSpec(memory_space=pltpu.VMEM)
+    return pl.pallas_call(
+        forward_kernel,
         out_shape=(
             jax.ShapeDtypeStruct((SX, SY, SZ, C), BF),
-            jax.ShapeDtypeStruct((4, HALF, C), BF),
-            jax.ShapeDtypeStruct((4, HALF, C), F32),
+            jax.ShapeDtypeStruct((6 * 144, 3 * C), BF),
+            jax.ShapeDtypeStruct((SX, SY, SZ, C), F32),
+            jax.ShapeDtypeStruct((9 * C, 3 * C), BF),
+            jax.ShapeDtypeStruct(GRADIENT, F32),
+            jax.ShapeDtypeStruct(GRADIENT, F32),
         ),
         in_specs=[vmem] * 11,
-        out_specs=(vmem, vmem, vmem),
+        out_specs=(vmem,) * 6,
         scratch_shapes=[
             pltpu.VMEM((108, 64, C), BF),
-            pltpu.VMEM((9 * C, 3 * C), BF),
             pltpu.VMEM((8 * 160, 3 * C), BF),
-            pltpu.VMEM((6 * 144, 3 * C), BF),
-            pltpu.VMEM((54, C, C), F32),
+            pltpu.VMEM((27, C, C), F32),
         ],
-        compiler_params=pltpu.CompilerParams(vmem_limit_bytes=44 * 2**20),
-        cost_estimate=pl.CostEstimate(flops=3_500_000_000, bytes_accessed=8_000_000, transcendentals=1_000_000),
-        name="unet_step",
+        compiler_params=pltpu.CompilerParams(vmem_limit_bytes=40 * 2**20),
+        cost_estimate=pl.CostEstimate(flops=2_500_000_000, bytes_accessed=8_000_000, transcendentals=1_000_000),
+        name="forward",
     )(field, upstream, master, *pieces)
+
+
+def backward(field, dlt, slope, flipped):
+    vmem = pl.BlockSpec(memory_space=pltpu.VMEM)
+    return pl.pallas_call(
+        backward_kernel,
+        out_shape=(jax.ShapeDtypeStruct(GRADIENT, BF), jax.ShapeDtypeStruct(GRADIENT, F32)),
+        in_specs=[vmem] * 4,
+        out_specs=(vmem,) * 2,
+        scratch_shapes=[pltpu.VMEM((27, C, C), F32)],
+        compiler_params=pltpu.CompilerParams(vmem_limit_bytes=32 * 2**20),
+        cost_estimate=pl.CostEstimate(flops=8_000_000_000, bytes_accessed=8_000_000, transcendentals=0),
+        name="backward",
+    )(field, dlt, slope, flipped)
+
+
+def pair_kernel(keep_one, got_one, keep_two, got_two, out):
+    for layer, (keep, got) in enumerate(((keep_one, got_one), (keep_two, got_two))):
+        for shard in range(2):
+            total = keep[shard] + got[shard].astype(F32)
+            for piece in range(16):
+                out[piece, 2 * layer + shard] = total[piece].astype(BF)
+
+
+def pair_sum(keep_one, got_one, keep_two, got_two):
+    vmem = pl.BlockSpec(memory_space=pltpu.VMEM)
+    return pl.pallas_call(
+        pair_kernel,
+        out_shape=jax.ShapeDtypeStruct((16, 4, PIECE, C), BF),
+        in_specs=[vmem] * 4,
+        out_specs=vmem,
+        compiler_params=pltpu.CompilerParams(vmem_limit_bytes=16 * 2**20),
+        name="pair_sum",
+    )(keep_one, got_one, keep_two, got_two)
 
 
 def plane_kernel(parts, out):
@@ -387,10 +445,12 @@
     mates = [exchanged(part, "c", 2, 1) for part in mine]
     pieces = mine + mates
     field, upstream = prepare(vol, cot, near, far, even, odd, mates[1], mates[2])
-    act, send, keep = device_step(field, upstream, master, pieces)
-
-    pair = (keep + exchanged(send, "c", 2, 1).astype(F32)).astype(BF)
-    spread = pair.reshape(4, 16, PIECE, C).transpose(1, 0, 2, 3).reshape(16, 4 * PIECE, C)
+    act, dlt, slope, flipped, send_two, keep_two = forward(field, upstream, master, pieces)
+    got_two = exchanged(send_two, "c", 2, 1)
+    send_one, keep_one = backward(field, dlt, slope, flipped)
+    got_one = exchanged(send_one, "c", 2, 1)
+
+    spread = pair_sum(keep_one, got_one, keep_two, got_two).reshape(16, 4 * PIECE, C)
     plane = lax.all_to_all(spread, ("x", "gy"), 0, 0)
     column = lax.all_to_all(plane_sum(plane.reshape(16, 4, PIECE, C)), ("dp", "zl"), 0, 0)
     column = jnp.sum(column.astype(F32), axis=0).astype(BF)

time: 90.8 us -> 90.6 us (level)
    ppermute x11 -> x12, waiting for transfers between devices: 8.57 us -> 8.03 us  [exchanged(): return lax.ppermute(cells, axis, [(i, i ^ by) for i in range(count)])]
    ppermute x11 -> x12, starting transfers between devices: 12.8 us -> 13.1 us  [exchanged(): return lax.ppermute(cells, axis, [(i, i ^ by) for i in range(count)])]
    pallas_call x1 -> x3, Pallas kernels: 7.26 us -> 7.47 us  [the longest x1 5.08 us: forward(): pl.pallas_call(forward_kernel, out_shape=(jax.ShapeDtypeStruct((SX, SY, S...]
  transfers between devices with their start and end apart: 13 -> 14, of which waited for: 8 -> 8; matrix products, arithmetic and copies ran while one was open for 0% -> 0% of each run, Pallas kernels for 2% -> 4%
where the time goes in v4:
time: 90.6 us; the launch traced here: 90.3 us
  blocking collectives  42.7 us (47%)
  starting transfers between devices  25.4 us (28%)
  Pallas kernels  12.2 us (13%)
  waiting for transfers between devices  9.05 us (10%)
    all_to_all x1, blocking collectives, per_device(): plane = lax.all_to_all(spread, ('x', 'gy'), 0, 0)  20.3 us
    ppermute x12, starting transfers between devices, exchanged(): return lax.ppermute(cells, axis, [(i, i ^ by) for i in range(count)])  13.1 us
    all_to_all x1, blocking collectives, per_device(): lax.all_to_all(plane_sum(plane.reshape(16, 4, PIECE, C)), ('dp', 'zl'), 0...  11.6 us
    all_to_all x1, blocking collectives, per_device(): lax.all_to_all(jnp.broadcast_to(column, (16, PIECE, C)), ('x', 'gy'), 0, 0)  10.7 us
    ppermute x12, waiting for transfers between devices, exchanged(): return lax.ppermute(cells, axis, [(i, i ^ by) for i in range(count)])  8.03 us
    ppermute x1, starting transfers between devices, over_dp(): lax.ppermute(whole, ('dp', 'c'), [(2 * d + c, 2 * (d ^ 1 + 2 * c) + c) fo...  6.94 us
    ppermute x1, starting transfers between devices, paired(): return lax.ppermute(cells, axis, pairs + [(j, i) for i, j in pairs])  5.32 us
    pallas_call x1, Pallas kernels, forward(): pl.pallas_call(forward_kernel, out_shape=(jax.ShapeDtypeStruct((SX, SY, S...  5.08 us
  transfers between devices with their start and end apart: 14, of which 8 were waited for; matrix products, arithmetic and copies ran while one was open for 0% of the time, Pallas kernels for 4%

profile of v4, /device:TPU:1, one launch (start us, length us, event | category | flops | bytes accessed | tf_op | source)
XLA Modules:
  0.0 90.3 jit_solution(1611580775094708801)
XLA Ops:
  0.6 1.3 %payloads.1 = (bf16[27,16,128]{2,1,0:T(8,128)(2,1)S(1)}, bf16[14,16,128]{2,1,0:T(8,128)(2,1)S(1)}, bf16[4,16,8,128]{3,2,1,0:T(8,128)(2,1)S(1)}, bf16[4,16,8,128]...) custom-call(bf16[4,16,8,128]{3,2,1,0:T(8,128)(2,1)} %bitcast.13, ...), custom_call_target="tpu_custom_call" | custom-call | tf_op jit(solution)/shard_map/payloads/pallas_call | solution.py:127
  1.9 6.9 %collective-permute-start = (bf16[27,16,128]{2,1,0:T(8,128)(2,1)S(1)}, bf16[27,16,128]{2,1,0:T(8,128)(2,1)S(1)}, u32[]{:S(2)}, u32[]{:S(2)}) collective-permute-start(bf16[27,16,128]{2,1,0:T(8,128)(2,1)S(1)} %get-tuple-element.33), channel_id=1, source_target_pairs={{0,64},{4,196},{64,0},{68,132},{128,192},{132,68},{192,128},{196,4... | collective-permute-start | bytes 331784 | tf_op jit(solution)/shard_map/ppermute | solution.py:425
  8.9 1.0 %collective-permute-start.1 = (bf16[14,16,128]{2,1,0:T(8,128)(2,1)S(1)}, bf16[14,16,128]{2,1,0:T(8,128)(2,1)S(1)}, u32[]{:S(2)}, u32[]{:S(2)}) collective-permute-start(bf16[14,16,128]{2,1,0:T(8,128)(2,1)S(1)} %get-tuple-element.34), channel_id=1, source_target_pairs={{0,128},{64,192},{128,0},{192,64},{1,129},{65,193},{129,1},{193,65... | collective-permute-start | bytes 172040 | tf_op jit(solution)/shard_map/ppermute | solution.py:416
  9.9 5.3 %collective-permute-start.2 = (bf16[4,16,8,128]{3,2,1,0:T(8,128)(2,1)S(1)}, bf16[4,16,8,128]{3,2,1,0:T(8,128)(2,1)S(1)}, u32[]{:S(2)}, u32[]{:S(2)}) collective-permute-start(bf16[4,16,8,128]{3,2,1,0:T(8,128)(2,1)S(1)} %get-tuple-element.35), channel_id=1, source_target_pairs={{4,8},{12,16},{20,24},{28,32},{36,40},{44,48},{52,56},{8,4},{16,12... | collective-permute-start | bytes 393224 | tf_op jit(solution)/shard_map/ppermute | solution.py:421
  15.2 1.6 %collective-permute-done.1 = bf16[14,16,128]{2,1,0:T(8,128)(2,1)S(1)} collective-permute-done((bf16[14,16,128]{2,1,0:T(8,128)(2,1)S(1)}, bf16[14,16,128]{2,1,0:T(8,128)(2,1)S(1)}, u32[]{:S(2)}, u32[]{:S(2)}) %collective-permute-start.1) | collective-permute-done | bytes 57376 | tf_op jit(solution)/shard_map/ppermute | solution.py:416
  16.8 1.0 %collective-permute-done.2.far = bf16[4,16,8,128]{3,2,1,0:T(8,128)(2,1)S(1)} collective-permute-done((bf16[4,16,8,128]{3,2,1,0:T(8,128)(2,1)S(1)}, bf16[4,16,8,128]{3,2,1,0:T(8,128)(2,1)S(1)}, u32[]{:S(2)}, u32[]{:S(2)}) %collective-permute-start.2) | collective-permute-done | bytes 131104 | tf_op jit(solution)/shard_map/ppermute | solution.py:421
  17.8 0.1 relay.1
  17.9 1.4 %collective-permute-start.3 = (bf16[54,16,128]{2,1,0:T(8,128)(2,1)S(1)}, bf16[54,16,128]{2,1,0:T(8,128)(2,1)S(1)}, u32[]{:S(2)}, u32[]{:S(2)}) collective-permute-start(bf16[54,16,128]{2,1,0:T(8,128)(2,1)S(1)} %get-tuple-element.36), channel_id=1, source_target_pairs={{0,1},{1,0},{2,3},{3,2},{4,5},{5,4},{6,7},{7,6},{8,9},{9,8},{10,11... | collective-permute-start | bytes 663560 | tf_op jit(solution)/shard_map/ppermute | solution.py:416
  19.3 1.9 %collective-permute-start.4 = (bf16[54,16,128]{2,1,0:T(8,128)(2,1)S(1)}, bf16[54,16,128]{2,1,0:T(8,128)(2,1)S(1)}, u32[]{:S(2)}, u32[]{:S(2)}) collective-permute-start(bf16[54,16,128]{2,1,0:T(8,128)(2,1)S(1)} %get-tuple-element.37), channel_id=1, source_target_pairs={{0,3},{1,2},{2,1},{3,0},{4,7},{5,6},{6,5},{7,4},{8,11},{9,10},{10,... | collective-permute-start | bytes 663560 | tf_op jit(solution)/shard_map/ppermute | solution.py:416
  21.2 0.4 collective-permute-start.5
  21.6 2.0 %collective-permute-start.8 = (bf16[41,16,128]{2,1,0:T(8,128)(2,1)S(1)}, bf16[41,16,128]{2,1,0:T(8,128)(2,1)S(1)}, u32[]{:S(2)}, u32[]{:S(2)}) collective-permute-start(bf16[41,16,128]{2,1,0:T(8,128)(2,1)S(1)} %constant_dynamic-update-slice_fusion.stack.rest_0_), channel_id=1, source_target_pairs={{0,8},{8,0},{16,24},{24,16},{1,9},{9,1},{17,25},{25,17},{2,10},{10... | collective-permute-start | bytes 503816 | tf_op jit(solution)/shard_map/ppermute | solution.py:416
  23.6 1.5 %collective-permute-done.3.even.rest_1_ = bf16[54,16,128]{2,1,0:T(8,128)(2,1)S(1)} collective-permute-done((bf16[54,16,128]{2,1,0:T(8,128)(2,1)S(1)}, bf16[54,16,128]{2,1,0:T(8,128)(2,1)S(1)}, u32[]{:S(2)}, u32[]{:S(2)}) %collective-permute-start.3) | collective-permute-done | bytes 221216 | tf_op jit(solution)/shard_map/ppermute | solution.py:416
  25.1 2.3 %collective-permute-done.4.odd.rest_2_ = bf16[54,16,128]{2,1,0:T(8,128)(2,1)S(1)} collective-permute-done((bf16[54,16,128]{2,1,0:T(8,128)(2,1)S(1)}, bf16[54,16,128]{2,1,0:T(8,128)(2,1)S(1)}, u32[]{:S(2)}, u32[]{:S(2)}) %collective-permute-start.4) | collective-permute-done | bytes 221216 | tf_op jit(solution)/shard_map/ppermute | solution.py:416
  27.4 0.9 %collective-permute-start.6 = (bf16[54,16,128]{2,1,0:T(8,128)(2,1)S(1)}, bf16[54,16,128]{2,1,0:T(8,128)(2,1)S(1)}, u32[]{:S(2)}, u32[]{:S(2)}) collective-permute-start(bf16[54,16,128]{2,1,0:T(8,128)(2,1)S(1)} %collective-permute-done.3.even.rest_1_), channel_id=1, source_target_pairs={{0,4},{4,0},{1,5},{5,1},{2,6},{6,2},{3,7},{7,3},{8,12},{12,8},{9,1... | collective-permute-start | bytes 663560 | tf_op jit(solution)/shard_map/ppermute | solution.py:416
  28.3 0.5 collective-permute-start.9
  28.9 0.6 collective-permute-done.6.mate_even.rest_5_
  29.4 0.4 collective-permute-done.7.mate_odd.rest_6_
  29.8 0.4 prepare.1
  30.2 0.1 collective-permute-done.10.rest_7_
  30.3 5.1 %forward.1 = (bf16[4,16,8,128]{3,2,1,0:T(8,128)(2,1)}, bf16[864,384]{1,0:T(8,128)(2,1)S(1)}, f32[4,16,8,128]{3,2,1,0:T(8,128)S(1)}, bf16[1152,384]{1,0:T(8,128)(...) custom-call(bf16[1760,384]{1,0:T(8,128)(2,1)S(1)} %get-tuple-element.42.field, ...), custom_call_target="tpu_custom_call" | custom-call | flops 2500000000 | bytes 8000000 | tf_op jit(solution)/shard_map/forward/pallas_call | solution.py:275
  35.4 0.6 collective-permute-start.12
  35.9 2.2 %backward.1 = (bf16[2,16,56,128]{3,2,1,0:T(8,128)(2,1)S(1)}, f32[2,16,56,128]{3,2,1,0:T(8,128)S(1)}) custom-call(bf16[1760,384]{1,0:T(8,128)(2,1)S(1)} %get-tuple-element.42.field, bf16[864,384]{1,0:T(8,128)(2,1)S(1)} %get-tuple-element.45.dlt, f32[4,16,8,128]{3,2,1,0:T(8,128)S(1)} %get-tuple-element.46.slope, bf16[1152,384]{1,0:T(8,128)(2,1)S(1)} %get-tuple-element.47.flipped), custom_call_target="tpu_custom_call" | custom-call | flops 8000000000 | bytes 8000000 | tf_op jit(solution)/shard_map/backward/pallas_call | solution.py:300
  38.2 0.3 collective-permute-start.11
  38.4 1.6 %collective-permute-done.11.got_one = bf16[2,16,56,128]{3,2,1,0:T(8,128)(2,1)S(1)} collective-permute-done((bf16[2,16,56,128]{3,2,1,0:T(8,128)(2,1)S(1)}, bf16[2,16,56,128]{3,2,1,0:T(8,128)(2,1)S(1)}, u32[]{:S(2)}, u32[]{:S(2)}) %collective-permute-start.11) | collective-permute-done | bytes 458784 | tf_op jit(solution)/shard_map/ppermute | solution.py:416
  40.1 0.2 pair_sum.1
  40.2 20.3 %all_to_all.15 = bf16[16,224,128]{2,1,0:T(8,128)(2,1)S(1)} all-to-all(bf16[16,224,128]{2,1,0:T(8,128)(2,1)S(1)} %bitcast.9), channel_id=1, replica_groups=mesh['dp'=4,'zl'=2,'x'=4,'c'=2,'gy'=4] {'x','gy'}, dimensions={0} | all-to-all | bytes 1835008 | tf_op jit(solution)/shard_map/all_to_all | solution.py:454
  60.6 0.1 plane_sum.1
  60.7 11.6 %all_to_all.16 = bf16[8,56,128]{2,1,0:T(8,128)(2,1)S(1)} all-to-all(bf16[8,56,128]{2,1,0:T(8,128)(2,1)S(1)} %plane_sum.1), channel_id=1, replica_groups=mesh['dp'=4,'zl'=2,'x'=4,'c'=2,'gy'=4] {'dp','zl'}, dimensions={0} | all-to-all | bytes 229376 | tf_op jit(solution)/shard_map/all_to_all | solution.py:455
  72.4 10.7 %all_to_all.17 = bf16[16,56,128]{2,1,0:T(8,128)(2,1)S(1)} all-to-all(bf16[16,56,128]{2,1,0:T(8,128)(2,1)S(1)} %broadcast_in_dim.7), channel_id=1, replica_groups=mesh['dp'=4,'zl'=2,'x'=4,'c'=2,'gy'=4] {'x','gy'}, dimensions={0} | all-to-all | bytes 458752 | tf_op jit(solution)/shard_map/all_to_all | solution.py:457
  83.1 4.2 %collective-permute-start.13 = (bf16[896,128]{1,0:T(8,128)(2,1)S(1)}, bf16[896,128]{1,0:T(8,128)(2,1)S(1)}, u32[]{:S(2)}, u32[]{:S(2)}) collective-permute-start(bf16[896,128]{1,0:T(8,128)(2,1)S(1)} %bitcast.10), channel_id=1, source_target_pairs={{0,4},{4,0},{1,5},{5,1},{2,6},{6,2},{3,7},{7,3},{8,12},{12,8},{9,1... | collective-permute-start | bytes 688136 | tf_op jit(solution)/shard_map/ppermute | solution.py:416
  87.3 1.4 %adam_own.1 = (f32[1728,128]{1,0:T(8,128)}, f32[1728,128]{1,0:T(8,128)}, f32[1728,128]{1,0:T(8,128)}) custom-call(bf16[896,128]{1,0:T(8,128)(2,1)S(1)} %bitcast.11, f32[1728,128]{1,0:T(8,128)S(1)} %copy-done, f32[1728,128]{1,0:T(8,128)S(1)} %copy-done.1, f32[1728,128]{1,0:T(8,128)S(1)} %copy-done.2), custom_call_target="tpu_custom_call" | custom-call | flops 3000000 | bytes 4000000 | tf_op jit(solution)/shard_map/adam_own/pallas_call | solution.py:395
  88.7 1.5 %adam_rest.1 = (f32[1728,128]{1,0:T(8,128)}, f32[1728,128]{1,0:T(8,128)}, f32[1728,128]{1,0:T(8,128)}) custom-call(bf16[896,128]{1,0:T(8,128)(2,1)S(1)} %bitcast.12, bf16[896,128]{1,0:T(8,128)(2,1)S(1)} %collective-permute-done.13.refs_1_, f32[1728,128]{1,0:T(8,128)S(1)} %copy-done, ...), custom_call_target="tpu_custom_call", output_to_operand_aliasing={{0}: (5, {}), {1}: (6, {}), {2}: (7, {})} | custom-call | flops 3000000 | bytes 4000000 | tf_op jit(solution)/shard_map/adam_rest/pallas_call | solution.py:395
  (18 shorter events, 0.1 us)
Async XLA Ops:
  1.9 28.4 %copy-start = (f32[1728,128]{1,0:T(8,128)S(1)}, f32[1728,128]{1,0:T(8,128)}, u32[]{:S(2)}) copy-start(f32[1728,128]{1,0:T(8,128)} %refs_2_.3) | copy-start | bytes 2654212
  1.9 13.3 %collective-permute-start = (bf16[27,16,128]{2,1,0:T(8,128)(2,1)S(1)}, bf16[27,16,128]{2,1,0:T(8,128)(2,1)S(1)}, u32[]{:S(2)}, u32[]{:S(2)}) collective-permute-start(bf16[27,16,128]{2,1,0:T(8,128)(2,1)S(1)} %get-tuple-element.33), channel_id=1, source_target_pairs={{0,64},{4,196},{64,0},{68,132},{128,192},{132,68},{192,128},{196,4... | collective-permute-start | bytes 331784 | tf_op jit(solution)/shard_map/ppermute | solution.py:425
  8.9 7.9 %collective-permute-start.1 = (bf16[14,16,128]{2,1,0:T(8,128)(2,1)S(1)}, bf16[14,16,128]{2,1,0:T(8,128)(2,1)S(1)}, u32[]{:S(2)}, u32[]{:S(2)}) collective-permute-start(bf16[14,16,128]{2,1,0:T(8,128)(2,1)S(1)} %get-tuple-element.34), channel_id=1, source_target_pairs={{0,128},{64,192},{128,0},{192,64},{1,129},{65,193},{129,1},{193,65... | collective-permute-start | bytes 172040 | tf_op jit(solution)/shard_map/ppermute | solution.py:416
  9.9 8.0 %collective-permute-start.2 = (bf16[4,16,8,128]{3,2,1,0:T(8,128)(2,1)S(1)}, bf16[4,16,8,128]{3,2,1,0:T(8,128)(2,1)S(1)}, u32[]{:S(2)}, u32[]{:S(2)}) collective-permute-start(bf16[4,16,8,128]{3,2,1,0:T(8,128)(2,1)S(1)} %get-tuple-element.35), channel_id=1, source_target_pairs={{4,8},{12,16},{20,24},{28,32},{36,40},{44,48},{52,56},{8,4},{16,12... | collective-permute-start | bytes 393224 | tf_op jit(solution)/shard_map/ppermute | solution.py:421
  17.9 7.2 %collective-permute-start.3 = (bf16[54,16,128]{2,1,0:T(8,128)(2,1)S(1)}, bf16[54,16,128]{2,1,0:T(8,128)(2,1)S(1)}, u32[]{:S(2)}, u32[]{:S(2)}) collective-permute-start(bf16[54,16,128]{2,1,0:T(8,128)(2,1)S(1)} %get-tuple-element.36), channel_id=1, source_target_pairs={{0,1},{1,0},{2,3},{3,2},{4,5},{5,4},{6,7},{7,6},{8,9},{9,8},{10,11... | collective-permute-start | bytes 663560 | tf_op jit(solution)/shard_map/ppermute | solution.py:416
  19.3 8.1 %collective-permute-start.4 = (bf16[54,16,128]{2,1,0:T(8,128)(2,1)S(1)}, bf16[54,16,128]{2,1,0:T(8,128)(2,1)S(1)}, u32[]{:S(2)}, u32[]{:S(2)}) collective-permute-start(bf16[54,16,128]{2,1,0:T(8,128)(2,1)S(1)} %get-tuple-element.37), channel_id=1, source_target_pairs={{0,3},{1,2},{2,1},{3,0},{4,7},{5,6},{6,5},{7,4},{8,11},{9,10},{10,... | collective-permute-start | bytes 663560 | tf_op jit(solution)/shard_map/ppermute | solution.py:416
  21.2 2.4 %collective-permute-start.5 = (bf16[4,16,8,128]{3,2,1,0:T(8,128)(2,1)S(1)}, bf16[4,16,8,128]{3,2,1,0:T(8,128)(2,1)S(1)}, u32[]{:S(2)}, u32[]{:S(2)}) collective-permute-start(bf16[4,16,8,128]{3,2,1,0:T(8,128)(2,1)S(1)} %get-tuple-element.38), channel_id=1, source_target_pairs={{0,4},{4,0},{1,5},{5,1},{2,6},{6,2},{3,7},{7,3},{8,12},{12,8},{9,1... | collective-permute-start | bytes 393224 | tf_op jit(solution)/shard_map/ppermute | solution.py:416
  21.6 7.2 %collective-permute-start.8 = (bf16[41,16,128]{2,1,0:T(8,128)(2,1)S(1)}, bf16[41,16,128]{2,1,0:T(8,128)(2,1)S(1)}, u32[]{:S(2)}, u32[]{:S(2)}) collective-permute-start(bf16[41,16,128]{2,1,0:T(8,128)(2,1)S(1)} %constant_dynamic-update-slice_fusion.stack.rest_0_), channel_id=1, source_target_pairs={{0,8},{8,0},{16,24},{24,16},{1,9},{9,1},{17,25},{25,17},{2,10},{10... | collective-permute-start | bytes 503816 | tf_op jit(solution)/shard_map/ppermute | solution.py:416
  27.4 2.1 %collective-permute-start.6 = (bf16[54,16,128]{2,1,0:T(8,128)(2,1)S(1)}, bf16[54,16,128]{2,1,0:T(8,128)(2,1)S(1)}, u32[]{:S(2)}, u32[]{:S(2)}) collective-permute-start(bf16[54,16,128]{2,1,0:T(8,128)(2,1)S(1)} %collective-permute-done.3.even.rest_1_), channel_id=1, source_target_pairs={{0,4},{4,0},{1,5},{5,1},{2,6},{6,2},{3,7},{7,3},{8,12},{12,8},{9,1... | collective-permute-start | bytes 663560 | tf_op jit(solution)/shard_map/ppermute | solution.py:416
  28.3 1.5 %collective-permute-start.7 = (bf16[54,16,128]{2,1,0:T(8,128)(2,1)S(1)}, bf16[54,16,128]{2,1,0:T(8,128)(2,1)S(1)}, u32[]{:S(2)}, u32[]{:S(2)}) collective-permute-start(bf16[54,16,128]{2,1,0:T(8,128)(2,1)S(1)} %collective-permute-done.4.odd.rest_2_), channel_id=1, source_target_pairs={{0,4},{4,0},{1,5},{5,1},{2,6},{6,2},{3,7},{7,3},{8,12},{12,8},{9,1... | collective-permute-start | bytes 663560 | tf_op jit(solution)/shard_map/ppermute | solution.py:416
  28.3 1.9 %collective-permute-start.9 = (bf16[41,16,128]{2,1,0:T(8,128)(2,1)S(1)}, bf16[41,16,128]{2,1,0:T(8,128)(2,1)S(1)}, u32[]{:S(2)}, u32[]{:S(2)}) collective-permute-start(bf16[41,16,128]{2,1,0:T(8,128)(2,1)S(1)} %constant_dynamic-update-slice_fusion.stack.rest_0_), channel_id=1, source_target_pairs={{0,4},{4,0},{1,5},{5,1},{2,6},{6,2},{3,7},{7,3},{8,12},{12,8},{9,1... | collective-permute-start | bytes 503816 | tf_op jit(solution)/shard_map/ppermute | solution.py:416
  28.9 1.4 %collective-permute-start.10 = (bf16[41,16,128]{2,1,0:T(8,128)(2,1)S(1)}, bf16[41,16,128]{2,1,0:T(8,128)(2,1)S(1)}, u32[]{:S(2)}, u32[]{:S(2)}) collective-permute-start(bf16[41,16,128]{2,1,0:T(8,128)(2,1)S(1)} %collective-permute-done.8.rest_3_), channel_id=1, source_target_pairs={{0,4},{4,0},{1,5},{5,1},{2,6},{6,2},{3,7},{7,3},{8,12},{12,8},{9,1... | collective-permute-start | bytes 503816 | tf_op jit(solution)/shard_map/ppermute | solution.py:416
  35.4 4.7 %collective-permute-start.12 = (f32[2,16,56,128]{3,2,1,0:T(8,128)S(1)}, f32[2,16,56,128]{3,2,1,0:T(8,128)S(1)}, u32[]{:S(2)}, u32[]{:S(2)}) collective-permute-start(f32[2,16,56,128]{3,2,1,0:T(8,128)S(1)} %get-tuple-element.51), channel_id=1, source_target_pairs={{0,4},{4,0},{1,5},{5,1},{2,6},{6,2},{3,7},{7,3},{8,12},{12,8},{9,1... | collective-permute-start | bytes 2752520 | tf_op jit(solution)/shard_map/ppermute | solution.py:416
  38.2 1.9 %collective-permute-start.11 = (bf16[2,16,56,128]{3,2,1,0:T(8,128)(2,1)S(1)}, bf16[2,16,56,128]{3,2,1,0:T(8,128)(2,1)S(1)}, u32[]{:S(2)}, u32[]{:S(2)}) collective-permute-start(bf16[2,16,56,128]{3,2,1,0:T(8,128)(2,1)S(1)} %get-tuple-element.49), channel_id=1, source_target_pairs={{0,4},{4,0},{1,5},{5,1},{2,6},{6,2},{3,7},{7,3},{8,12},{12,8},{9,1... | collective-permute-start | bytes 1376264 | tf_op jit(solution)/shard_map/ppermute | solution.py:416
  60.6 26.7 %copy-start.1 = (f32[1728,128]{1,0:T(8,128)S(1)}, f32[1728,128]{1,0:T(8,128)}, u32[]{:S(2)}) copy-start(f32[1728,128]{1,0:T(8,128)} %refs_3_.3) | copy-start | bytes 2654212
  60.6 26.7 %copy-start.2 = (f32[1728,128]{1,0:T(8,128)S(1)}, f32[1728,128]{1,0:T(8,128)}, u32[]{:S(2)}) copy-start(f32[1728,128]{1,0:T(8,128)} %refs_4_.1) | copy-start | bytes 2654212
  83.1 5.6 %collective-permute-start.13 = (bf16[896,128]{1,0:T(8,128)(2,1)S(1)}, bf16[896,128]{1,0:T(8,128)(2,1)S(1)}, u32[]{:S(2)}, u32[]{:S(2)}) collective-permute-start(bf16[896,128]{1,0:T(8,128)(2,1)S(1)} %bitcast.10), channel_id=1, source_target_pairs={{0,4},{4,0},{1,5},{5,1},{2,6},{6,2},{3,7},{7,3},{8,12},{12,8},{9,1... | collective-permute-start | bytes 688136 | tf_op jit(solution)/shard_map/ppermute | solution.py:416

commit v5 on v4

--- a/solution.py
+++ b/solution.py
@@ -222,9 +222,9 @@
     for index, piece in enumerate(pieces):
         owner_core = core if index < 4 else 1 - core
         rows = pl.ds(pl.multiple_of((quarter ^ (0, 1, 3, 2)[index % 4]) * 16, 16), 16)
-        whole = dp ^ (1 + 2 * owner_core)
+        whole = dp ^ (1 + owner_core)
         taps[pl.ds(whole * 27, 27), rows, :] = piece[0:27]
-        taps[pl.ds((dp ^ 2) * 27 + 13 * owner_core, 14), rows, :] = piece[27:41]
+        taps[pl.ds((dp ^ 3) * 27 + 13 * owner_core, 14), rows, :] = piece[27:41]
     tap_rows = taps[...].reshape(54 * C, C)
 
     weights = layer_weights(tap_rows, 0)
@@ -423,9 +423,9 @@
 
 def over_dp(whole, half):
     whole = lax.ppermute(
-        whole, ("dp", "c"), [(2 * d + c, 2 * (d ^ (1 + 2 * c)) + c) for d in range(4) for c in range(2)]
+        whole, ("dp", "c"), [(2 * d + c, 2 * (d ^ (1 + c)) + c) for d in range(4) for c in range(2)]
     )
-    return whole, exchanged(half, "dp", 4, 2)
+    return whole, exchanged(half, "dp", 4, 3)
 
 
 def per_device(volume, cotangent, master, moment_one, moment_two):

time: 90.6 us -> 90.4 us (level)
  starting transfers between devices: 25.4 us -> 24.2 us
  blocking collectives: 42.7 us -> 43.7 us
    ppermute x12, starting transfers between devices: 13.1 us -> 11.9 us  [exchanged(): return lax.ppermute(cells, axis, [(i, i ^ by) for i in range(count)])]
    all_to_all x1, blocking collectives: 20.3 us -> 21.5 us  [per_device(): plane = lax.all_to_all(spread, ('x', 'gy'), 0, 0)]
  transfers between devices with their start and end apart: 14 -> 14, of which waited for: 8 -> 7; matrix products, arithmetic and copies ran while one was open for 0% -> 0% of each run, Pallas kernels for 4% -> 4%
where the time goes in v5:
time: 90.4 us; the launch traced here: 90.2 us
  blocking collectives  43.7 us (48%)
  starting transfers between devices  24.2 us (27%)
  Pallas kernels  12.2 us (13%)
  waiting for transfers between devices  8.93 us (10%)
    all_to_all x1, blocking collectives, per_device(): plane = lax.all_to_all(spread, ('x', 'gy'), 0, 0)  21.5 us
    ppermute x12, starting transfers between devices, exchanged(): return lax.ppermute(cells, axis, [(i, i ^ by) for i in range(count)])  11.9 us
    all_to_all x1, blocking collectives, per_device(): lax.all_to_all(plane_sum(plane.reshape(16, 4, PIECE, C)), ('dp', 'zl'), 0...  11.6 us
    all_to_all x1, blocking collectives, per_device(): lax.all_to_all(jnp.broadcast_to(column, (16, PIECE, C)), ('x', 'gy'), 0, 0)  10.7 us
    ppermute x1, starting transfers between devices, over_dp(): lax.ppermute(whole, ('dp', 'c'), [(2 * d + c, 2 * (d ^ 1 + c) + c) for d...  7.83 us
    ppermute x12, waiting for transfers between devices, exchanged(): return lax.ppermute(cells, axis, [(i, i ^ by) for i in range(count)])  7.56 us
    pallas_call x1, Pallas kernels, forward(): pl.pallas_call(forward_kernel, out_shape=(jax.ShapeDtypeStruct((SX, SY, S...  5.08 us
    ppermute x1, starting transfers between devices, paired(): return lax.ppermute(cells, axis, pairs + [(j, i) for i, j in pairs])  4.51 us
  transfers between devices with their start and end apart: 14, of which 7 were waited for; matrix products, arithmetic and copies ran while one was open for 0% of the time, Pallas kernels for 4%

profile of v5, /device:TPU:1, one launch (start us, length us, event | category | flops | bytes accessed | tf_op | source)
XLA Modules:
  0.0 90.2 jit_solution(10242192808488907699)
XLA Ops:
  0.6 1.3 %payloads.1 = (bf16[27,16,128]{2,1,0:T(8,128)(2,1)S(1)}, bf16[14,16,128]{2,1,0:T(8,128)(2,1)S(1)}, bf16[4,16,8,128]{3,2,1,0:T(8,128)(2,1)S(1)}, bf16[4,16,8,128]...) custom-call(bf16[4,16,8,128]{3,2,1,0:T(8,128)(2,1)} %bitcast.13, ...), custom_call_target="tpu_custom_call" | custom-call | tf_op jit(solution)/shard_map/payloads/pallas_call | solution.py:127
  1.9 0.0 copy-start
  1.9 7.8 %collective-permute-start = (bf16[27,16,128]{2,1,0:T(8,128)(2,1)S(1)}, bf16[27,16,128]{2,1,0:T(8,128)(2,1)S(1)}, u32[]{:S(2)}, u32[]{:S(2)}) collective-permute-start(bf16[27,16,128]{2,1,0:T(8,128)(2,1)S(1)} %get-tuple-element.33), channel_id=1, source_target_pairs={{0,64},{4,132},{64,0},{68,196},{128,192},{132,4},{192,128},{196,68... | collective-permute-start | bytes 331784 | tf_op jit(solution)/shard_map/ppermute | solution.py:425
  9.8 4.5 %collective-permute-start.2 = (bf16[4,16,8,128]{3,2,1,0:T(8,128)(2,1)S(1)}, bf16[4,16,8,128]{3,2,1,0:T(8,128)(2,1)S(1)}, u32[]{:S(2)}, u32[]{:S(2)}) collective-permute-start(bf16[4,16,8,128]{3,2,1,0:T(8,128)(2,1)S(1)} %get-tuple-element.35), channel_id=1, source_target_pairs={{4,8},{12,16},{20,24},{28,32},{36,40},{44,48},{52,56},{8,4},{16,12... | collective-permute-start | bytes 393224 | tf_op jit(solution)/shard_map/ppermute | solution.py:421
  14.3 1.2 %collective-permute-done.1 = bf16[14,16,128]{2,1,0:T(8,128)(2,1)S(1)} collective-permute-done((bf16[14,16,128]{2,1,0:T(8,128)(2,1)S(1)}, bf16[14,16,128]{2,1,0:T(8,128)(2,1)S(1)}, u32[]{:S(2)}, u32[]{:S(2)}) %collective-permute-start.1) | collective-permute-done | bytes 57376 | tf_op jit(solution)/shard_map/ppermute | solution.py:416
  15.6 1.4 %collective-permute-done.2.far = bf16[4,16,8,128]{3,2,1,0:T(8,128)(2,1)S(1)} collective-permute-done((bf16[4,16,8,128]{3,2,1,0:T(8,128)(2,1)S(1)}, bf16[4,16,8,128]{3,2,1,0:T(8,128)(2,1)S(1)}, u32[]{:S(2)}, u32[]{:S(2)}) %collective-permute-start.2) | collective-permute-done | bytes 131104 | tf_op jit(solution)/shard_map/ppermute | solution.py:421
  16.9 0.1 relay.1
  17.0 1.4 %collective-permute-start.3 = (bf16[54,16,128]{2,1,0:T(8,128)(2,1)S(1)}, bf16[54,16,128]{2,1,0:T(8,128)(2,1)S(1)}, u32[]{:S(2)}, u32[]{:S(2)}) collective-permute-start(bf16[54,16,128]{2,1,0:T(8,128)(2,1)S(1)} %get-tuple-element.36), channel_id=1, source_target_pairs={{0,1},{1,0},{2,3},{3,2},{4,5},{5,4},{6,7},{7,6},{8,9},{9,8},{10,11... | collective-permute-start | bytes 663560 | tf_op jit(solution)/shard_map/ppermute | solution.py:416
  18.4 1.9 %collective-permute-start.4 = (bf16[54,16,128]{2,1,0:T(8,128)(2,1)S(1)}, bf16[54,16,128]{2,1,0:T(8,128)(2,1)S(1)}, u32[]{:S(2)}, u32[]{:S(2)}) collective-permute-start(bf16[54,16,128]{2,1,0:T(8,128)(2,1)S(1)} %get-tuple-element.37), channel_id=1, source_target_pairs={{0,3},{1,2},{2,1},{3,0},{4,7},{5,6},{6,5},{7,4},{8,11},{9,10},{10,... | collective-permute-start | bytes 663560 | tf_op jit(solution)/shard_map/ppermute | solution.py:416
  20.3 2.4 %collective-permute-start.8 = (bf16[41,16,128]{2,1,0:T(8,128)(2,1)S(1)}, bf16[41,16,128]{2,1,0:T(8,128)(2,1)S(1)}, u32[]{:S(2)}, u32[]{:S(2)}) collective-permute-start(bf16[41,16,128]{2,1,0:T(8,128)(2,1)S(1)} %constant_dynamic-update-slice_fusion.stack.rest_0_), channel_id=1, source_target_pairs={{0,8},{8,0},{16,24},{24,16},{1,9},{9,1},{17,25},{25,17},{2,10},{10... | collective-permute-start | bytes 503816 | tf_op jit(solution)/shard_map/ppermute | solution.py:416
  22.7 0.9 %collective-permute-done.3.even.rest_1_ = bf16[54,16,128]{2,1,0:T(8,128)(2,1)S(1)} collective-permute-done((bf16[54,16,128]{2,1,0:T(8,128)(2,1)S(1)}, bf16[54,16,128]{2,1,0:T(8,128)(2,1)S(1)}, u32[]{:S(2)}, u32[]{:S(2)}) %collective-permute-start.3) | collective-permute-done | bytes 221216 | tf_op jit(solution)/shard_map/ppermute | solution.py:416
  23.6 2.5 %collective-permute-done.4.odd.rest_2_ = bf16[54,16,128]{2,1,0:T(8,128)(2,1)S(1)} collective-permute-done((bf16[54,16,128]{2,1,0:T(8,128)(2,1)S(1)}, bf16[54,16,128]{2,1,0:T(8,128)(2,1)S(1)}, u32[]{:S(2)}, u32[]{:S(2)}) %collective-permute-start.4) | collective-permute-done | bytes 221216 | tf_op jit(solution)/shard_map/ppermute | solution.py:416
  26.1 0.1 collective-permute-start.6
  26.2 0.4 collective-permute-start.7
  26.6 0.1 collective-permute-start.9
  26.7 0.6 collective-permute-done.8.rest_3_
  27.3 0.6 collective-permute-start.10
  27.9 0.4 prepare.1
  28.4 0.6 collective-permute-done.10.rest_7_
  29.0 5.1 %forward.1 = (bf16[4,16,8,128]{3,2,1,0:T(8,128)(2,1)}, bf16[864,384]{1,0:T(8,128)(2,1)S(1)}, f32[4,16,8,128]{3,2,1,0:T(8,128)S(1)}, bf16[1152,384]{1,0:T(8,128)(...) custom-call(bf16[1760,384]{1,0:T(8,128)(2,1)S(1)} %get-tuple-element.42.field, ...), custom_call_target="tpu_custom_call" | custom-call | flops 2500000000 | bytes 8000000 | tf_op jit(solution)/shard_map/forward/pallas_call | solution.py:275
  34.0 0.6 collective-permute-start.12
  34.7 2.2 %backward.1 = (bf16[2,16,56,128]{3,2,1,0:T(8,128)(2,1)S(1)}, f32[2,16,56,128]{3,2,1,0:T(8,128)S(1)}) custom-call(bf16[1760,384]{1,0:T(8,128)(2,1)S(1)} %get-tuple-element.42.field, bf16[864,384]{1,0:T(8,128)(2,1)S(1)} %get-tuple-element.45.dlt, f32[4,16,8,128]{3,2,1,0:T(8,128)S(1)} %get-tuple-element.46.slope, bf16[1152,384]{1,0:T(8,128)(2,1)S(1)} %get-tuple-element.47.flipped), custom_call_target="tpu_custom_call" | custom-call | flops 8000000000 | bytes 8000000 | tf_op jit(solution)/shard_map/backward/pallas_call | solution.py:300
  36.9 0.2 collective-permute-start.11
  37.1 1.7 %collective-permute-done.11.got_one = bf16[2,16,56,128]{3,2,1,0:T(8,128)(2,1)S(1)} collective-permute-done((bf16[2,16,56,128]{3,2,1,0:T(8,128)(2,1)S(1)}, bf16[2,16,56,128]{3,2,1,0:T(8,128)(2,1)S(1)}, u32[]{:S(2)}, u32[]{:S(2)}) %collective-permute-start.11) | collective-permute-done | bytes 458784 | tf_op jit(solution)/shard_map/ppermute | solution.py:416
  38.8 0.2 pair_sum.1
  39.0 21.5 %all_to_all.15 = bf16[16,224,128]{2,1,0:T(8,128)(2,1)S(1)} all-to-all(bf16[16,224,128]{2,1,0:T(8,128)(2,1)S(1)} %bitcast.9), channel_id=1, replica_groups=mesh['dp'=4,'zl'=2,'x'=4,'c'=2,'gy'=4] {'x','gy'}, dimensions={0} | all-to-all | bytes 1835008 | tf_op jit(solution)/shard_map/all_to_all | solution.py:454
  60.5 0.1 plane_sum.1
  60.6 11.6 %all_to_all.16 = bf16[8,56,128]{2,1,0:T(8,128)(2,1)S(1)} all-to-all(bf16[8,56,128]{2,1,0:T(8,128)(2,1)S(1)} %plane_sum.1), channel_id=1, replica_groups=mesh['dp'=4,'zl'=2,'x'=4,'c'=2,'gy'=4] {'dp','zl'}, dimensions={0} | all-to-all | bytes 229376 | tf_op jit(solution)/shard_map/all_to_all | solution.py:455
  72.2 10.7 %all_to_all.17 = bf16[16,56,128]{2,1,0:T(8,128)(2,1)S(1)} all-to-all(bf16[16,56,128]{2,1,0:T(8,128)(2,1)S(1)} %broadcast_in_dim.7), channel_id=1, replica_groups=mesh['dp'=4,'zl'=2,'x'=4,'c'=2,'gy'=4] {'x','gy'}, dimensions={0} | all-to-all | bytes 458752 | tf_op jit(solution)/shard_map/all_to_all | solution.py:457
  82.9 4.2 %collective-permute-start.13 = (bf16[896,128]{1,0:T(8,128)(2,1)S(1)}, bf16[896,128]{1,0:T(8,128)(2,1)S(1)}, u32[]{:S(2)}, u32[]{:S(2)}) collective-permute-start(bf16[896,128]{1,0:T(8,128)(2,1)S(1)} %bitcast.10), channel_id=1, source_target_pairs={{0,4},{4,0},{1,5},{5,1},{2,6},{6,2},{3,7},{7,3},{8,12},{12,8},{9,1... | collective-permute-start | bytes 688136 | tf_op jit(solution)/shard_map/ppermute | solution.py:416
  87.1 1.4 %adam_own.1 = (f32[1728,128]{1,0:T(8,128)}, f32[1728,128]{1,0:T(8,128)}, f32[1728,128]{1,0:T(8,128)}) custom-call(bf16[896,128]{1,0:T(8,128)(2,1)S(1)} %bitcast.11, f32[1728,128]{1,0:T(8,128)S(1)} %copy-done, f32[1728,128]{1,0:T(8,128)S(1)} %copy-done.1, f32[1728,128]{1,0:T(8,128)S(1)} %copy-done.2), custom_call_target="tpu_custom_call" | custom-call | flops 3000000 | bytes 4000000 | tf_op jit(solution)/shard_map/adam_own/pallas_call | solution.py:395
  88.5 1.5 %adam_rest.1 = (f32[1728,128]{1,0:T(8,128)}, f32[1728,128]{1,0:T(8,128)}, f32[1728,128]{1,0:T(8,128)}) custom-call(bf16[896,128]{1,0:T(8,128)(2,1)S(1)} %bitcast.12, bf16[896,128]{1,0:T(8,128)(2,1)S(1)} %collective-permute-done.13.refs_1_, f32[1728,128]{1,0:T(8,128)S(1)} %copy-done, ...), custom_call_target="tpu_custom_call", output_to_operand_aliasing={{0}: (5, {}), {1}: (6, {}), {2}: (7, {})} | custom-call | flops 3000000 | bytes 4000000 | tf_op jit(solution)/shard_map/adam_rest/pallas_call | solution.py:395
  (18 shorter events, 0.1 us)
Async XLA Ops:
  1.9 27.0 %copy-start = (f32[1728,128]{1,0:T(8,128)S(1)}, f32[1728,128]{1,0:T(8,128)}, u32[]{:S(2)}) copy-start(f32[1728,128]{1,0:T(8,128)} %refs_2_.3) | copy-start | bytes 2654212
  1.9 12.3 %collective-permute-start = (bf16[27,16,128]{2,1,0:T(8,128)(2,1)S(1)}, bf16[27,16,128]{2,1,0:T(8,128)(2,1)S(1)}, u32[]{:S(2)}, u32[]{:S(2)}) collective-permute-start(bf16[27,16,128]{2,1,0:T(8,128)(2,1)S(1)} %get-tuple-element.33), channel_id=1, source_target_pairs={{0,64},{4,132},{64,0},{68,196},{128,192},{132,4},{192,128},{196,68... | collective-permute-start | bytes 331784 | tf_op jit(solution)/shard_map/ppermute | solution.py:425
  9.8 5.8 %collective-permute-start.1 = (bf16[14,16,128]{2,1,0:T(8,128)(2,1)S(1)}, bf16[14,16,128]{2,1,0:T(8,128)(2,1)S(1)}, u32[]{:S(2)}, u32[]{:S(2)}) collective-permute-start(bf16[14,16,128]{2,1,0:T(8,128)(2,1)S(1)} %get-tuple-element.34), channel_id=1, source_target_pairs={{0,192},{64,128},{128,64},{192,0},{1,193},{65,129},{129,65},{193,1... | collective-permute-start | bytes 172040 | tf_op jit(solution)/shard_map/ppermute | solution.py:416
  9.8 7.2 %collective-permute-start.2 = (bf16[4,16,8,128]{3,2,1,0:T(8,128)(2,1)S(1)}, bf16[4,16,8,128]{3,2,1,0:T(8,128)(2,1)S(1)}, u32[]{:S(2)}, u32[]{:S(2)}) collective-permute-start(bf16[4,16,8,128]{3,2,1,0:T(8,128)(2,1)S(1)} %get-tuple-element.35), channel_id=1, source_target_pairs={{4,8},{12,16},{20,24},{28,32},{36,40},{44,48},{52,56},{8,4},{16,12... | collective-permute-start | bytes 393224 | tf_op jit(solution)/shard_map/ppermute | solution.py:421
  17.0 6.6 %collective-permute-start.3 = (bf16[54,16,128]{2,1,0:T(8,128)(2,1)S(1)}, bf16[54,16,128]{2,1,0:T(8,128)(2,1)S(1)}, u32[]{:S(2)}, u32[]{:S(2)}) collective-permute-start(bf16[54,16,128]{2,1,0:T(8,128)(2,1)S(1)} %get-tuple-element.36), channel_id=1, source_target_pairs={{0,1},{1,0},{2,3},{3,2},{4,5},{5,4},{6,7},{7,6},{8,9},{9,8},{10,11... | collective-permute-start | bytes 663560 | tf_op jit(solution)/shard_map/ppermute | solution.py:416
  18.4 7.7 %collective-permute-start.4 = (bf16[54,16,128]{2,1,0:T(8,128)(2,1)S(1)}, bf16[54,16,128]{2,1,0:T(8,128)(2,1)S(1)}, u32[]{:S(2)}, u32[]{:S(2)}) collective-permute-start(bf16[54,16,128]{2,1,0:T(8,128)(2,1)S(1)} %get-tuple-element.37), channel_id=1, source_target_pairs={{0,3},{1,2},{2,1},{3,0},{4,7},{5,6},{6,5},{7,4},{8,11},{9,10},{10,... | collective-permute-start | bytes 663560 | tf_op jit(solution)/shard_map/ppermute | solution.py:416
  20.3 2.4 %collective-permute-start.5 = (bf16[4,16,8,128]{3,2,1,0:T(8,128)(2,1)S(1)}, bf16[4,16,8,128]{3,2,1,0:T(8,128)(2,1)S(1)}, u32[]{:S(2)}, u32[]{:S(2)}) collective-permute-start(bf16[4,16,8,128]{3,2,1,0:T(8,128)(2,1)S(1)} %get-tuple-element.38), channel_id=1, source_target_pairs={{0,4},{4,0},{1,5},{5,1},{2,6},{6,2},{3,7},{7,3},{8,12},{12,8},{9,1... | collective-permute-start | bytes 393224 | tf_op jit(solution)/shard_map/ppermute | solution.py:416
  20.3 7.1 %collective-permute-start.8 = (bf16[41,16,128]{2,1,0:T(8,128)(2,1)S(1)}, bf16[41,16,128]{2,1,0:T(8,128)(2,1)S(1)}, u32[]{:S(2)}, u32[]{:S(2)}) collective-permute-start(bf16[41,16,128]{2,1,0:T(8,128)(2,1)S(1)} %constant_dynamic-update-slice_fusion.stack.rest_0_), channel_id=1, source_target_pairs={{0,8},{8,0},{16,24},{24,16},{1,9},{9,1},{17,25},{25,17},{2,10},{10... | collective-permute-start | bytes 503816 | tf_op jit(solution)/shard_map/ppermute | solution.py:416
  26.1 1.8 %collective-permute-start.6 = (bf16[54,16,128]{2,1,0:T(8,128)(2,1)S(1)}, bf16[54,16,128]{2,1,0:T(8,128)(2,1)S(1)}, u32[]{:S(2)}, u32[]{:S(2)}) collective-permute-start(bf16[54,16,128]{2,1,0:T(8,128)(2,1)S(1)} %collective-permute-done.3.even.rest_1_), channel_id=1, source_target_pairs={{0,4},{4,0},{1,5},{5,1},{2,6},{6,2},{3,7},{7,3},{8,12},{12,8},{9,1... | collective-permute-start | bytes 663560 | tf_op jit(solution)/shard_map/ppermute | solution.py:416
  26.2 1.7 %collective-permute-start.7 = (bf16[54,16,128]{2,1,0:T(8,128)(2,1)S(1)}, bf16[54,16,128]{2,1,0:T(8,128)(2,1)S(1)}, u32[]{:S(2)}, u32[]{:S(2)}) collective-permute-start(bf16[54,16,128]{2,1,0:T(8,128)(2,1)S(1)} %collective-permute-done.4.odd.rest_2_), channel_id=1, source_target_pairs={{0,4},{4,0},{1,5},{5,1},{2,6},{6,2},{3,7},{7,3},{8,12},{12,8},{9,1... | collective-permute-start | bytes 663560 | tf_op jit(solution)/shard_map/ppermute | solution.py:416
  26.6 1.7 %collective-permute-start.9 = (bf16[41,16,128]{2,1,0:T(8,128)(2,1)S(1)}, bf16[41,16,128]{2,1,0:T(8,128)(2,1)S(1)}, u32[]{:S(2)}, u32[]{:S(2)}) collective-permute-start(bf16[41,16,128]{2,1,0:T(8,128)(2,1)S(1)} %constant_dynamic-update-slice_fusion.stack.rest_0_), channel_id=1, source_target_pairs={{0,4},{4,0},{1,5},{5,1},{2,6},{6,2},{3,7},{7,3},{8,12},{12,8},{9,1... | collective-permute-start | bytes 503816 | tf_op jit(solution)/shard_map/ppermute | solution.py:416
  27.3 1.6 %collective-permute-start.10 = (bf16[41,16,128]{2,1,0:T(8,128)(2,1)S(1)}, bf16[41,16,128]{2,1,0:T(8,128)(2,1)S(1)}, u32[]{:S(2)}, u32[]{:S(2)}) collective-permute-start(bf16[41,16,128]{2,1,0:T(8,128)(2,1)S(1)} %collective-permute-done.8.rest_3_), channel_id=1, source_target_pairs={{0,4},{4,0},{1,5},{5,1},{2,6},{6,2},{3,7},{7,3},{8,12},{12,8},{9,1... | collective-permute-start | bytes 503816 | tf_op jit(solution)/shard_map/ppermute | solution.py:416
  34.0 4.8 %collective-permute-start.12 = (f32[2,16,56,128]{3,2,1,0:T(8,128)S(1)}, f32[2,16,56,128]{3,2,1,0:T(8,128)S(1)}, u32[]{:S(2)}, u32[]{:S(2)}) collective-permute-start(f32[2,16,56,128]{3,2,1,0:T(8,128)S(1)} %get-tuple-element.51), channel_id=1, source_target_pairs={{0,4},{4,0},{1,5},{5,1},{2,6},{6,2},{3,7},{7,3},{8,12},{12,8},{9,1... | collective-permute-start | bytes 2752520 | tf_op jit(solution)/shard_map/ppermute | solution.py:416
  36.9 1.9 %collective-permute-start.11 = (bf16[2,16,56,128]{3,2,1,0:T(8,128)(2,1)S(1)}, bf16[2,16,56,128]{3,2,1,0:T(8,128)(2,1)S(1)}, u32[]{:S(2)}, u32[]{:S(2)}) collective-permute-start(bf16[2,16,56,128]{3,2,1,0:T(8,128)(2,1)S(1)} %get-tuple-element.49), channel_id=1, source_target_pairs={{0,4},{4,0},{1,5},{5,1},{2,6},{6,2},{3,7},{7,3},{8,12},{12,8},{9,1... | collective-permute-start | bytes 1376264 | tf_op jit(solution)/shard_map/ppermute | solution.py:416
  60.5 26.6 %copy-start.1 = (f32[1728,128]{1,0:T(8,128)S(1)}, f32[1728,128]{1,0:T(8,128)}, u32[]{:S(2)}) copy-start(f32[1728,128]{1,0:T(8,128)} %refs_3_.3) | copy-start | bytes 2654212
  60.5 26.6 %copy-start.2 = (f32[1728,128]{1,0:T(8,128)S(1)}, f32[1728,128]{1,0:T(8,128)}, u32[]{:S(2)}) copy-start(f32[1728,128]{1,0:T(8,128)} %refs_4_.1) | copy-start | bytes 2654212
  82.9 5.6 %collective-permute-start.13 = (bf16[896,128]{1,0:T(8,128)(2,1)S(1)}, bf16[896,128]{1,0:T(8,128)(2,1)S(1)}, u32[]{:S(2)}, u32[]{:S(2)}) collective-permute-start(bf16[896,128]{1,0:T(8,128)(2,1)S(1)} %bitcast.10), channel_id=1, source_target_pairs={{0,4},{4,0},{1,5},{5,1},{2,6},{6,2},{3,7},{7,3},{8,12},{12,8},{9,1... | collective-permute-start | bytes 688136 | tf_op jit(solution)/shard_map/ppermute | solution.py:416

commit v6 on v5

--- a/solution.py
+++ b/solution.py
@@ -428,6 +428,39 @@
     return whole, exchanged(half, "dp", 4, 3)
 
 
+QUAD = ((0, 0), (1, 0), (0, 1), (1, 1))
+
+
+def quad(part, by):
+    return [
+        lax.ppermute(
+            part,
+            ("x", "gy"),
+            [(4 * i + j, 4 * (i ^ (by * ex)) + (j ^ (by * ey))) for i in range(4) for j in range(4)],
+        )
+        for ex, ey in QUAD[1:]
+    ]
+
+
+def order_kernel(*refs):
+    x, gy = lax.axis_index("x"), lax.axis_index("gy")
+    for ref, (fx, fy) in zip(refs[:4], QUAD):
+        for slot, (ex, ey) in enumerate(QUAD):
+            refs[4][4 * (x ^ (3 * fx) ^ ex) + (gy ^ (3 * fy) ^ ey)] = ref[slot]
+
+
+def ordered_pieces(parts):
+    vmem = pl.BlockSpec(memory_space=pltpu.VMEM)
+    return pl.pallas_call(
+        order_kernel,
+        out_shape=jax.ShapeDtypeStruct((16, PIECE, C), BF),
+        in_specs=[vmem] * 4,
+        out_specs=vmem,
+        compiler_params=pltpu.CompilerParams(vmem_limit_bytes=8 * 2**20),
+        name="ordered_pieces",
+    )(*parts)
+
+
 def per_device(volume, cotangent, master, moment_one, moment_two):
     vol, cot = volume[0], cotangent[0]
     whole, half, near, far, vol, cot = payloads(vol, cot, master)
@@ -454,7 +487,8 @@
     plane = lax.all_to_all(spread, ("x", "gy"), 0, 0)
     column = lax.all_to_all(plane_sum(plane.reshape(16, 4, PIECE, C)), ("dp", "zl"), 0, 0)
     column = jnp.sum(column.astype(F32), axis=0).astype(BF)
-    mine = lax.all_to_all(jnp.broadcast_to(column, (16, PIECE, C)), ("x", "gy"), 0, 0).reshape(HALF, C)
+    one = jnp.stack([column] + quad(column, 1))
+    mine = ordered_pieces([one] + quad(one, 3)).reshape(HALF, C)
     other = exchanged(mine, "c", 2, 1)
     state = (master, moment_one, moment_two)
     held = adam_step(True, (mine,), state)

time: 90.4 us -> 94 us (1.040)
  blocking collectives: 43.7 us -> 33.1 us
  starting transfers between devices: 24.2 us -> 34.4 us
  waiting for transfers between devices: 8.93 us -> 13.1 us
    all_to_all x1 -> x0, blocking collectives: 10.7 us -> none  [per_device(): lax.all_to_all(jnp.broadcast_to(column, (16, PIECE, C)), ('x', 'gy'), 0, 0)]
    ppermute x0 -> x6, starting transfers between devices: none -> 7.88 us  [quad(): lax.ppermute(part, ('x', 'gy'), [(4 * i + j, 4 * (i ^ by * ex) + (j ^ by...]
    ppermute x0 -> x6, waiting for transfers between devices: none -> 4.13 us  [quad(): lax.ppermute(part, ('x', 'gy'), [(4 * i + j, 4 * (i ^ by * ex) + (j ^ by...]
    ppermute x12, starting transfers between devices: 11.9 us -> 14.2 us  [exchanged(): return lax.ppermute(cells, axis, [(i, i ^ by) for i in range(count)])]
  transfers between devices with their start and end apart: 14 -> 20, of which waited for: 7 -> 12; matrix products, arithmetic and copies ran while one was open for 0% -> 0% of each run, Pallas kernels for 4% -> 4%
where the time goes in v6:
time: 94 us; the launch traced here: 93.8 us
  starting transfers between devices  34.4 us (37%)
  blocking collectives  33.1 us (35%)
  waiting for transfers between devices  13.1 us (14%)
  Pallas kernels  12.3 us (13%)
    all_to_all x1, blocking collectives, per_device(): plane = lax.all_to_all(spread, ('x', 'gy'), 0, 0)  21.5 us
    ppermute x12, starting transfers between devices, exchanged(): return lax.ppermute(cells, axis, [(i, i ^ by) for i in range(count)])  14.2 us
    all_to_all x1, blocking collectives, per_device(): lax.all_to_all(plane_sum(plane.reshape(16, 4, PIECE, C)), ('dp', 'zl'), 0...  11.6 us
    ppermute x6, starting transfers between devices, quad(): lax.ppermute(part, ('x', 'gy'), [(4 * i + j, 4 * (i ^ by * ex) + (j ^ by...  7.88 us
    ppermute x1, starting transfers between devices, over_dp(): lax.ppermute(whole, ('dp', 'c'), [(2 * d + c, 2 * (d ^ 1 + c) + c) for d...  7.83 us
    ppermute x12, waiting for transfers between devices, exchanged(): return lax.ppermute(cells, axis, [(i, i ^ by) for i in range(count)])  7.56 us
    pallas_call x1, Pallas kernels, forward(): pl.pallas_call(forward_kernel, out_shape=(jax.ShapeDtypeStruct((SX, SY, S...  5.08 us
    ppermute x1, starting transfers between devices, paired(): return lax.ppermute(cells, axis, pairs + [(j, i) for i, j in pairs])  4.51 us
  transfers between devices with their start and end apart: 20, of which 12 were waited for; matrix products, arithmetic and copies ran while one was open for 0% of the time, Pallas kernels for 4%

profile of v6, /device:TPU:1, one launch (start us, length us, event | category | flops | bytes accessed | tf_op | source)
XLA Modules:
  0.0 93.8 jit_solution(13522950772549545564)
XLA Ops:
  0.6 1.3 %payloads.1 = (bf16[27,16,128]{2,1,0:T(8,128)(2,1)S(1)}, bf16[14,16,128]{2,1,0:T(8,128)(2,1)S(1)}, bf16[4,16,8,128]{3,2,1,0:T(8,128)(2,1)S(1)}, bf16[4,16,8,128]...) custom-call(bf16[4,16,8,128]{3,2,1,0:T(8,128)(2,1)} %bitcast.17, ...), custom_call_target="tpu_custom_call" | custom-call | tf_op jit(solution)/shard_map/payloads/pallas_call | solution.py:127
  1.9 7.8 %collective-permute-start = (bf16[27,16,128]{2,1,0:T(8,128)(2,1)S(1)}, bf16[27,16,128]{2,1,0:T(8,128)(2,1)S(1)}, u32[]{:S(2)}, u32[]{:S(2)}) collective-permute-start(bf16[27,16,128]{2,1,0:T(8,128)(2,1)S(1)} %get-tuple-element.33), channel_id=1, source_target_pairs={{0,64},{4,132},{64,0},{68,196},{128,192},{132,4},{192,128},{196,68... | collective-permute-start | bytes 331784 | tf_op jit(solution)/shard_map/ppermute | solution.py:425
  9.8 4.5 %collective-permute-start.2 = (bf16[4,16,8,128]{3,2,1,0:T(8,128)(2,1)S(1)}, bf16[4,16,8,128]{3,2,1,0:T(8,128)(2,1)S(1)}, u32[]{:S(2)}, u32[]{:S(2)}) collective-permute-start(bf16[4,16,8,128]{3,2,1,0:T(8,128)(2,1)S(1)} %get-tuple-element.35), channel_id=1, source_target_pairs={{4,8},{12,16},{20,24},{28,32},{36,40},{44,48},{52,56},{8,4},{16,12... | collective-permute-start | bytes 393224 | tf_op jit(solution)/shard_map/ppermute | solution.py:421
  14.3 1.2 %collective-permute-done.1 = bf16[14,16,128]{2,1,0:T(8,128)(2,1)S(1)} collective-permute-done((bf16[14,16,128]{2,1,0:T(8,128)(2,1)S(1)}, bf16[14,16,128]{2,1,0:T(8,128)(2,1)S(1)}, u32[]{:S(2)}, u32[]{:S(2)}) %collective-permute-start.1) | collective-permute-done | bytes 57376 | tf_op jit(solution)/shard_map/ppermute | solution.py:416
  15.6 1.4 %collective-permute-done.2.far = bf16[4,16,8,128]{3,2,1,0:T(8,128)(2,1)S(1)} collective-permute-done((bf16[4,16,8,128]{3,2,1,0:T(8,128)(2,1)S(1)}, bf16[4,16,8,128]{3,2,1,0:T(8,128)(2,1)S(1)}, u32[]{:S(2)}, u32[]{:S(2)}) %collective-permute-start.2) | collective-permute-done | bytes 131104 | tf_op jit(solution)/shard_map/ppermute | solution.py:421
  17.0 1.4 %collective-permute-start.3 = (bf16[54,16,128]{2,1,0:T(8,128)(2,1)S(1)}, bf16[54,16,128]{2,1,0:T(8,128)(2,1)S(1)}, u32[]{:S(2)}, u32[]{:S(2)}) collective-permute-start(bf16[54,16,128]{2,1,0:T(8,128)(2,1)S(1)} %get-tuple-element.36), channel_id=1, source_target_pairs={{0,1},{1,0},{2,3},{3,2},{4,5},{5,4},{6,7},{7,6},{8,9},{9,8},{10,11... | collective-permute-start | bytes 663560 | tf_op jit(solution)/shard_map/ppermute | solution.py:416
  18.4 1.9 %collective-permute-start.4 = (bf16[54,16,128]{2,1,0:T(8,128)(2,1)S(1)}, bf16[54,16,128]{2,1,0:T(8,128)(2,1)S(1)}, u32[]{:S(2)}, u32[]{:S(2)}) collective-permute-start(bf16[54,16,128]{2,1,0:T(8,128)(2,1)S(1)} %get-tuple-element.37), channel_id=1, source_target_pairs={{0,3},{1,2},{2,1},{3,0},{4,7},{5,6},{6,5},{7,4},{8,11},{9,10},{10,... | collective-permute-start | bytes 663560 | tf_op jit(solution)/shard_map/ppermute | solution.py:416
  20.3 2.4 %collective-permute-start.8 = (bf16[41,16,128]{2,1,0:T(8,128)(2,1)S(1)}, bf16[41,16,128]{2,1,0:T(8,128)(2,1)S(1)}, u32[]{:S(2)}, u32[]{:S(2)}) collective-permute-start(bf16[41,16,128]{2,1,0:T(8,128)(2,1)S(1)} %constant_dynamic-update-slice_fusion.stack.rest_0_), channel_id=1, source_target_pairs={{0,8},{8,0},{16,24},{24,16},{1,9},{9,1},{17,25},{25,17},{2,10},{10... | collective-permute-start | bytes 503816 | tf_op jit(solution)/shard_map/ppermute | solution.py:416
  22.7 0.9 collective-permute-done.3.even.rest_1_
  23.6 2.5 %collective-permute-done.4.odd.rest_2_ = bf16[54,16,128]{2,1,0:T(8,128)(2,1)S(1)} collective-permute-done((bf16[54,16,128]{2,1,0:T(8,128)(2,1)S(1)}, bf16[54,16,128]{2,1,0:T(8,128)(2,1)S(1)}, u32[]{:S(2)}, u32[]{:S(2)}) %collective-permute-start.4) | collective-permute-done | bytes 221216 | tf_op jit(solution)/shard_map/ppermute | solution.py:416
  26.7 0.6 collective-permute-done.8.rest_3_
  27.3 0.6 collective-permute-start.10
  27.9 0.4 prepare.1
  28.4 0.6 collective-permute-done.10.rest_7_
  29.0 5.1 %forward.1 = (bf16[4,16,8,128]{3,2,1,0:T(8,128)(2,1)}, bf16[864,384]{1,0:T(8,128)(2,1)S(1)}, f32[4,16,8,128]{3,2,1,0:T(8,128)S(1)}, bf16[1152,384]{1,0:T(8,128)(...) custom-call(bf16[1760,384]{1,0:T(8,128)(2,1)S(1)} %get-tuple-element.42.field, ...), custom_call_target="tpu_custom_call" | custom-call | flops 2500000000 | bytes 8000000 | tf_op jit(solution)/shard_map/forward/pallas_call | solution.py:275
  34.0 0.6 collective-permute-start.12
  34.7 2.2 %backward.1 = (bf16[2,16,56,128]{3,2,1,0:T(8,128)(2,1)S(1)}, f32[2,16,56,128]{3,2,1,0:T(8,128)S(1)}) custom-call(bf16[1760,384]{1,0:T(8,128)(2,1)S(1)} %get-tuple-element.42.field, bf16[864,384]{1,0:T(8,128)(2,1)S(1)} %get-tuple-element.45.dlt, f32[4,16,8,128]{3,2,1,0:T(8,128)S(1)} %get-tuple-element.46.slope, bf16[1152,384]{1,0:T(8,128)(2,1)S(1)} %get-tuple-element.47.flipped), custom_call_target="tpu_custom_call" | custom-call | flops 8000000000 | bytes 8000000 | tf_op jit(solution)/shard_map/backward/pallas_call | solution.py:300
  37.1 1.7 %collective-permute-done.11.got_one = bf16[2,16,56,128]{3,2,1,0:T(8,128)(2,1)S(1)} collective-permute-done((bf16[2,16,56,128]{3,2,1,0:T(8,128)(2,1)S(1)}, bf16[2,16,56,128]{3,2,1,0:T(8,128)(2,1)S(1)}, u32[]{:S(2)}, u32[]{:S(2)}) %collective-permute-start.11) | collective-permute-done | bytes 458784 | tf_op jit(solution)/shard_map/ppermute | solution.py:416
  39.0 21.5 %all_to_all.10 = bf16[16,224,128]{2,1,0:T(8,128)(2,1)S(1)} all-to-all(bf16[16,224,128]{2,1,0:T(8,128)(2,1)S(1)} %bitcast.13), channel_id=1, replica_groups=mesh['dp'=4,'zl'=2,'x'=4,'c'=2,'gy'=4] {'x','gy'}, dimensions={0} | all-to-all | bytes 1835008 | tf_op jit(solution)/shard_map/all_to_all | solution.py:487
  60.6 11.6 %all_to_all.11 = bf16[8,56,128]{2,1,0:T(8,128)(2,1)S(1)} all-to-all(bf16[8,56,128]{2,1,0:T(8,128)(2,1)S(1)} %plane_sum.1), channel_id=1, replica_groups=mesh['dp'=4,'zl'=2,'x'=4,'c'=2,'gy'=4] {'dp','zl'}, dimensions={0} | all-to-all | bytes 229376 | tf_op jit(solution)/shard_map/all_to_all | solution.py:488
  72.3 0.8 collective-permute-start.14
  73.1 1.8 %collective-permute-start.13 = (bf16[56,128]{1,0:T(8,128)(2,1)S(1)}, bf16[56,128]{1,0:T(8,128)(2,1)S(1)}, u32[]{:S(2)}, u32[]{:S(2)}) collective-permute-start(bf16[56,128]{1,0:T(8,128)(2,1)S(1)} %reduce_sum.12), channel_id=1, source_target_pairs={{0,8},{1,9},{2,10},{3,11},{8,0},{9,1},{10,2},{11,3},{16,24},{17,25... | collective-permute-start | bytes 43016 | tf_op jit(solution)/shard_map/ppermute | solution.py:436
  74.9 0.8 collective-permute-done.15
  76.0 2.1 %collective-permute-start.18 = (bf16[4,56,128]{2,1,0:T(8,128)(2,1)S(1)}, bf16[4,56,128]{2,1,0:T(8,128)(2,1)S(1)}, u32[]{:S(2)}, u32[]{:S(2)}) collective-permute-start(bf16[4,56,128]{2,1,0:T(8,128)(2,1)S(1)} %pad_maximum_fusion.refs_0_), channel_id=1, source_target_pairs={{0,27},{1,26},{2,25},{3,24},{8,19},{9,18},{10,17},{11,16},{16,11},... | collective-permute-start | bytes 172040 | tf_op jit(solution)/shard_map/ppermute | solution.py:436
  78.2 1.8 %collective-permute-start.17 = (bf16[4,56,128]{2,1,0:T(8,128)(2,1)S(1)}, bf16[4,56,128]{2,1,0:T(8,128)(2,1)S(1)}, u32[]{:S(2)}, u32[]{:S(2)}) collective-permute-start(bf16[4,56,128]{2,1,0:T(8,128)(2,1)S(1)} %pad_maximum_fusion.refs_0_), channel_id=1, source_target_pairs={{0,3},{1,2},{2,1},{3,0},{8,11},{9,10},{10,9},{11,8},{16,19},{17,18... | collective-permute-start | bytes 172040 | tf_op jit(solution)/shard_map/ppermute | solution.py:436
  80.0 1.2 %collective-permute-start.16 = (bf16[4,56,128]{2,1,0:T(8,128)(2,1)S(1)}, bf16[4,56,128]{2,1,0:T(8,128)(2,1)S(1)}, u32[]{:S(2)}, u32[]{:S(2)}) collective-permute-start(bf16[4,56,128]{2,1,0:T(8,128)(2,1)S(1)} %pad_maximum_fusion.refs_0_), channel_id=1, source_target_pairs={{0,24},{1,25},{2,26},{3,27},{8,16},{9,17},{10,18},{11,19},{16,8},{... | collective-permute-start | bytes 172040 | tf_op jit(solution)/shard_map/ppermute | solution.py:436
  81.2 1.4 %collective-permute-done.18.refs_3_ = bf16[4,56,128]{2,1,0:T(8,128)(2,1)S(1)} collective-permute-done((bf16[4,56,128]{2,1,0:T(8,128)(2,1)S(1)}, bf16[4,56,128]{2,1,0:T(8,128)(2,1)S(1)}, u32[]{:S(2)}, u32[]{:S(2)}) %collective-permute-start.18) | collective-permute-done | bytes 57376 | tf_op jit(solution)/shard_map/ppermute | solution.py:436
  82.6 0.5 collective-permute-done.17.refs_2_
  83.0 1.2 %collective-permute-done.16.refs_1_ = bf16[4,56,128]{2,1,0:T(8,128)(2,1)S(1)} collective-permute-done((bf16[4,56,128]{2,1,0:T(8,128)(2,1)S(1)}, bf16[4,56,128]{2,1,0:T(8,128)(2,1)S(1)}, u32[]{:S(2)}, u32[]{:S(2)}) %collective-permute-start.16) | collective-permute-done | bytes 57376 | tf_op jit(solution)/shard_map/ppermute | solution.py:436
  84.3 6.5 %collective-permute-start.19 = (bf16[896,128]{1,0:T(8,128)(2,1)S(1)}, bf16[896,128]{1,0:T(8,128)(2,1)S(1)}, u32[]{:S(2)}, u32[]{:S(2)}) collective-permute-start(bf16[896,128]{1,0:T(8,128)(2,1)S(1)} %bitcast.14), channel_id=1, source_target_pairs={{0,4},{4,0},{1,5},{5,1},{2,6},{6,2},{3,7},{7,3},{8,12},{12,8},{9,1... | collective-permute-start | bytes 688136 | tf_op jit(solution)/shard_map/ppermute | solution.py:416
  90.7 1.4 %adam_own.1 = (f32[1728,128]{1,0:T(8,128)}, f32[1728,128]{1,0:T(8,128)}, f32[1728,128]{1,0:T(8,128)}) custom-call(bf16[896,128]{1,0:T(8,128)(2,1)S(1)} %bitcast.15, f32[1728,128]{1,0:T(8,128)S(1)} %copy-done, f32[1728,128]{1,0:T(8,128)S(1)} %copy-done.1, f32[1728,128]{1,0:T(8,128)S(1)} %copy-done.2), custom_call_target="tpu_custom_call" | custom-call | flops 3000000 | bytes 4000000 | tf_op jit(solution)/shard_map/adam_own/pallas_call | solution.py:395
  92.1 1.5 %adam_rest.1 = (f32[1728,128]{1,0:T(8,128)}, f32[1728,128]{1,0:T(8,128)}, f32[1728,128]{1,0:T(8,128)}) custom-call(bf16[896,128]{1,0:T(8,128)(2,1)S(1)} %bitcast.16, bf16[896,128]{1,0:T(8,128)(2,1)S(1)} %collective-permute-done.19.refs_1_, f32[1728,128]{1,0:T(8,128)S(1)} %copy-done, ...), custom_call_target="tpu_custom_call", output_to_operand_aliasing={{0}: (5, {}), {1}: (6, {}), {2}: (7, {})} | custom-call | flops 3000000 | bytes 4000000 | tf_op jit(solution)/shard_map/adam_rest/pallas_call | solution.py:395
  (30 shorter events, 1.7 us)
Async XLA Ops:
  1.9 27.0 %copy-start = (f32[1728,128]{1,0:T(8,128)S(1)}, f32[1728,128]{1,0:T(8,128)}, u32[]{:S(2)}) copy-start(f32[1728,128]{1,0:T(8,128)} %refs_2_.3) | copy-start | bytes 2654212
  1.9 12.3 %collective-permute-start = (bf16[27,16,128]{2,1,0:T(8,128)(2,1)S(1)}, bf16[27,16,128]{2,1,0:T(8,128)(2,1)S(1)}, u32[]{:S(2)}, u32[]{:S(2)}) collective-permute-start(bf16[27,16,128]{2,1,0:T(8,128)(2,1)S(1)} %get-tuple-element.33), channel_id=1, source_target_pairs={{0,64},{4,132},{64,0},{68,196},{128,192},{132,4},{192,128},{196,68... | collective-permute-start | bytes 331784 | tf_op jit(solution)/shard_map/ppermute | solution.py:425
  9.8 5.8 %collective-permute-start.1 = (bf16[14,16,128]{2,1,0:T(8,128)(2,1)S(1)}, bf16[14,16,128]{2,1,0:T(8,128)(2,1)S(1)}, u32[]{:S(2)}, u32[]{:S(2)}) collective-permute-start(bf16[14,16,128]{2,1,0:T(8,128)(2,1)S(1)} %get-tuple-element.34), channel_id=1, source_target_pairs={{0,192},{64,128},{128,64},{192,0},{1,193},{65,129},{129,65},{193,1... | collective-permute-start | bytes 172040 | tf_op jit(solution)/shard_map/ppermute | solution.py:416
  9.8 7.2 %collective-permute-start.2 = (bf16[4,16,8,128]{3,2,1,0:T(8,128)(2,1)S(1)}, bf16[4,16,8,128]{3,2,1,0:T(8,128)(2,1)S(1)}, u32[]{:S(2)}, u32[]{:S(2)}) collective-permute-start(bf16[4,16,8,128]{3,2,1,0:T(8,128)(2,1)S(1)} %get-tuple-element.35), channel_id=1, source_target_pairs={{4,8},{12,16},{20,24},{28,32},{36,40},{44,48},{52,56},{8,4},{16,12... | collective-permute-start | bytes 393224 | tf_op jit(solution)/shard_map/ppermute | solution.py:421
  17.0 6.6 %collective-permute-start.3 = (bf16[54,16,128]{2,1,0:T(8,128)(2,1)S(1)}, bf16[54,16,128]{2,1,0:T(8,128)(2,1)S(1)}, u32[]{:S(2)}, u32[]{:S(2)}) collective-permute-start(bf16[54,16,128]{2,1,0:T(8,128)(2,1)S(1)} %get-tuple-element.36), channel_id=1, source_target_pairs={{0,1},{1,0},{2,3},{3,2},{4,5},{5,4},{6,7},{7,6},{8,9},{9,8},{10,11... | collective-permute-start | bytes 663560 | tf_op jit(solution)/shard_map/ppermute | solution.py:416
  18.4 7.7 %collective-permute-start.4 = (bf16[54,16,128]{2,1,0:T(8,128)(2,1)S(1)}, bf16[54,16,128]{2,1,0:T(8,128)(2,1)S(1)}, u32[]{:S(2)}, u32[]{:S(2)}) collective-permute-start(bf16[54,16,128]{2,1,0:T(8,128)(2,1)S(1)} %get-tuple-element.37), channel_id=1, source_target_pairs={{0,3},{1,2},{2,1},{3,0},{4,7},{5,6},{6,5},{7,4},{8,11},{9,10},{10,... | collective-permute-start | bytes 663560 | tf_op jit(solution)/shard_map/ppermute | solution.py:416
  20.3 2.4 %collective-permute-start.5 = (bf16[4,16,8,128]{3,2,1,0:T(8,128)(2,1)S(1)}, bf16[4,16,8,128]{3,2,1,0:T(8,128)(2,1)S(1)}, u32[]{:S(2)}, u32[]{:S(2)}) collective-permute-start(bf16[4,16,8,128]{3,2,1,0:T(8,128)(2,1)S(1)} %get-tuple-element.38), channel_id=1, source_target_pairs={{0,4},{4,0},{1,5},{5,1},{2,6},{6,2},{3,7},{7,3},{8,12},{12,8},{9,1... | collective-permute-start | bytes 393224 | tf_op jit(solution)/shard_map/ppermute | solution.py:416
  20.3 7.1 %collective-permute-start.8 = (bf16[41,16,128]{2,1,0:T(8,128)(2,1)S(1)}, bf16[41,16,128]{2,1,0:T(8,128)(2,1)S(1)}, u32[]{:S(2)}, u32[]{:S(2)}) collective-permute-start(bf16[41,16,128]{2,1,0:T(8,128)(2,1)S(1)} %constant_dynamic-update-slice_fusion.stack.rest_0_), channel_id=1, source_target_pairs={{0,8},{8,0},{16,24},{24,16},{1,9},{9,1},{17,25},{25,17},{2,10},{10... | collective-permute-start | bytes 503816 | tf_op jit(solution)/shard_map/ppermute | solution.py:416
  26.1 1.8 %collective-permute-start.6 = (bf16[54,16,128]{2,1,0:T(8,128)(2,1)S(1)}, bf16[54,16,128]{2,1,0:T(8,128)(2,1)S(1)}, u32[]{:S(2)}, u32[]{:S(2)}) collective-permute-start(bf16[54,16,128]{2,1,0:T(8,128)(2,1)S(1)} %collective-permute-done.3.even.rest_1_), channel_id=1, source_target_pairs={{0,4},{4,0},{1,5},{5,1},{2,6},{6,2},{3,7},{7,3},{8,12},{12,8},{9,1... | collective-permute-start | bytes 663560 | tf_op jit(solution)/shard_map/ppermute | solution.py:416
  26.2 1.7 %collective-permute-start.7 = (bf16[54,16,128]{2,1,0:T(8,128)(2,1)S(1)}, bf16[54,16,128]{2,1,0:T(8,128)(2,1)S(1)}, u32[]{:S(2)}, u32[]{:S(2)}) collective-permute-start(bf16[54,16,128]{2,1,0:T(8,128)(2,1)S(1)} %collective-permute-done.4.odd.rest_2_), channel_id=1, source_target_pairs={{0,4},{4,0},{1,5},{5,1},{2,6},{6,2},{3,7},{7,3},{8,12},{12,8},{9,1... | collective-permute-start | bytes 663560 | tf_op jit(solution)/shard_map/ppermute | solution.py:416
  26.6 1.7 %collective-permute-start.9 = (bf16[41,16,128]{2,1,0:T(8,128)(2,1)S(1)}, bf16[41,16,128]{2,1,0:T(8,128)(2,1)S(1)}, u32[]{:S(2)}, u32[]{:S(2)}) collective-permute-start(bf16[41,16,128]{2,1,0:T(8,128)(2,1)S(1)} %constant_dynamic-update-slice_fusion.stack.rest_0_), channel_id=1, source_target_pairs={{0,4},{4,0},{1,5},{5,1},{2,6},{6,2},{3,7},{7,3},{8,12},{12,8},{9,1... | collective-permute-start | bytes 503816 | tf_op jit(solution)/shard_map/ppermute | solution.py:416
  27.3 1.6 %collective-permute-start.10 = (bf16[41,16,128]{2,1,0:T(8,128)(2,1)S(1)}, bf16[41,16,128]{2,1,0:T(8,128)(2,1)S(1)}, u32[]{:S(2)}, u32[]{:S(2)}) collective-permute-start(bf16[41,16,128]{2,1,0:T(8,128)(2,1)S(1)} %collective-permute-done.8.rest_3_), channel_id=1, source_target_pairs={{0,4},{4,0},{1,5},{5,1},{2,6},{6,2},{3,7},{7,3},{8,12},{12,8},{9,1... | collective-permute-start | bytes 503816 | tf_op jit(solution)/shard_map/ppermute | solution.py:416
  34.0 4.8 %collective-permute-start.12 = (f32[2,16,56,128]{3,2,1,0:T(8,128)S(1)}, f32[2,16,56,128]{3,2,1,0:T(8,128)S(1)}, u32[]{:S(2)}, u32[]{:S(2)}) collective-permute-start(f32[2,16,56,128]{3,2,1,0:T(8,128)S(1)} %get-tuple-element.51), channel_id=1, source_target_pairs={{0,4},{4,0},{1,5},{5,1},{2,6},{6,2},{3,7},{7,3},{8,12},{12,8},{9,1... | collective-permute-start | bytes 2752520 | tf_op jit(solution)/shard_map/ppermute | solution.py:416
  36.9 1.9 %collective-permute-start.11 = (bf16[2,16,56,128]{3,2,1,0:T(8,128)(2,1)S(1)}, bf16[2,16,56,128]{3,2,1,0:T(8,128)(2,1)S(1)}, u32[]{:S(2)}, u32[]{:S(2)}) collective-permute-start(bf16[2,16,56,128]{3,2,1,0:T(8,128)(2,1)S(1)} %get-tuple-element.49), channel_id=1, source_target_pairs={{0,4},{4,0},{1,5},{5,1},{2,6},{6,2},{3,7},{7,3},{8,12},{12,8},{9,1... | collective-permute-start | bytes 1376264 | tf_op jit(solution)/shard_map/ppermute | solution.py:416
  60.5 30.2 %copy-start.1 = (f32[1728,128]{1,0:T(8,128)S(1)}, f32[1728,128]{1,0:T(8,128)}, u32[]{:S(2)}) copy-start(f32[1728,128]{1,0:T(8,128)} %refs_3_.3) | copy-start | bytes 2654212
  60.5 30.2 %copy-start.2 = (f32[1728,128]{1,0:T(8,128)S(1)}, f32[1728,128]{1,0:T(8,128)}, u32[]{:S(2)}) copy-start(f32[1728,128]{1,0:T(8,128)} %refs_4_.1) | copy-start | bytes 2654212
  72.2 3.6 %collective-permute-start.15 = (bf16[56,128]{1,0:T(8,128)(2,1)S(1)}, bf16[56,128]{1,0:T(8,128)(2,1)S(1)}, u32[]{:S(2)}, u32[]{:S(2)}) collective-permute-start(bf16[56,128]{1,0:T(8,128)(2,1)S(1)} %reduce_sum.12), channel_id=1, source_target_pairs={{0,9},{1,8},{2,11},{3,10},{8,1},{9,0},{10,3},{11,2},{16,25},{17,24... | collective-permute-start | bytes 43016 | tf_op jit(solution)/shard_map/ppermute | solution.py:436
  72.3 3.5 %collective-permute-start.14 = (bf16[56,128]{1,0:T(8,128)(2,1)S(1)}, bf16[56,128]{1,0:T(8,128)(2,1)S(1)}, u32[]{:S(2)}, u32[]{:S(2)}) collective-permute-start(bf16[56,128]{1,0:T(8,128)(2,1)S(1)} %reduce_sum.12), channel_id=1, source_target_pairs={{0,1},{1,0},{2,3},{3,2},{8,9},{9,8},{10,11},{11,10},{16,17},{17,16... | collective-permute-start | bytes 43016 | tf_op jit(solution)/shard_map/ppermute | solution.py:436
  73.1 2.9 %collective-permute-start.13 = (bf16[56,128]{1,0:T(8,128)(2,1)S(1)}, bf16[56,128]{1,0:T(8,128)(2,1)S(1)}, u32[]{:S(2)}, u32[]{:S(2)}) collective-permute-start(bf16[56,128]{1,0:T(8,128)(2,1)S(1)} %reduce_sum.12), channel_id=1, source_target_pairs={{0,8},{1,9},{2,10},{3,11},{8,0},{9,1},{10,2},{11,3},{16,24},{17,25... | collective-permute-start | bytes 43016 | tf_op jit(solution)/shard_map/ppermute | solution.py:436
  76.0 6.5 %collective-permute-start.18 = (bf16[4,56,128]{2,1,0:T(8,128)(2,1)S(1)}, bf16[4,56,128]{2,1,0:T(8,128)(2,1)S(1)}, u32[]{:S(2)}, u32[]{:S(2)}) collective-permute-start(bf16[4,56,128]{2,1,0:T(8,128)(2,1)S(1)} %pad_maximum_fusion.refs_0_), channel_id=1, source_target_pairs={{0,27},{1,26},{2,25},{3,24},{8,19},{9,18},{10,17},{11,16},{16,11},... | collective-permute-start | bytes 172040 | tf_op jit(solution)/shard_map/ppermute | solution.py:436
  78.2 4.9 %collective-permute-start.17 = (bf16[4,56,128]{2,1,0:T(8,128)(2,1)S(1)}, bf16[4,56,128]{2,1,0:T(8,128)(2,1)S(1)}, u32[]{:S(2)}, u32[]{:S(2)}) collective-permute-start(bf16[4,56,128]{2,1,0:T(8,128)(2,1)S(1)} %pad_maximum_fusion.refs_0_), channel_id=1, source_target_pairs={{0,3},{1,2},{2,1},{3,0},{8,11},{9,10},{10,9},{11,8},{16,19},{17,18... | collective-permute-start | bytes 172040 | tf_op jit(solution)/shard_map/ppermute | solution.py:436
  80.0 4.2 %collective-permute-start.16 = (bf16[4,56,128]{2,1,0:T(8,128)(2,1)S(1)}, bf16[4,56,128]{2,1,0:T(8,128)(2,1)S(1)}, u32[]{:S(2)}, u32[]{:S(2)}) collective-permute-start(bf16[4,56,128]{2,1,0:T(8,128)(2,1)S(1)} %pad_maximum_fusion.refs_0_), channel_id=1, source_target_pairs={{0,24},{1,25},{2,26},{3,27},{8,16},{9,17},{10,18},{11,19},{16,8},{... | collective-permute-start | bytes 172040 | tf_op jit(solution)/shard_map/ppermute | solution.py:436
  84.3 7.9 %collective-permute-start.19 = (bf16[896,128]{1,0:T(8,128)(2,1)S(1)}, bf16[896,128]{1,0:T(8,128)(2,1)S(1)}, u32[]{:S(2)}, u32[]{:S(2)}) collective-permute-start(bf16[896,128]{1,0:T(8,128)(2,1)S(1)} %bitcast.14), channel_id=1, source_target_pairs={{0,4},{4,0},{1,5},{5,1},{2,6},{6,2},{3,7},{7,3},{8,12},{12,8},{9,1... | collective-permute-start | bytes 688136 | tf_op jit(solution)/shard_map/ppermute | solution.py:416
